TPU v7x, 256 devices: a whole 4x4x8 slice. The times are simulated.
256 devices in a mesh: dp: 4 (over y_hi, core), seq: 32 (over x, z), tensor: 2 (over y_lo).
Axes of the slice: x: 4, y: 4 (y_hi: 2, y_lo: 2; y = y_hi * 2 + y_lo), z: 8, core: 2. Of those that a mesh axis runs over, the one named last changes fastest.
Arguments:
- latents: bfloat16 [4, 32, 128, 1152], P('dp', 'seq'), may hold values from -6 to 6
- modulation: float32 [4, 6, 1152], P('dp'), may hold values from -3 to 3
- cotangent: bfloat16 [4, 32, 128, 1152], P('dp', 'seq'), may hold values from -6 to 6
- proj_spatial: bfloat16 [1152, 3, 1152], P(None, None, 'tensor'), may hold values from -1 to 1
- out_spatial: bfloat16 [1152, 1152], P(None, 'tensor'), may hold values from -0.1875 to 0.1875
- proj_temporal: bfloat16 [1152, 3, 1152], P(None, None, 'tensor'), may hold values from -1 to 1
- out_temporal: bfloat16 [1152, 1152], P(None, 'tensor'), may hold values from -0.1875 to 0.1875
Outputs:
- block_output: bfloat16 [4, 32, 128, 1152], P('dp', 'seq')
- latent_grad: float32 [4, 32, 128, 1152], P('dp', 'seq')
- out_spatial_grad: float32 [1152, 1152], P(('dp', 'seq'), 'tensor')
- out_temporal_grad: float32 [1152, 1152], P(('dp', 'seq'), 'tensor')
All inputs are finite; a program needn't handle non-finite values.
Results may differ from a plain program's by a relative error of at most 0.019.
Values may be sent and summed in bfloat16 or wider, within the bound.
No kernel may reach another device: no remote copies, remote signals or barrier semaphores. Data moves between devices by JAX's collectives and lax.ppermute only.
A program may use at most 128 MiB of HBM per device.

v0:
```python
import jax
import jax.numpy as jnp
from jax import lax
from jax.sharding import PartitionSpec as P

HEAD_DIM = 72


NORM_EPS = 1e-06
SPATIAL_FORMS = ("bfphe,bfqhe->bfhpq", "bfhpq,bfqhe->bfphe", "bfhpq,bfphe->bfqhe")
TEMPORAL_FORMS = ("bfphe,bgphe->bphfg", "bphfg,bgphe->bfphe", "bphfg,bfphe->bgphe")


def contract(einsum_form, left_side, right_side):
    return jnp.einsum(einsum_form, left_side, right_side, preferred_element_type=jnp.float32)


def matmul(left_side, right_side):
    return jnp.dot(left_side, right_side, preferred_element_type=jnp.float32)


def matmul_left_t(left_side, right_side):
    return lax.dot_general(
        left_side, right_side, (((0,), (0,)), ((), ())), preferred_element_type=jnp.float32
    )


def matmul_right_t(left_side, right_side):
    return lax.dot_general(
        left_side, right_side, (((1,), (1,)), ((), ())), preferred_element_type=jnp.float32
    )


def norm_mod(values, shift_row, scale_row):
    average = jnp.mean(values, axis=-1, keepdims=True)
    centred = values - average
    variance = jnp.mean(centred * centred, axis=-1, keepdims=True)
    return centred * lax.rsqrt(variance + NORM_EPS) * (1.0 + scale_row) + shift_row


def norm_back(values, shift_row, scale_row, incoming):
    _, pull_back = jax.vjp(
        lambda inner_values: norm_mod(inner_values, shift_row, scale_row), values
    )
    return pull_back(incoming)[0]


def probabilities(queries, keys_in, form_set):
    scores = contract(form_set[0], queries, keys_in) * queries.shape[-1] ** (-0.5)
    top_score = jnp.max(scores, axis=-1, keepdims=True)
    raised = jnp.exp(scores - top_score)
    return raised / jnp.sum(raised, axis=-1, keepdims=True)


def attend(queries, keys_in, values_in, form_set):
    weights = probabilities(queries, keys_in, form_set).astype(jnp.bfloat16)
    return contract(form_set[1], weights, values_in).astype(jnp.bfloat16)


def attend_back(queries, keys_in, values_in, grad_out, form_set):
    weights = probabilities(queries, keys_in, form_set)
    rounded = weights.astype(jnp.bfloat16)
    grad_weights = contract(form_set[0], grad_out, values_in)
    inner_sum = jnp.sum(grad_weights * weights, axis=-1, keepdims=True)
    grad_scores = (weights * (grad_weights - inner_sum) * queries.shape[-1] ** (-0.5)).astype(
        jnp.bfloat16
    )
    grad_queries = contract(form_set[1], grad_scores, keys_in).astype(jnp.bfloat16)
    grad_keys = contract(form_set[2], grad_scores, queries).astype(jnp.bfloat16)
    grad_values = contract(form_set[2], rounded, grad_out).astype(jnp.bfloat16)
    return jnp.stack((grad_queries, grad_keys, grad_values), axis=3)


def per_device(
    latents, modulation, cotangent, proj_spatial, out_spatial, proj_temporal, out_temporal
):
    clip_count, frame_count, patch_count, model_width = latents.shape
    local_width = out_spatial.shape[1]
    head_count = local_width // HEAD_DIM
    frame_shape = (clip_count, frame_count, patch_count, 3, head_count, HEAD_DIM)
    head_shape = (clip_count, frame_count, patch_count, head_count, HEAD_DIM)
    mod_rows = modulation[:, :, None, None, :]
    proj_flat_s = proj_spatial.reshape(model_width, 3 * local_width)
    proj_flat_t = proj_temporal.reshape(model_width, 3 * local_width)
    inputs = latents.astype(jnp.float32)
    normed_s = norm_mod(inputs, mod_rows[:, 0], mod_rows[:, 1]).astype(jnp.bfloat16)
    flat_s = normed_s.reshape(-1, model_width)
    packed_s = matmul(flat_s, proj_flat_s).astype(jnp.bfloat16).reshape(frame_shape)
    heads_s = attend(
        packed_s[:, :, :, 0], packed_s[:, :, :, 1], packed_s[:, :, :, 2], SPATIAL_FORMS
    )
    heads_flat_s = heads_s.reshape(-1, local_width)
    mixed_s = lax.psum(matmul_right_t(heads_flat_s, out_spatial), "tensor")
    middle = inputs + mod_rows[:, 2] * mixed_s.reshape(inputs.shape)
    normed_t = norm_mod(middle, mod_rows[:, 3], mod_rows[:, 4]).astype(jnp.bfloat16)
    packed_t = matmul(normed_t.reshape(-1, model_width), proj_flat_t).astype(jnp.bfloat16)
    packed_t = packed_t.reshape(clip_count, frame_count, patch_count, 3 * local_width)
    arrived = lax.all_to_all(packed_t, "seq", split_axis=2, concat_axis=1, tiled=True)
    frames_all = arrived.shape[1]
    patches_loc = arrived.shape[2]
    arrived = arrived.reshape(clip_count, frames_all, patches_loc, 3, head_count, HEAD_DIM)
    heads_t = attend(arrived[:, :, :, 0], arrived[:, :, :, 1], arrived[:, :, :, 2], TEMPORAL_FORMS)
    heads_t = heads_t.reshape(clip_count, frames_all, patches_loc, local_width)
    heads_back = lax.all_to_all(heads_t, "seq", split_axis=1, concat_axis=2, tiled=True)
    heads_flat_t = heads_back.reshape(-1, local_width)
    mixed_t = lax.psum(
        matmul_right_t(heads_flat_t, out_temporal).astype(jnp.bfloat16), "tensor"
    ).astype(jnp.float32)
    block_output = (middle + mod_rows[:, 5] * mixed_t.reshape(inputs.shape)).astype(jnp.bfloat16)
    upstream = cotangent.astype(jnp.float32)
    scaled_t = (mod_rows[:, 5] * upstream).astype(jnp.bfloat16).reshape(-1, model_width)
    grad_out_t = matmul_left_t(scaled_t, heads_flat_t)
    grad_heads_t = matmul(scaled_t, out_temporal).astype(jnp.bfloat16)
    grad_heads_t = grad_heads_t.reshape(clip_count, frame_count, patch_count, local_width)
    grad_moved = lax.all_to_all(grad_heads_t, "seq", split_axis=2, concat_axis=1, tiled=True)
    grad_moved = grad_moved.reshape(clip_count, frames_all, patches_loc, head_count, HEAD_DIM)
    grad_packed_t = attend_back(
        arrived[:, :, :, 0], arrived[:, :, :, 1], arrived[:, :, :, 2], grad_moved, TEMPORAL_FORMS
    )
    grad_packed_t = grad_packed_t.reshape(clip_count, frames_all, patches_loc, 3 * local_width)
    grad_packed_back = lax.all_to_all(grad_packed_t, "seq", split_axis=1, concat_axis=2, tiled=True)
    grad_packed_back = grad_packed_back.reshape(-1, 3 * local_width)
    partial_t = matmul_right_t(grad_packed_back, proj_flat_t)
    grad_normed_t = lax.psum(partial_t.astype(jnp.bfloat16), "tensor").astype(jnp.float32)
    grad_middle = upstream + norm_back(
        middle, mod_rows[:, 3], mod_rows[:, 4], grad_normed_t.reshape(inputs.shape)
    )
    scaled_s = (mod_rows[:, 2] * grad_middle).astype(jnp.bfloat16).reshape(-1, model_width)
    grad_out_s = matmul_left_t(scaled_s, heads_flat_s)
    grad_heads_s = matmul(scaled_s, out_spatial).astype(jnp.bfloat16).reshape(head_shape)
    grad_packed_s = attend_back(
        packed_s[:, :, :, 0],
        packed_s[:, :, :, 1],
        packed_s[:, :, :, 2],
        grad_heads_s,
        SPATIAL_FORMS,
    )
    grad_packed_s = grad_packed_s.reshape(-1, 3 * local_width)
    grad_normed_s = lax.psum(
        matmul_right_t(grad_packed_s, proj_flat_s).astype(jnp.bfloat16), "tensor"
    ).astype(jnp.float32)
    latent_grad = grad_middle + norm_back(
        inputs, mod_rows[:, 0], mod_rows[:, 1], grad_normed_s.reshape(inputs.shape)
    )
    summed_out_s, summed_out_t = (
        lax.psum_scatter(grad_out_s, ("dp", "seq"), scatter_dimension=0, tiled=True),
        lax.psum_scatter(grad_out_t, ("dp", "seq"), scatter_dimension=0, tiled=True),
    )
    return (block_output, latent_grad, summed_out_s, summed_out_t)


def solution(mesh):
    placed = (
        P("dp", "seq", None, None),
        P("dp", None, None),
        P("dp", "seq", None, None),
        P(None, None, "tensor"),
        P(None, "tensor"),
        P(None, None, "tensor"),
        P(None, "tensor"),
    )
    return jax.shard_map(
        per_device,
        mesh=mesh,
        in_specs=placed,
        out_specs=(
            P("dp", "seq", None, None),
            P("dp", "seq", None, None),
            P(("dp", "seq"), "tensor"),
            P(("dp", "seq"), "tensor"),
        ),
        check_vma=False,
    )
```

profile of v0, /device:TPU:32, one launch (start us, length us, event | category | flops | bytes accessed | tf_op | source)
XLA Modules:
  0.0 1555.2 jit_solution(5561686761399622996)
XLA Ops:
  11.1 4.4 convolution_convert_fusion.3
  24.1 11.2 all-to-all-start.2
  35.4 29.6 %all-reduce.9.cloned.1.call-done = f32[128,1152]{1,0:T(8,128)} async-done(((f32[128,1152]{1,0:T(8,128)}), f32[128,1152]{1,0:T(8,128)}) %all-reduce.9.cloned.1.call-update) | async-done | bytes 589840 | tf_op jit(solution)/shard_map/psum | solution.py:93
  67.5 4.2 fusion.4
  71.7 3.1 copy.40
  74.8 5.2 reduce.36
  82.2 10.1 all-to-all-start
  99.0 9.4 all-to-all-done
  108.4 3.9 reshape.391
  112.3 4.5 bitcast_reduce_fusion
  116.8 2.7 reshape.364
  121.5 2.8 fusion.95
  128.4 2.7 fusion.19
  131.1 2.7 fusion.18
  136.2 2.8 reshape.379
  139.0 4.8 all-to-all-start.3
  147.9 11.9 all-to-all-done.3
  159.8 4.8 all-to-all-start.1
  166.7 3.8 convolution_convert_fusion.1
  170.7 3.9 all-to-all-done.1
  178.3 28.4 %all-reduce.11.cloned.1.call-done = bf16[128,1152]{1,0:T(8,128)(2,1)} async-done(((bf16[128,1152]{1,0:T(8,128)(2,1)}), bf16[128,1152]{1,0:T(8,128)(2,1)}) %all-reduce.11.cloned.1.call-update) | async-done | bytes 294928 | tf_op jit(solution)/shard_map/psum | solution.py:124
  218.7 3.6 convolution_convert_fusion
  228.8 36.7 %all-reduce.15.cloned.1.call-done = (bf16[128,1152]{1,0:T(8,128)(2,1)}, bf16[128,1152]{1,0:T(8,128)(2,1)}) async-done(((bf16[128,1152]{1,0:T(8,128)(2,1)}, bf16[128,1152]{1,0:T(8,128)(2,1)}), (bf16[128,1152]{1,0:T(8,128)(2,1)}, bf16[128,1152]{1,0:T(8,128)(2,1)})) %all-reduce.15.cloned.1.call-update) | async-done | bytes 589840 | tf_op jit(solution)/shard_map/psum | solution.py:106
  270.9 1276.3 %all-reduce.13.cloned.1.call-done = (f32[1152,576]{1,0:T(8,128)}, f32[1152,576]{1,0:T(8,128)}) async-done(((f32[1152,576]{1,0:T(8,128)}, f32[1152,576]{1,0:T(8,128)}), (f32[1152,576]{1,0:T(8,128)}, f32[1152,576]{1,0:T(8,128)})) %all-reduce.13.cloned.1.call-update) | async-done | bytes 5308432
  (117 shorter events, 67.1 us)
Async XLA Ops:
  7.2 13.2 copy-start
  7.2 57.8 %all-reduce.9.cloned.1.call-start = ((), (), s32[]{:S(2)}) async-start(), calls=%async_computation.4 | async-start | bytes 1179648 | tf_op jit(solution)/shard_map/psum | solution.py:93
  9.9 7.8 copy-start.12
  11.1 8.0 copy-start.20
  11.1 8.0 copy-start.15
  11.1 8.0 copy-start.2
  15.5 4.9 copy-start.5
  19.1 45.8 %copy-start.1 = (bf16[1,1,128,1152]{3,2,1,0:T(8,128)(2,1)S(1)}, bf16[1,1,128,1152]{3,2,1,0:T(8,128)(2,1)}, u32[]{:S(2)}) copy-start(bf16[1,1,128,1152]{3,2,1,0:T(8,128)(2,1)} %param.7) | copy-start | bytes 884740
  24.1 58.1 %all-to-all-start.2 = ((bf16[32,2,1152]{2,1,0:T(2,128)(2,1)}), bf16[32,2,1152]{2,1,0:T(2,128)(2,1)}, u32[]{:S(2)}, u32[]{:S(2)}) async-start(bf16[32,2,1152]{2,1,0:T(2,128)(2,1)} %reshape.392), calls=%async_computation.2 | async-start | bytes 294912 | tf_op jit(solution)/shard_map/all_to_all | solution.py:115
  82.2 26.1 %all-to-all-start = ((bf16[32,2,3456]{2,1,0:T(2,128)(2,1)}), bf16[32,2,3456]{2,1,0:T(2,128)(2,1)}, u32[]{:S(2)}, u32[]{:S(2)}) async-start(bf16[32,2,3456]{2,1,0:T(2,128)(2,1)} %reshape.390), calls=%async_computation | async-start | bytes 884736 | tf_op jit(solution)/shard_map/all_to_all | solution.py:98
  139.0 20.8 %all-to-all-start.3 = ((bf16[1,32,4,1728]{3,2,0,1:T(4,128)(2,1)}), bf16[1,32,4,1728]{3,2,0,1:T(4,128)(2,1)}, u32[]{:S(2)}, u32[]{:S(2)}) async-start(bf16[1,32,4,1728]{3,2,0,1:T(4,128)(2,1)} %reshape.379), calls=%async_computation.3 | async-start | bytes 917504 | tf_op jit(solution)/shard_map/all_to_all | solution.py:121
  159.8 14.8 all-to-all-start.1
  164.6 42.1 %all-reduce.11.cloned.1.call-start = ((), (), s32[]{:S(2)}) async-start(), calls=%async_computation.5 | async-start | bytes 589824 | tf_op jit(solution)/shard_map/psum | solution.py:124
  170.4 95.0 %all-reduce.15.cloned.1.call-start = ((), (), s32[]{:S(2)}) async-start(), calls=%async_computation.7 | async-start | bytes 1179648 | tf_op jit(solution)/shard_map/psum | solution.py:106
  206.7 5.6 copy-start.24
  206.7 5.6 copy-start.26
  217.7 4.7 copy-start.6
  217.7 4.7 copy-start.9
  222.4 1324.8 %all-reduce.13.cloned.1.call-start = ((), (), s32[]{:S(2)}) async-start(), calls=%async_computation.6 | async-start | bytes 11796480
  226.8 38.7 %copy-start.13 = (f32[128]{0:T(128)S(1)}, f32[128]{0:T(128)}, u32[]{:S(2)}) copy-start(f32[128]{0:T(128)} %copy-done.12) | copy-start | bytes 1540
  226.8 40.6 %copy-start.21 = (f32[128]{0:T(128)S(1)}, f32[128]{0:T(128)}, u32[]{:S(2)}) copy-start(f32[128]{0:T(128)} %copy-done.20) | copy-start | bytes 1540
  226.8 40.7 %copy-start.16 = (f32[128]{0:T(128)S(1)}, f32[128]{0:T(128)}, u32[]{:S(2)}) copy-start(f32[128]{0:T(128)} %copy-done.15) | copy-start | bytes 1540
  226.9 41.9 %copy-start.4 = (f32[1,1,128,1152]{3,2,1,0:T(8,128)S(1)}, f32[1,1,128,1152]{3,2,1,0:T(8,128)}, u32[]{:S(2)}) copy-start(f32[1,1,128,1152]{3,2,1,0:T(8,128)} %copy-done.3) | copy-start | bytes 1769476
  226.9 41.9 %copy-start.19 = (f32[128]{0:T(128)S(1)}, f32[128]{0:T(128)}, u32[]{:S(2)}) copy-start(f32[128]{0:T(128)} %copy-done.18) | copy-start | bytes 1540
  (12 other events, 16.6 us)
Sparse Core Ops, SparseCore 0:
  20.5 44.3 all-reduce.8
  170.6 36.1 all-reduce.10
  222.5 42.9 all-reduce.14
  268.1 1279.0 all-reduce.12
where the time goes:
time: 1560 us
  waiting for transfers between devices  1400 us (90%)
  matrix products  47.2 us (3%)
  local copies, waits for them, and re-layouts  41.7 us (3%)
  starting transfers between devices  31.3 us (2%)
  other arithmetic  23.9 us (2%)
    unnamed x5, waiting for transfers between devices  1280 us
    psum x1, waiting for transfers between devices, per_device(): lax.psum(matmul_right_t(heads_flat_t, out_temporal).astype(jnp.bfloat16),...  36.7 us
  transfers between devices with their start and end apart: 8, of which 7 were waited for; matrix products, arithmetic and copies ran while one was open for 3% of the time, Pallas kernels for 0%

commit v1 on v0

v1 whole, which is shorter than its diff:
```python
import functools

import jax
import jax.numpy as jnp
from jax import lax
from jax.experimental import pallas as pl
from jax.experimental.pallas import tpu as pltpu
from jax.sharding import PartitionSpec as P

HEAD_DIM = 72
NORM_EPS = 1e-06
PAIR = ((0, 1), (1, 0))
DP = 4
SEQ = 32
BF = jnp.bfloat16
F32 = jnp.float32
ROWS = 24


def mm(left, right):
    return jnp.dot(left, right, preferred_element_type=F32)


def mm_rt(left, right):
    return lax.dot_general(left, right, (((1,), (1,)), ((), ())), preferred_element_type=F32)


def mm_lt(left, right):
    return lax.dot_general(left, right, (((0,), (0,)), ((), ())), preferred_element_type=F32)


def normalise(values):
    average = jnp.mean(values, axis=-1, keepdims=True)
    centred = values - average
    inverse = lax.rsqrt(jnp.mean(centred * centred, axis=-1, keepdims=True) + NORM_EPS)
    return centred * inverse, inverse


def norm_back(values, scale_row, incoming):
    unit, inverse = normalise(values)
    scaled = incoming * (1.0 + scale_row)
    mean_plain = jnp.mean(scaled, axis=-1, keepdims=True)
    mean_unit = jnp.mean(scaled * unit, axis=-1, keepdims=True)
    return inverse * (scaled - mean_plain - unit * mean_unit)


def stack_heads(values):
    width = values.shape[1]
    owner = lax.broadcasted_iota(jnp.int32, (1, width), 1) // HEAD_DIM
    parts = [values * (owner == head).astype(F32).astype(BF) for head in range(width // HEAD_DIM)]
    return jnp.concatenate(parts, axis=0)


def side_by_side(stacked):
    tokens = stacked.shape[1]
    heads = stacked.shape[0] // tokens
    return jnp.concatenate([stacked[h * tokens : (h + 1) * tokens] for h in range(heads)], axis=1)


def softmax_weights(queries, keys_in, same=None):
    scores = mm_rt(stack_heads(queries), keys_in) * HEAD_DIM**-0.5
    if same is not None:
        scores = jnp.where(same, scores, -1e30)
    raised = jnp.exp(scores - jnp.max(scores, axis=-1, keepdims=True))
    return raised / jnp.sum(raised, axis=-1, keepdims=True)


def attend_back(queries, keys_in, values_in, grad_out, weights):
    grad_stacked = stack_heads(grad_out)
    grad_weights = mm_rt(grad_stacked, values_in)
    inner_sum = jnp.sum(grad_weights * weights, axis=-1, keepdims=True)
    grad_scores = (weights * (grad_weights - inner_sum) * HEAD_DIM**-0.5).astype(BF)
    grad_queries = mm(side_by_side(grad_scores), stack_heads(keys_in)).astype(BF)
    grad_keys = mm_lt(grad_scores, stack_heads(queries)).astype(BF)
    grad_values = mm_lt(weights.astype(BF), grad_stacked).astype(BF)
    return grad_queries, grad_keys, grad_values


def wire_row(index, tokens):
    part, token = index // tokens, index % tokens
    return 16 * (token // 4) + 4 * part + token % 4


def to_wire(parts):
    tokens = parts[0].shape[0]
    rows = 4 * tokens
    held = wire_row(lax.broadcasted_iota(jnp.int32, (1, rows), 1), tokens)
    place = lax.broadcasted_iota(jnp.int32, (rows, rows), 0) == held
    return mm(place.astype(F32).astype(BF), jnp.concatenate(parts, axis=0)).astype(BF)


def from_wire(rows_in):
    rows = rows_in.shape[0]
    tokens = rows // 4
    held = wire_row(lax.broadcasted_iota(jnp.int32, (rows, 1), 0), tokens)
    place = lax.broadcasted_iota(jnp.int32, (rows, rows), 1) == held
    full = mm(place.astype(F32).astype(BF), rows_in).astype(BF)
    return [full[i * tokens : (i + 1) * tokens] for i in range(4)]


def spatial_forward(x_ref, mod_ref, proj_ref, out_ref, packed_ref, weights_ref, heads_ref, mixed_ref):
    unit, _ = normalise(x_ref[...].astype(F32))
    normed = (unit * (1.0 + mod_ref[1:2]) + mod_ref[0:1]).astype(BF)
    queries, keys_in, values_in = [mm(normed, proj_ref[i]).astype(BF) for i in range(3)]
    packed_ref[0] = queries
    packed_ref[1] = keys_in
    packed_ref[2] = values_in
    weights = softmax_weights(queries, keys_in)
    weights_ref[...] = weights
    heads = mm(side_by_side(weights.astype(BF)), stack_heads(values_in)).astype(BF)
    heads_ref[...] = heads
    mixed_ref[...] = mm_rt(heads, out_ref[...]).astype(BF)


def split_columns(scaled, place, held_ref, block_refs):
    wide = scaled.shape[1] // DP
    for i in range(DP):
        held_ref[i] = scaled[:, i * wide : (i + 1) * wide]
    for i in range(DP):
        block_refs[i][...] = held_ref[place ^ i]


def upstream_start(place_ref, cot_ref, mod_ref, out_ref, grad_ref, b0, b1, b2, b3, held_ref):
    scaled = (mod_ref[5:6] * cot_ref[...].astype(F32)).astype(BF)
    grad_ref[...] = mm(scaled, out_ref[...]).astype(BF)
    split_columns(scaled, place_ref[0], held_ref, (b0, b1, b2, b3))


def middle_step(x_ref, mod_ref, mine_ref, other_ref, proj_ref, grad_ref, middle_ref, wire_ref):
    mixed = mine_ref[...].astype(F32) + other_ref[...].astype(F32)
    middle = x_ref[...].astype(F32) + mod_ref[2:3] * mixed
    middle_ref[...] = middle
    unit, _ = normalise(middle)
    normed = (unit * (1.0 + mod_ref[4:5]) + mod_ref[3:4]).astype(BF)
    parts = [mm(normed, proj_ref[i]).astype(BF) for i in range(3)]
    wire_ref[...] = to_wire(parts + [grad_ref[...]])


def temporal_step(arrived_ref, wire_ref):
    queries, keys_in, values_in, grad_out = from_wire(arrived_ref[...])
    tokens = queries.shape[0]
    heads = queries.shape[1] // HEAD_DIM
    row = lax.broadcasted_iota(jnp.int32, (heads * tokens, tokens), 0)
    column = lax.broadcasted_iota(jnp.int32, (heads * tokens, tokens), 1)
    weights = softmax_weights(queries, keys_in, row % 4 == column % 4)
    out = mm(side_by_side(weights.astype(BF)), stack_heads(values_in)).astype(BF)
    grads = attend_back(queries, keys_in, values_in, grad_out, weights)
    wire_ref[...] = to_wire(list(grads) + [out])


def temporal_return(arrived_ref, proj_ref, partial_ref, heads_ref):
    *grads, heads = from_wire(arrived_ref[...])
    heads_ref[...] = heads
    total = mm_rt(grads[0], proj_ref[0]) + mm_rt(grads[1], proj_ref[1])
    partial_ref[...] = (total + mm_rt(grads[2], proj_ref[2])).astype(BF)


def mix_temporal(heads_ref, out_ref, mixed_ref):
    mixed_ref[...] = mm_rt(heads_ref[...], out_ref[...]).astype(BF)


def middle_back(
    place_ref, cot_ref, middle_ref, mod_ref, mine_ref, other_ref, grad_ref, scaled_ref,
    b0, b1, b2, b3, held_ref,
):
    incoming = mine_ref[...].astype(F32) + other_ref[...].astype(F32)
    grad = cot_ref[...].astype(F32) + norm_back(middle_ref[...], mod_ref[4:5], incoming)
    grad_ref[...] = grad
    scaled = (mod_ref[2:3] * grad).astype(BF)
    scaled_ref[...] = scaled
    split_columns(scaled, place_ref[0], held_ref, (b0, b1, b2, b3))


def spatial_back(scaled_ref, packed_ref, weights_ref, out_ref, proj_ref, partial_ref):
    grad_heads = mm(scaled_ref[...], out_ref[...]).astype(BF)
    grads = attend_back(
        packed_ref[0], packed_ref[1], packed_ref[2], grad_heads, weights_ref[...]
    )
    total = mm_rt(grads[0], proj_ref[0]) + mm_rt(grads[1], proj_ref[1])
    partial_ref[...] = (total + mm_rt(grads[2], proj_ref[2])).astype(BF)


def latent_step(x_ref, mod_ref, grad_ref, mine_ref, other_ref, latent_ref):
    incoming = mine_ref[...].astype(F32) + other_ref[...].astype(F32)
    latent_ref[...] = grad_ref[...] + norm_back(x_ref[...].astype(F32), mod_ref[1:2], incoming)


def output_step(middle_ref, mod_ref, mine_ref, other_ref, block_ref):
    mixed = mine_ref[...].astype(F32) + other_ref[...].astype(F32)
    block_ref[...] = (middle_ref[...] + mod_ref[5:6] * mixed).astype(BF)


def weight_products(*refs):
    wire_ref = refs[-1]
    totals = []
    for which in range(2):
        base = which * 2 * DP
        total = mm_lt(refs[base][...], refs[base + DP][...])
        for i in range(1, DP):
            total = total + mm_lt(refs[base + i][...], refs[base + DP + i][...])
        totals.append(total.astype(BF))
    rows = totals[0].shape[0]
    part = rows // SEQ
    shape = (SEQ * ROWS, rows)
    row = lax.broadcasted_iota(jnp.int32, shape, 0)
    column = lax.broadcasted_iota(jnp.int32, (1, rows), 1)
    held = ROWS * (column // part) + column % part
    first = (row == held).astype(F32).astype(BF)
    second = (row == held + part).astype(F32).astype(BF)
    wire_ref[...] = (mm(first, totals[0]) + mm(second, totals[1])).astype(BF)


def weight_sums(arrived_ref, spatial_ref, temporal_ref):
    part = spatial_ref.shape[0]
    shape = (16, SEQ * ROWS)
    row = lax.broadcasted_iota(jnp.int32, shape, 0)
    column = lax.broadcasted_iota(jnp.int32, shape, 1) % ROWS
    arrived = arrived_ref[...]
    for start, ref in ((0, spatial_ref), (part, temporal_ref)):
        take = (column == row + start).astype(F32).astype(BF)
        ref[...] = mm(take, arrived)[:part]


def call(body, outs, *operands, scalars=0, scratch=(), flops=0):
    specs = [pl.BlockSpec(memory_space=pltpu.SMEM)] * scalars
    specs += [pl.BlockSpec(memory_space=pltpu.VMEM)] * (len(operands) - scalars)
    shapes = [jax.ShapeDtypeStruct(shape, dtype) for shape, dtype in outs]
    moved = sum(x.size * x.dtype.itemsize for x in [*operands, *shapes])
    single = len(shapes) == 1
    return pl.pallas_call(
        body,
        out_shape=shapes[0] if single else shapes,
        in_specs=specs,
        out_specs=specs[-1] if single else [specs[-1]] * len(shapes),
        scratch_shapes=list(scratch),
        cost_estimate=pl.CostEstimate(flops=flops, bytes_accessed=moved, transcendentals=0),
        compiler_params=pltpu.CompilerParams(vmem_limit_bytes=40 * 1024 * 1024),
    )(*operands)


def swap_pair(array):
    return lax.ppermute(array, "tensor", PAIR)


def swap_dp(array, mask):
    return lax.ppermute(array, "dp", [(i, i ^ mask) for i in range(DP)])


def all_to_all(array):
    rows, width = array.shape
    cut = array.reshape(SEQ, rows // SEQ, width)
    moved = lax.all_to_all(cut, "seq", split_axis=0, concat_axis=0, tiled=True)
    return moved.reshape(rows, width)


def per_device(
    latents, modulation, cotangent, proj_spatial, out_spatial, proj_temporal, out_temporal
):
    tokens, width = latents.shape[-2:]
    local = out_spatial.shape[1]
    heads = local // HEAD_DIM
    x = latents.reshape(tokens, width)
    cot = cotangent.reshape(tokens, width)
    mod = modulation.reshape(-1, width)
    proj_s = proj_spatial.transpose(1, 0, 2)
    proj_t = proj_temporal.transpose(1, 0, 2)
    place = lax.axis_index("dp").astype(jnp.int32).reshape(1)
    wide = ((tokens, width), BF)
    narrow = ((tokens, local), BF)
    full = ((tokens, width), F32)
    block = ((tokens, width // DP), BF)
    wire = ((4 * tokens, local), BF)
    held = pltpu.VMEM((DP, tokens, width // DP), BF)
    product = 2 * tokens * width * local
    attention = 4 * heads * tokens * tokens * local

    packed_s, weights_s, heads_s, mixed_s = call(
        spatial_forward,
        [((3, tokens, local), BF), ((heads * tokens, tokens), F32), narrow, wide],
        x, mod, proj_s, out_spatial, flops=4 * product + attention,
    )
    mixed_other = swap_pair(mixed_s)
    grad_heads_t, *blocks_t = call(
        upstream_start, [narrow] + [block] * DP,
        place, cot, mod, out_temporal, scalars=1, scratch=[held], flops=product,
    )
    middle, wire_out = call(
        middle_step, [full, wire],
        x, mod, mixed_s, mixed_other, proj_t, grad_heads_t, flops=4 * product,
    )
    arrived = all_to_all(wire_out)
    heads_all_s = [heads_s] + [swap_dp(heads_s, i) for i in range(1, DP)]
    blocks_t = blocks_t[:1] + [swap_dp(blocks_t[i], i) for i in range(1, DP)]
    wire_back = call(temporal_step, [wire], arrived, flops=6 * attention)
    returned = all_to_all(wire_back)
    partial_t, heads_t = call(temporal_return, [wide, narrow], returned, proj_t, flops=4 * product)
    partial_other = swap_pair(partial_t)
    mixed_t = call(mix_temporal, [wide], heads_t, out_temporal, flops=product)
    heads_all_t = [heads_t] + [swap_dp(heads_t, i) for i in range(1, DP)]
    mixed_t_other = swap_pair(mixed_t)
    grad_middle, scaled_s, *blocks_s = call(
        middle_back, [full, wide] + [block] * DP,
        place, cot, middle, mod, partial_t, partial_other, scalars=1, scratch=[held],
    )
    blocks_s = blocks_s[:1] + [swap_dp(blocks_s[i], i) for i in range(1, DP)]
    partial_s = call(
        spatial_back, [wide],
        scaled_s, packed_s, weights_s, out_spatial, proj_s, flops=4 * product + 5 * attention,
    )
    partial_s_other = swap_pair(partial_s)
    sums_out = call(
        weight_products, [((SEQ * ROWS, local), BF)],
        *blocks_s, *heads_all_s, *blocks_t, *heads_all_t, flops=4 * product,
    )
    sums_in = all_to_all(sums_out)
    block_output = call(output_step, [wide], middle, mod, mixed_t, mixed_t_other)
    latent_grad = call(latent_step, [full], x, mod, grad_middle, partial_s, partial_s_other)
    part = ((width // DP // SEQ, local), F32)
    grad_out_s, grad_out_t = call(weight_sums, [part, part], sums_in)
    return (
        block_output.reshape(latents.shape),
        latent_grad.reshape(latents.shape),
        grad_out_s,
        grad_out_t,
    )


def solution(mesh):
    placed = (
        P("dp", "seq", None, None),
        P("dp", None, None),
        P("dp", "seq", None, None),
        P(None, None, "tensor"),
        P(None, "tensor"),
        P(None, None, "tensor"),
        P(None, "tensor"),
    )
    return jax.shard_map(
        per_device,
        mesh=mesh,
        in_specs=placed,
        out_specs=(
            P("dp", "seq", None, None),
            P("dp", "seq", None, None),
            P(("dp", "seq"), "tensor"),
            P(("dp", "seq"), "tensor"),
        ),
        check_vma=False,
    )
```

time: 1560 us -> 166 us (0.11)
  waiting for transfers between devices: 1400 us -> 29.1 us
  blocking collectives: 0 us -> 55.7 us
  matrix products: 47.2 us -> 0 us
  other arithmetic: 23.9 us -> 0.01 us
  Pallas kernels: 0 us -> 23.3 us
    unnamed x5 -> x0, waiting for transfers between devices: 1280 us -> none
    psum x3 -> x0, waiting for transfers between devices: 94.7 us -> none  [the longest x1 36.7 us: per_device(): lax.psum(matmul_right_t(heads_flat_t, out_temporal).astype(jnp.bfloat16),...]
    all_to_all x0 -> x2, blocking collectives: none -> 55.7 us  [all_to_all(): moved = lax.all_to_all(cut, 'seq', split_axis=0, concat_axis=0, tiled=True)]
    dot_general x20 -> x0, matrix products: 42.3 us -> none  [the longest x10 17.6 us: contract(): jnp.einsum(einsum_form, left_side, right_side, preferred_element_type=jnp...]
    all_to_all x4 -> x1, starting transfers between devices: 31 us -> 6.37 us  [all_to_all(): moved = lax.all_to_all(cut, 'seq', split_axis=0, concat_axis=0, tiled=True)]
    pallas_call x0 -> x12, Pallas kernels: none -> 23.3 us  [call(): pl.pallas_call(body, out_shape=shapes[0] if single else shapes, in_specs=...]
    ppermute x0 -> x16, waiting for transfers between devices: none -> 21.1 us  [the longest x12 15.4 us: swap_dp(): return lax.ppermute(array, 'dp', [(i, i ^ mask) for i in range(DP)])]
    ppermute x0 -> x16, starting transfers between devices: none -> 18.9 us  [the longest x12 14.2 us: swap_dp(): return lax.ppermute(array, 'dp', [(i, i ^ mask) for i in range(DP)])]
  transfers between devices with their start and end apart: 8 -> 17, of which waited for: 7 -> 8; matrix products, arithmetic and copies ran while one was open for 3% -> 5% of each run, Pallas kernels for 0% -> 4%
where the time goes in v1:
time: 166 us; the launch traced here: 165 us
  blocking collectives  55.7 us (34%)
  local copies, waits for them, and re-layouts  31.2 us (19%)
  waiting for transfers between devices  29.1 us (18%)
  starting transfers between devices  25.3 us (15%)
  Pallas kernels  23.3 us (14%)
    all_to_all x2, blocking collectives, all_to_all(): moved = lax.all_to_all(cut, 'seq', split_axis=0, concat_axis=0, tiled=True)  55.7 us
    unnamed x49, local copies, waits for them, and re-layouts  31.2 us
    pallas_call x12, Pallas kernels, call(): pl.pallas_call(body, out_shape=shapes[0] if single else shapes, in_specs=...  23.3 us
    ppermute x12, waiting for transfers between devices, swap_dp(): return lax.ppermute(array, 'dp', [(i, i ^ mask) for i in range(DP)])  15.4 us
    ppermute x12, starting transfers between devices, swap_dp(): return lax.ppermute(array, 'dp', [(i, i ^ mask) for i in range(DP)])  14.2 us
    all_to_all x1, waiting for transfers between devices, all_to_all(): moved = lax.all_to_all(cut, 'seq', split_axis=0, concat_axis=0, tiled=True)  7.98 us
    all_to_all x1, starting transfers between devices, all_to_all(): moved = lax.all_to_all(cut, 'seq', split_axis=0, concat_axis=0, tiled=True)  6.37 us
    ppermute x4, waiting for transfers between devices, swap_pair(): return lax.ppermute(array, 'tensor', PAIR)  5.74 us
  transfers between devices with their start and end apart: 17, of which 8 were waited for; matrix products, arithmetic and copies ran while one was open for 5% of the time, Pallas kernels for 4%

profile of v1, /device:TPU:32, one launch (start us, length us, event | category | flops | bytes accessed | tf_op | source)
XLA Modules:
  0.0 165.5 jit_solution(12578668205569211032)
XLA Ops:
  1.4 6.7 %copy.11 = bf16[1152,3,576]{2,0,1:T(8,128)(2,1)} copy(bf16[1152,3,576]{0,2,1:T(8,128)(2,1)} %param.10) | data formatting | bytes 7962624 | tf_op args[3]
  9.2 2.2 %copy-done.1 = bf16[1152,3,576]{2,0,1:T(8,128)(2,1)S(1)} copy-done((bf16[1152,3,576]{2,0,1:T(8,128)(2,1)S(1)}, bf16[1152,3,576]{2,0,1:T(8,128)(2,1)}, u32[]{:S(2)}) %copy-start.1) | copy-done | bytes 3981336
  11.5 3.4 %shard_map.102 = (bf16[3,128,576]{2,1,0:T(8,128)(2,1)S(1)}, f32[1024,128]{1,0:T(8,128)S(1)}, bf16[128,576]{1,0:T(8,128)(2,1)S(1)}, bf16[128,1152]{1,0:T(8,128)(2,1)}) custom-call(bf16[128,1152]{1,0:T(8,128)(2,1)S(1)} %bitcast.23, f32[6,1152]{1,0:T(8,128)S(1)} %bitcast.27, bf16[3,1152,576]{2,1,0:T(8,128)(2,1)S(1)} %bitcast.20, bf16[1152,576]{1,0:T(8,128)(2,1)S(1)} %copy.12.out_ref), custom_call_target="tpu_custom_call" | custom-call | flops 981467136 | bytes 7040000 | tf_op jit(solution)/shard_map/pallas_call | solution.py:230
  18.7 2.1 %copy.14.out_ref = bf16[1152,576]{1,0:T(8,128)(2,1)S(1)} copy(bf16[1152,576]{0,1:T(8,128)(2,1)} %param.13) | data formatting | bytes 2654208 | tf_op args[6]
  20.8 6.6 %copy.13 = bf16[1152,3,576]{2,0,1:T(8,128)(2,1)} copy(bf16[1152,3,576]{0,2,1:T(8,128)(2,1)} %param.12) | data formatting | bytes 7962624 | tf_op args[5]
  28.8 2.2 %copy-done = bf16[1152,3,576]{2,0,1:T(8,128)(2,1)S(1)} copy-done((bf16[1152,3,576]{2,0,1:T(8,128)(2,1)S(1)}, bf16[1152,3,576]{2,0,1:T(8,128)(2,1)}, u32[]{:S(2)}) %copy-start) | copy-done | bytes 3981336
  31.1 2.7 %shard_map.104 = (f32[128,1152]{1,0:T(8,128)S(1)}, bf16[512,576]{1,0:T(8,128)(2,1)S(1)}) custom-call(bf16[128,1152]{1,0:T(8,128)(2,1)S(1)} %bitcast.24, f32[6,1152]{1,0:T(8,128)S(1)} %bitcast.29, bf16[128,1152]{1,0:T(8,128)(2,1)} %get-tuple-element.25.mine_ref, bf16[128,1152]{1,0:T(8,128)(2,1)} %collective-permute-done.other_ref, ...), custom_call_target="tpu_custom_call" | custom-call | flops 679477248 | bytes 6220800 | tf_op jit(solution)/shard_map/pallas_call | solution.py:230
  33.8 31.3 %all_to_all.15 = bf16[32,16,576]{2,1,0:T(8,128)(2,1)S(1)} all-to-all(bf16[32,16,576]{2,1,0:T(8,128)(2,1)S(1)} %bitcast.35), channel_id=1, replica_groups=mesh['dp'=4,'seq'=32,'tensor'=2] {'seq'}, dimensions={0} | all-to-all | bytes 1179648 | tf_op jit(solution)/shard_map/all_to_all | solution.py:252
  65.0 3.4 %shard_map.105 = bf16[512,576]{1,0:T(8,128)(2,1)S(1)} custom-call(bf16[512,576]{1,0:T(8,128)(2,1)S(1)} %bitcast.36), custom_call_target="tpu_custom_call" | custom-call | flops 1811939328 | bytes 1179648 | tf_op jit(solution)/shard_map/pallas_call | solution.py:230
  68.4 24.4 %all_to_all.16 = bf16[32,16,576]{2,1,0:T(8,128)(2,1)S(1)} all-to-all(bf16[32,16,576]{2,1,0:T(8,128)(2,1)S(1)} %bitcast.37), channel_id=1, replica_groups=mesh['dp'=4,'seq'=32,'tensor'=2] {'seq'}, dimensions={0} | all-to-all | bytes 1179648 | tf_op jit(solution)/shard_map/all_to_all | solution.py:252
  92.8 2.4 %shard_map.106 = (bf16[128,1152]{1,0:T(8,128)(2,1)S(1)}, bf16[128,576]{1,0:T(8,128)(2,1)S(1)}) custom-call(bf16[512,576]{1,0:T(8,128)(2,1)S(1)} %bitcast.26, bf16[3,1152,576]{2,1,0:T(8,128)(2,1)S(1)} %bitcast.19), custom_call_target="tpu_custom_call" | custom-call | flops 679477248 | bytes 5013504 | tf_op jit(solution)/shard_map/pallas_call | solution.py:230
  96.4 3.2 %collective-permute-start.11 = (bf16[128,288]{1,0:T(8,128)(2,1)S(1)}, bf16[128,288]{1,0:T(8,128)(2,1)S(1)}, u32[]{:S(2)}, u32[]{:S(2)}) collective-permute-start(bf16[128,288]{1,0:T(8,128)(2,1)S(1)} %get-tuple-element.42), channel_id=1, source_target_pairs={{0,128},{64,192},{128,0},{192,64},{1,129},{65,193},{129,1},{193,65... | collective-permute-start | bytes 221192 | tf_op jit(solution)/shard_map/ppermute | solution.py:246
  99.6 2.9 %collective-permute-start.8 = (bf16[128,576]{1,0:T(8,128)(2,1)S(1)}, bf16[128,576]{1,0:T(8,128)(2,1)S(1)}, u32[]{:S(2)}, u32[]{:S(2)}) collective-permute-start(bf16[128,576]{1,0:T(8,128)(2,1)S(1)} %copy-done.12), channel_id=1, source_target_pairs={{0,128},{64,192},{128,0},{192,64},{1,129},{65,193},{129,1},{193,65... | collective-permute-start | bytes 442376 | tf_op jit(solution)/shard_map/ppermute | solution.py:246
  102.5 4.9 %collective-permute-done.11.refs_10_ = bf16[128,288]{1,0:T(8,128)(2,1)S(1)} collective-permute-done((bf16[128,288]{1,0:T(8,128)(2,1)S(1)}, bf16[128,288]{1,0:T(8,128)(2,1)S(1)}, u32[]{:S(2)}, u32[]{:S(2)}) %collective-permute-start.11) | collective-permute-done | bytes 73760 | tf_op jit(solution)/shard_map/ppermute | solution.py:246
  107.4 1.9 %collective-permute-start.13 = (bf16[128,576]{1,0:T(8,128)(2,1)S(1)}, bf16[128,576]{1,0:T(8,128)(2,1)S(1)}, u32[]{:S(2)}, u32[]{:S(2)}) collective-permute-start(bf16[128,576]{1,0:T(8,128)(2,1)S(1)} %get-tuple-element.29.heads_ref.refs_12_), channel_id=1, source_target_pairs={{0,64},{64,0},{128,192},{192,128},{1,65},{65,1},{129,193},{193,129... | collective-permute-start | bytes 442376 | tf_op jit(solution)/shard_map/ppermute | solution.py:246
  118.0 4.4 %collective-permute-done.15.refs_15_ = bf16[128,576]{1,0:T(8,128)(2,1)S(1)} collective-permute-done((bf16[128,576]{1,0:T(8,128)(2,1)S(1)}, bf16[128,576]{1,0:T(8,128)(2,1)S(1)}, u32[]{:S(2)}, u32[]{:S(2)}) %collective-permute-start.15) | collective-permute-done | bytes 147488 | tf_op jit(solution)/shard_map/ppermute | solution.py:246
  123.6 2.6 %collective-permute-done.6.refs_3_ = bf16[128,288]{1,0:T(8,128)(2,1)S(1)} collective-permute-done((bf16[128,288]{1,0:T(8,128)(2,1)S(1)}, bf16[128,288]{1,0:T(8,128)(2,1)S(1)}, u32[]{:S(2)}, u32[]{:S(2)}) %collective-permute-start.6) | collective-permute-done | bytes 73760 | tf_op jit(solution)/shard_map/ppermute | solution.py:246
  126.2 2.5 %shard_map.112 = bf16[768,576]{1,0:T(8,128)(2,1)S(1)} custom-call(bf16[128,288]{1,0:T(8,128)(2,1)S(1)} %get-tuple-element.35.refs_0_, bf16[128,288]{1,0:T(8,128)(2,1)S(1)} %collective-permute-done.4.refs_1_, bf16[128,288]{1,0:T(8,128)(2,1)S(1)} %collective-permute-done.5.refs_2_, bf16[128,288]{1,0:T(8,128)(2,1)S(1)} %collective-permute-done.6.refs_3_, ...), custom_call_target="tpu_custom_call" | custom-call | flops 679477248 | bytes 2654208 | tf_op jit(solution)/shard_map/pallas_call | solution.py:230
  129.7 6.4 %all-to-all-start.2 = ((bf16[32,24,576]{2,1,0:T(8,128)(2,1)}), bf16[32,24,576]{2,1,0:T(8,128)(2,1)}, u32[]{:S(2)}, u32[]{:S(2)}) async-start(bf16[32,24,576]{2,1,0:T(8,128)(2,1)} %bitcast.22), calls=%async_computation.2 | async-start | bytes 1966080 | tf_op jit(solution)/shard_map/all_to_all | solution.py:252
  137.6 2.3 %copy-done.2 = bf16[1152,3,576]{2,0,1:T(8,128)(2,1)S(1)} copy-done((bf16[1152,3,576]{2,0,1:T(8,128)(2,1)S(1)}, bf16[1152,3,576]{2,0,1:T(8,128)(2,1)}, u32[]{:S(2)}) %copy-start.2) | copy-done | bytes 3981336
  142.9 3.1 %shard_map.110.mine_ref = bf16[128,1152]{1,0:T(8,128)(2,1)S(1)} custom-call(bf16[128,1152]{1,0:T(8,128)(2,1)S(1)} %copy-done.18, bf16[3,128,576]{2,1,0:T(8,128)(2,1)S(1)} %copy-done.16, f32[1024,128]{1,0:T(8,128)S(1)} %copy-done.14, bf16[1152,576]{1,0:T(8,128)(2,1)S(1)} %copy.12.out_ref, bf16[3,1152,576]{2,1,0:T(8,128)(2,1)S(1)} %bitcast.21), custom_call_target="tpu_custom_call" | custom-call | flops 2189426688 | bytes 6864896 | tf_op jit(solution)/shard_map/pallas_call | solution.py:230
  148.3 5.7 %collective-permute-done.3.other_ref = bf16[128,1152]{1,0:T(8,128)(2,1)S(1)} collective-permute-done((bf16[128,1152]{1,0:T(8,128)(2,1)S(1)}, bf16[128,1152]{1,0:T(8,128)(2,1)S(1)}, u32[]{:S(2)}, u32[]{:S(2)}) %collective-permute-start.3) | collective-permute-done | bytes 294944 | tf_op jit(solution)/shard_map/ppermute | solution.py:242
  155.3 8.0 %all-to-all-done.2 = bf16[32,24,576]{2,1,0:T(8,128)(2,1)} async-done(((bf16[32,24,576]{2,1,0:T(8,128)(2,1)}), bf16[32,24,576]{2,1,0:T(8,128)(2,1)}, u32[]{:S(2)}, u32[]{:S(2)}) %all-to-all-start.2) | async-done | bytes 884768 | tf_op jit(solution)/shard_map/all_to_all | solution.py:252
  163.3 2.2 %shard_map.113 = (f32[9,576]{1,0:T(8,128)}, f32[9,576]{1,0:T(8,128)}) custom-call(bf16[768,576]{1,0:T(8,128)(2,1)} %bitcast.12.arrived_ref), custom_call_target="tpu_custom_call" | custom-call | bytes 926208 | tf_op jit(solution)/shard_map/pallas_call | solution.py:230
  (74 shorter events, 27.3 us)
Async XLA Ops:
  17.1 11.7 %collective-permute-start = (bf16[128,1152]{1,0:T(8,128)(2,1)}, bf16[128,1152]{1,0:T(8,128)(2,1)}, u32[]{:S(2)}, u32[]{:S(2)}) collective-permute-start(bf16[128,1152]{1,0:T(8,128)(2,1)} %get-tuple-element.25.mine_ref), channel_id=1, source_target_pairs={{0,1},{1,0},{2,3},{3,2},{4,5},{5,4},{6,7},{7,6},{8,9},{9,8},{10,11... | collective-permute-start | bytes 884744 | tf_op jit(solution)/shard_map/ppermute | solution.py:242
  33.7 78.5 %copy-start.5 = (f32[128,1152]{1,0:T(8,128)}, f32[128,1152]{1,0:T(8,128)S(1)}, u32[]{:S(2)}) copy-start(f32[128,1152]{1,0:T(8,128)S(1)} %get-tuple-element.27.middle_ref) | copy-start | bytes 1769476
  33.8 59.1 %slice-start = ((s8[4423680]{0:T(1024)(128)(4,1)}), s8[4194304]{0:T(1024)(128)(4,1)S(1)}, s32[]{:S(2)}) async-start(s8[4423680]{0:T(1024)(128)(4,1)} %bitcast.17), calls=%async_computation.3 | async-start | bytes 8388608
  65.0 27.8 %slice-start.1 = ((s8[4423680]{0:T(1024)(128)(4,1)}), s8[229376]{0:T(1024)(128)(4,1)S(1)}, s32[]{:S(2)}) async-start(s8[4423680]{0:T(1024)(128)(4,1)} %bitcast.17), calls=%async_computation.4 | async-start | bytes 458752
  68.4 27.5 %copy-start.12 = (bf16[128,576]{1,0:T(8,128)(2,1)S(1)}, bf16[128,576]{1,0:T(8,128)(2,1)}, u32[]{:S(2)}) copy-start(bf16[128,576]{1,0:T(8,128)(2,1)} %copy-done.11) | copy-start | bytes 442372
  68.4 43.8 %copy-start.8 = (bf16[1,1,128,1152]{3,2,1,0:T(8,128)(2,1)S(1)}, bf16[1,1,128,1152]{3,2,1,0:T(8,128)(2,1)}, u32[]{:S(2)}) copy-start(bf16[1,1,128,1152]{3,2,1,0:T(8,128)(2,1)} %param.9) | copy-start | bytes 884740
  95.2 15.9 %collective-permute-start.2 = (bf16[128,1152]{1,0:T(8,128)(2,1)S(1)}, bf16[128,1152]{1,0:T(8,128)(2,1)S(1)}, u32[]{:S(2)}, u32[]{:S(2)}) collective-permute-start(bf16[128,1152]{1,0:T(8,128)(2,1)S(1)} %get-tuple-element.30.mine_ref), channel_id=1, source_target_pairs={{0,1},{1,0},{2,3},{3,2},{4,5},{5,4},{6,7},{7,6},{8,9},{9,8},{10,11... | collective-permute-start | bytes 884744 | tf_op jit(solution)/shard_map/ppermute | solution.py:242
  95.9 3.7 %collective-permute-start.10 = (bf16[128,288]{1,0:T(8,128)(2,1)S(1)}, bf16[128,288]{1,0:T(8,128)(2,1)S(1)}, u32[]{:S(2)}, u32[]{:S(2)}) collective-permute-start(bf16[128,288]{1,0:T(8,128)(2,1)S(1)} %get-tuple-element.41), channel_id=1, source_target_pairs={{0,64},{64,0},{128,192},{192,128},{1,65},{65,1},{129,193},{193,129... | collective-permute-start | bytes 221192 | tf_op jit(solution)/shard_map/ppermute | solution.py:246
  95.9 13.4 %collective-permute-start.7 = (bf16[128,576]{1,0:T(8,128)(2,1)S(1)}, bf16[128,576]{1,0:T(8,128)(2,1)S(1)}, u32[]{:S(2)}, u32[]{:S(2)}) collective-permute-start(bf16[128,576]{1,0:T(8,128)(2,1)S(1)} %copy-done.12), channel_id=1, source_target_pairs={{0,64},{64,0},{128,192},{192,128},{1,65},{65,1},{129,193},{193,129... | collective-permute-start | bytes 442376 | tf_op jit(solution)/shard_map/ppermute | solution.py:246
  96.4 11.0 %collective-permute-start.11 = (bf16[128,288]{1,0:T(8,128)(2,1)S(1)}, bf16[128,288]{1,0:T(8,128)(2,1)S(1)}, u32[]{:S(2)}, u32[]{:S(2)}) collective-permute-start(bf16[128,288]{1,0:T(8,128)(2,1)S(1)} %get-tuple-element.42), channel_id=1, source_target_pairs={{0,128},{64,192},{128,0},{192,64},{1,129},{65,193},{129,1},{193,65... | collective-permute-start | bytes 221192 | tf_op jit(solution)/shard_map/ppermute | solution.py:246
  99.6 7.8 %collective-permute-start.12 = (bf16[128,288]{1,0:T(8,128)(2,1)S(1)}, bf16[128,288]{1,0:T(8,128)(2,1)S(1)}, u32[]{:S(2)}, u32[]{:S(2)}) collective-permute-start(bf16[128,288]{1,0:T(8,128)(2,1)S(1)} %get-tuple-element.43), channel_id=1, source_target_pairs={{0,192},{64,128},{128,64},{192,0},{1,193},{65,129},{129,65},{193,1... | collective-permute-start | bytes 221192 | tf_op jit(solution)/shard_map/ppermute | solution.py:246
  99.6 13.2 %collective-permute-start.8 = (bf16[128,576]{1,0:T(8,128)(2,1)S(1)}, bf16[128,576]{1,0:T(8,128)(2,1)S(1)}, u32[]{:S(2)}, u32[]{:S(2)}) collective-permute-start(bf16[128,576]{1,0:T(8,128)(2,1)S(1)} %copy-done.12), channel_id=1, source_target_pairs={{0,128},{64,192},{128,0},{192,64},{1,129},{65,193},{129,1},{193,65... | collective-permute-start | bytes 442376 | tf_op jit(solution)/shard_map/ppermute | solution.py:246
  107.4 8.0 %collective-permute-start.9 = (bf16[128,576]{1,0:T(8,128)(2,1)S(1)}, bf16[128,576]{1,0:T(8,128)(2,1)S(1)}, u32[]{:S(2)}, u32[]{:S(2)}) collective-permute-start(bf16[128,576]{1,0:T(8,128)(2,1)S(1)} %copy-done.12), channel_id=1, source_target_pairs={{0,192},{64,128},{128,64},{192,0},{1,193},{65,129},{129,65},{193,1... | collective-permute-start | bytes 442376 | tf_op jit(solution)/shard_map/ppermute | solution.py:246
  107.4 8.0 %collective-permute-start.13 = (bf16[128,576]{1,0:T(8,128)(2,1)S(1)}, bf16[128,576]{1,0:T(8,128)(2,1)S(1)}, u32[]{:S(2)}, u32[]{:S(2)}) collective-permute-start(bf16[128,576]{1,0:T(8,128)(2,1)S(1)} %get-tuple-element.29.heads_ref.refs_12_), channel_id=1, source_target_pairs={{0,64},{64,0},{128,192},{192,128},{1,65},{65,1},{129,193},{193,129... | collective-permute-start | bytes 442376 | tf_op jit(solution)/shard_map/ppermute | solution.py:246
  109.3 8.6 %collective-permute-start.14 = (bf16[128,576]{1,0:T(8,128)(2,1)S(1)}, bf16[128,576]{1,0:T(8,128)(2,1)S(1)}, u32[]{:S(2)}, u32[]{:S(2)}) collective-permute-start(bf16[128,576]{1,0:T(8,128)(2,1)S(1)} %get-tuple-element.29.heads_ref.refs_12_), channel_id=1, source_target_pairs={{0,128},{64,192},{128,0},{192,64},{1,129},{65,193},{129,1},{193,65... | collective-permute-start | bytes 442376 | tf_op jit(solution)/shard_map/ppermute | solution.py:246
  111.1 11.3 %collective-permute-start.15 = (bf16[128,576]{1,0:T(8,128)(2,1)S(1)}, bf16[128,576]{1,0:T(8,128)(2,1)S(1)}, u32[]{:S(2)}, u32[]{:S(2)}) collective-permute-start(bf16[128,576]{1,0:T(8,128)(2,1)S(1)} %get-tuple-element.29.heads_ref.refs_12_), channel_id=1, source_target_pairs={{0,192},{64,128},{128,64},{192,0},{1,193},{65,129},{129,65},{193,1... | collective-permute-start | bytes 442376 | tf_op jit(solution)/shard_map/ppermute | solution.py:246
  112.8 15.9 %copy-start.9 = (f32[128,1152]{1,0:T(8,128)}, f32[128,1152]{1,0:T(8,128)S(1)}, u32[]{:S(2)}) copy-start(f32[128,1152]{1,0:T(8,128)S(1)} %get-tuple-element.31.grad_ref) | copy-start | bytes 1769476
  112.8 15.9 %copy-start.17 = (bf16[128,1152]{1,0:T(8,128)(2,1)}, bf16[128,1152]{1,0:T(8,128)(2,1)S(1)}, u32[]{:S(2)}) copy-start(bf16[128,1152]{1,0:T(8,128)(2,1)S(1)} %get-tuple-element.32.scaled_ref) | copy-start | bytes 884740
  112.9 9.5 %collective-permute-start.4 = (bf16[128,288]{1,0:T(8,128)(2,1)S(1)}, bf16[128,288]{1,0:T(8,128)(2,1)S(1)}, u32[]{:S(2)}, u32[]{:S(2)}) collective-permute-start(bf16[128,288]{1,0:T(8,128)(2,1)S(1)} %get-tuple-element.36), channel_id=1, source_target_pairs={{0,64},{64,0},{128,192},{192,128},{1,65},{65,1},{129,193},{193,129... | collective-permute-start | bytes 221192 | tf_op jit(solution)/shard_map/ppermute | solution.py:246
  115.4 8.2 %collective-permute-start.5 = (bf16[128,288]{1,0:T(8,128)(2,1)S(1)}, bf16[128,288]{1,0:T(8,128)(2,1)S(1)}, u32[]{:S(2)}, u32[]{:S(2)}) collective-permute-start(bf16[128,288]{1,0:T(8,128)(2,1)S(1)} %get-tuple-element.37), channel_id=1, source_target_pairs={{0,128},{64,192},{128,0},{192,64},{1,129},{65,193},{129,1},{193,65... | collective-permute-start | bytes 221192 | tf_op jit(solution)/shard_map/ppermute | solution.py:246
  115.5 10.7 %collective-permute-start.6 = (bf16[128,288]{1,0:T(8,128)(2,1)S(1)}, bf16[128,288]{1,0:T(8,128)(2,1)S(1)}, u32[]{:S(2)}, u32[]{:S(2)}) collective-permute-start(bf16[128,288]{1,0:T(8,128)(2,1)S(1)} %get-tuple-element.38), channel_id=1, source_target_pairs={{0,192},{64,128},{128,64},{192,0},{1,193},{65,129},{129,65},{193,1... | collective-permute-start | bytes 221192 | tf_op jit(solution)/shard_map/ppermute | solution.py:246
  129.7 33.6 %all-to-all-start.2 = ((bf16[32,24,576]{2,1,0:T(8,128)(2,1)}), bf16[32,24,576]{2,1,0:T(8,128)(2,1)}, u32[]{:S(2)}, u32[]{:S(2)}) async-start(bf16[32,24,576]{2,1,0:T(8,128)(2,1)} %bitcast.22), calls=%async_computation.2 | async-start | bytes 1966080 | tf_op jit(solution)/shard_map/all_to_all | solution.py:252
  136.6 10.8 %collective-permute-start.1 = (bf16[128,1152]{1,0:T(8,128)(2,1)S(1)}, bf16[128,1152]{1,0:T(8,128)(2,1)S(1)}, u32[]{:S(2)}, u32[]{:S(2)}) collective-permute-start(bf16[128,1152]{1,0:T(8,128)(2,1)S(1)} %shard_map.107.mine_ref), channel_id=1, source_target_pairs={{0,1},{1,0},{2,3},{3,2},{4,5},{5,4},{6,7},{7,6},{8,9},{9,8},{10,11... | collective-permute-start | bytes 884744 | tf_op jit(solution)/shard_map/ppermute | solution.py:242
  146.0 8.0 %collective-permute-start.3 = (bf16[128,1152]{1,0:T(8,128)(2,1)S(1)}, bf16[128,1152]{1,0:T(8,128)(2,1)S(1)}, u32[]{:S(2)}, u32[]{:S(2)}) collective-permute-start(bf16[128,1152]{1,0:T(8,128)(2,1)S(1)} %shard_map.110.mine_ref), channel_id=1, source_target_pairs={{0,1},{1,0},{2,3},{3,2},{4,5},{5,4},{6,7},{7,6},{8,9},{9,8},{10,11... | collective-permute-start | bytes 884744 | tf_op jit(solution)/shard_map/ppermute | solution.py:242
  (15 other events, 44.1 us)

commit v2 on v1

--- a/solution.py
+++ b/solution.py
@@ -15,6 +15,10 @@
 BF = jnp.bfloat16
 F32 = jnp.float32
 ROWS = 24
+X_RING = 4
+Z_RING = 8
+X_GROUPS = tuple(tuple(z + Z_RING * x for x in range(X_RING)) for z in range(Z_RING))
+Z_GROUPS = tuple(tuple(z + Z_RING * x for z in range(Z_RING)) for x in range(X_RING))
 
 
 def mm(left, right):
@@ -98,18 +102,28 @@
     return [full[i * tokens : (i + 1) * tokens] for i in range(4)]
 
 
-def spatial_forward(x_ref, mod_ref, proj_ref, out_ref, packed_ref, weights_ref, heads_ref, mixed_ref):
+def spatial_forward(
+    x_ref, mod_ref, proj_hbm, out_hbm, packed_ref, weights_ref, heads_ref, mixed_ref,
+    proj_ref, out_ref, sems,
+):
+    copies = [pltpu.make_async_copy(proj_hbm.at[i], proj_ref.at[i], sems.at[i]) for i in range(3)]
+    copies.append(pltpu.make_async_copy(out_hbm, out_ref, sems.at[3]))
+    for copy in copies:
+        copy.start()
     unit, _ = normalise(x_ref[...].astype(F32))
-    normed = (unit * (1.0 + mod_ref[1:2]) + mod_ref[0:1]).astype(BF)
-    queries, keys_in, values_in = [mm(normed, proj_ref[i]).astype(BF) for i in range(3)]
-    packed_ref[0] = queries
-    packed_ref[1] = keys_in
-    packed_ref[2] = values_in
+    normed = (unit * (1.0 + mod_ref[1]) + mod_ref[0]).astype(BF)
+    parts = []
+    for i in range(3):
+        copies[i].wait()
+        parts.append(mm_rt(normed, proj_ref[i]).astype(BF))
+        packed_ref[i] = parts[i]
+    queries, keys_in, values_in = parts
     weights = softmax_weights(queries, keys_in)
     weights_ref[...] = weights
     heads = mm(side_by_side(weights.astype(BF)), stack_heads(values_in)).astype(BF)
     heads_ref[...] = heads
-    mixed_ref[...] = mm_rt(heads, out_ref[...]).astype(BF)
+    copies[3].wait()
+    mixed_ref[...] = mm(heads, out_ref[...]).astype(BF)
 
 
 def split_columns(scaled, place, held_ref, block_refs):
@@ -117,22 +131,27 @@
     for i in range(DP):
         held_ref[i] = scaled[:, i * wide : (i + 1) * wide]
     for i in range(DP):
-        block_refs[i][...] = held_ref[place ^ i]
-
-
-def upstream_start(place_ref, cot_ref, mod_ref, out_ref, grad_ref, b0, b1, b2, b3, held_ref):
-    scaled = (mod_ref[5:6] * cot_ref[...].astype(F32)).astype(BF)
-    grad_ref[...] = mm(scaled, out_ref[...]).astype(BF)
+        block_refs[i][:, block_refs[i].shape[1] - wide :] = held_ref[place ^ i]
+
+
+def upstream_start(
+    place_ref, cot_ref, mod_ref, out_ref, heads_ref, grad_ref, b0, b1, b2, b3, held_ref
+):
+    scaled = (mod_ref[5] * cot_ref[...].astype(F32)).astype(BF)
+    grad_ref[...] = mm_rt(scaled, out_ref[...]).astype(BF)
     split_columns(scaled, place_ref[0], held_ref, (b0, b1, b2, b3))
+    local = heads_ref.shape[1]
+    for ref in (b1, b2, b3):
+        ref[:, :local] = heads_ref[...]
 
 
 def middle_step(x_ref, mod_ref, mine_ref, other_ref, proj_ref, grad_ref, middle_ref, wire_ref):
     mixed = mine_ref[...].astype(F32) + other_ref[...].astype(F32)
-    middle = x_ref[...].astype(F32) + mod_ref[2:3] * mixed
+    middle = x_ref[...].astype(F32) + mod_ref[2] * mixed
     middle_ref[...] = middle
     unit, _ = normalise(middle)
-    normed = (unit * (1.0 + mod_ref[4:5]) + mod_ref[3:4]).astype(BF)
-    parts = [mm(normed, proj_ref[i]).astype(BF) for i in range(3)]
+    normed = (unit * (1.0 + mod_ref[4]) + mod_ref[3]).astype(BF)
+    parts = [mm_rt(normed, proj_ref[i]).astype(BF) for i in range(3)]
     wire_ref[...] = to_wire(parts + [grad_ref[...]])
 
 
@@ -151,12 +170,12 @@
 def temporal_return(arrived_ref, proj_ref, partial_ref, heads_ref):
     *grads, heads = from_wire(arrived_ref[...])
     heads_ref[...] = heads
-    total = mm_rt(grads[0], proj_ref[0]) + mm_rt(grads[1], proj_ref[1])
-    partial_ref[...] = (total + mm_rt(grads[2], proj_ref[2])).astype(BF)
+    total = mm(grads[0], proj_ref[0]) + mm(grads[1], proj_ref[1])
+    partial_ref[...] = (total + mm(grads[2], proj_ref[2])).astype(BF)
 
 
 def mix_temporal(heads_ref, out_ref, mixed_ref):
-    mixed_ref[...] = mm_rt(heads_ref[...], out_ref[...]).astype(BF)
+    mixed_ref[...] = mm(heads_ref[...], out_ref[...]).astype(BF)
 
 
 def middle_back(
@@ -164,66 +183,86 @@
     b0, b1, b2, b3, held_ref,
 ):
     incoming = mine_ref[...].astype(F32) + other_ref[...].astype(F32)
-    grad = cot_ref[...].astype(F32) + norm_back(middle_ref[...], mod_ref[4:5], incoming)
+    grad = cot_ref[...].astype(F32) + norm_back(middle_ref[...], mod_ref[4], incoming)
     grad_ref[...] = grad
-    scaled = (mod_ref[2:3] * grad).astype(BF)
+    scaled = (mod_ref[2] * grad).astype(BF)
     scaled_ref[...] = scaled
     split_columns(scaled, place_ref[0], held_ref, (b0, b1, b2, b3))
 
 
-def spatial_back(scaled_ref, packed_ref, weights_ref, out_ref, proj_ref, partial_ref):
-    grad_heads = mm(scaled_ref[...], out_ref[...]).astype(BF)
+def spatial_back(
+    scaled_ref, packed_ref, weights_ref, out_ref, proj_hbm, partial_ref, proj_ref, sem
+):
+    copy = pltpu.make_async_copy(proj_hbm, proj_ref, sem)
+    copy.start()
+    grad_heads = mm_rt(scaled_ref[...], out_ref[...]).astype(BF)
     grads = attend_back(
         packed_ref[0], packed_ref[1], packed_ref[2], grad_heads, weights_ref[...]
     )
-    total = mm_rt(grads[0], proj_ref[0]) + mm_rt(grads[1], proj_ref[1])
-    partial_ref[...] = (total + mm_rt(grads[2], proj_ref[2])).astype(BF)
+    copy.wait()
+    total = mm(grads[0], proj_ref[0]) + mm(grads[1], proj_ref[1])
+    partial_ref[...] = (total + mm(grads[2], proj_ref[2])).astype(BF)
 
 
 def latent_step(x_ref, mod_ref, grad_ref, mine_ref, other_ref, latent_ref):
     incoming = mine_ref[...].astype(F32) + other_ref[...].astype(F32)
-    latent_ref[...] = grad_ref[...] + norm_back(x_ref[...].astype(F32), mod_ref[1:2], incoming)
+    latent_ref[...] = grad_ref[...] + norm_back(x_ref[...].astype(F32), mod_ref[1], incoming)
 
 
 def output_step(middle_ref, mod_ref, mine_ref, other_ref, block_ref):
     mixed = mine_ref[...].astype(F32) + other_ref[...].astype(F32)
-    block_ref[...] = (middle_ref[...] + mod_ref[5:6] * mixed).astype(BF)
+    block_ref[...] = (middle_ref[...] + mod_ref[5] * mixed).astype(BF)
 
 
 def weight_products(*refs):
     wire_ref = refs[-1]
-    totals = []
-    for which in range(2):
-        base = which * 2 * DP
-        total = mm_lt(refs[base][...], refs[base + DP][...])
-        for i in range(1, DP):
-            total = total + mm_lt(refs[base + i][...], refs[base + DP + i][...])
-        totals.append(total.astype(BF))
-    rows = totals[0].shape[0]
-    part = rows // SEQ
-    shape = (SEQ * ROWS, rows)
-    row = lax.broadcasted_iota(jnp.int32, shape, 0)
-    column = lax.broadcasted_iota(jnp.int32, (1, rows), 1)
-    held = ROWS * (column // part) + column % part
-    first = (row == held).astype(F32).astype(BF)
-    second = (row == held + part).astype(F32).astype(BF)
-    wire_ref[...] = (mm(first, totals[0]) + mm(second, totals[1])).astype(BF)
+    own_s, *near_s = refs[:DP]
+    own_t, heads_s, heads_t = refs[DP : DP + 3]
+    near_t = refs[DP + 3 : 2 * DP + 2]
+    heads_near = refs[2 * DP + 2 : 3 * DP + 1]
+    local = heads_s.shape[1]
+    spatial = mm_lt(own_s[...], heads_s[...])
+    temporal = mm_lt(own_t[...], heads_t[...])
+    for i in range(DP - 1):
+        spatial = spatial + mm_lt(near_s[i][...], near_t[i][:, :local])
+        temporal = temporal + mm_lt(near_t[i][:, local:], heads_near[i][...])
+    cut = spatial.shape[0] // X_RING
+    for i in range(X_RING):
+        rows = slice(i * cut, (i + 1) * cut)
+        wire_ref[i] = jnp.concatenate([spatial[rows], temporal[rows]], axis=0).astype(BF)
+
+
+def add_sources(arrived_ref):
+    total = arrived_ref[0].astype(F32)
+    for i in range(1, arrived_ref.shape[0]):
+        total = total + arrived_ref[i].astype(F32)
+    return total
+
+
+def weight_halfway(arrived_ref, wire_ref):
+    total = add_sources(arrived_ref).astype(BF)
+    rows = total.shape[0]
+    part = rows // 2 // Z_RING
+    index = lax.broadcasted_iota(jnp.int32, (1, rows), 1)
+    which, index = index // (rows // 2), index % (rows // 2)
+    held = ROWS * (index // part) + part * which + index % part
+    place = lax.broadcasted_iota(jnp.int32, (Z_RING * ROWS, rows), 0) == held
+    wire_ref[...] = mm(place.astype(F32).astype(BF), total).astype(BF).reshape(wire_ref.shape)
 
 
 def weight_sums(arrived_ref, spatial_ref, temporal_ref):
     part = spatial_ref.shape[0]
-    shape = (16, SEQ * ROWS)
-    row = lax.broadcasted_iota(jnp.int32, shape, 0)
-    column = lax.broadcasted_iota(jnp.int32, shape, 1) % ROWS
-    arrived = arrived_ref[...]
-    for start, ref in ((0, spatial_ref), (part, temporal_ref)):
-        take = (column == row + start).astype(F32).astype(BF)
-        ref[...] = mm(take, arrived)[:part]
-
-
-def call(body, outs, *operands, scalars=0, scratch=(), flops=0):
+    total = add_sources(arrived_ref)
+    spatial_ref[...] = total[:part]
+    temporal_ref[...] = total[part : 2 * part]
+
+
+def call(body, outs, *operands, scalars=0, apart=(), scratch=(), flops=0, vmem=40):
     specs = [pl.BlockSpec(memory_space=pltpu.SMEM)] * scalars
     specs += [pl.BlockSpec(memory_space=pltpu.VMEM)] * (len(operands) - scalars)
+    whole = pl.BlockSpec(memory_space=pltpu.VMEM)
+    for i in apart:
+        specs[i] = pl.BlockSpec(memory_space=pl.ANY)
     shapes = [jax.ShapeDtypeStruct(shape, dtype) for shape, dtype in outs]
     moved = sum(x.size * x.dtype.itemsize for x in [*operands, *shapes])
     single = len(shapes) == 1
@@ -231,10 +270,10 @@
         body,
         out_shape=shapes[0] if single else shapes,
         in_specs=specs,
-        out_specs=specs[-1] if single else [specs[-1]] * len(shapes),
+        out_specs=whole if single else [whole] * len(shapes),
         scratch_shapes=list(scratch),
         cost_estimate=pl.CostEstimate(flops=flops, bytes_accessed=moved, transcendentals=0),
-        compiler_params=pltpu.CompilerParams(vmem_limit_bytes=40 * 1024 * 1024),
+        compiler_params=pltpu.CompilerParams(vmem_limit_bytes=vmem * 1024 * 1024),
     )(*operands)
 
 
@@ -251,6 +290,12 @@
     cut = array.reshape(SEQ, rows // SEQ, width)
     moved = lax.all_to_all(cut, "seq", split_axis=0, concat_axis=0, tiled=True)
     return moved.reshape(rows, width)
+
+
+def group_all_to_all(array, groups):
+    return lax.all_to_all(
+        array, "seq", split_axis=0, concat_axis=0, tiled=True, axis_index_groups=groups
+    )
 
 
 def per_device(
@@ -261,9 +306,11 @@
     heads = local // HEAD_DIM
     x = latents.reshape(tokens, width)
     cot = cotangent.reshape(tokens, width)
-    mod = modulation.reshape(-1, width)
-    proj_s = proj_spatial.transpose(1, 0, 2)
-    proj_t = proj_temporal.transpose(1, 0, 2)
+    mod = modulation.transpose(1, 0, 2)
+    proj_s = proj_spatial.transpose(1, 2, 0)
+    proj_t = proj_temporal.transpose(1, 2, 0)
+    out_s = out_spatial.T
+    out_t = out_temporal.T
     place = lax.axis_index("dp").astype(jnp.int32).reshape(1)
     wide = ((tokens, width), BF)
     narrow = ((tokens, local), BF)
@@ -277,27 +324,31 @@
     packed_s, weights_s, heads_s, mixed_s = call(
         spatial_forward,
         [((3, tokens, local), BF), ((heads * tokens, tokens), F32), narrow, wide],
-        x, mod, proj_s, out_spatial, flops=4 * product + attention,
+        x, mod, proj_s, out_s, apart=(2, 3), flops=4 * product + attention, vmem=60,
+        scratch=[
+            pltpu.VMEM(proj_s.shape, BF),
+            pltpu.VMEM(out_s.shape, BF),
+            pltpu.SemaphoreType.DMA((4,)),
+        ],
     )
     mixed_other = swap_pair(mixed_s)
-    grad_heads_t, *blocks_t = call(
-        upstream_start, [narrow] + [block] * DP,
-        place, cot, mod, out_temporal, scalars=1, scratch=[held], flops=product,
+    bundle = ((tokens, local + width // DP), BF)
+    grad_heads_t, own_t, *bundles = call(
+        upstream_start, [narrow, block] + [bundle] * (DP - 1),
+        place, cot, mod, out_t, heads_s, scalars=1, scratch=[held], flops=product,
     )
     middle, wire_out = call(
         middle_step, [full, wire],
         x, mod, mixed_s, mixed_other, proj_t, grad_heads_t, flops=4 * product,
     )
+    near_t = [swap_dp(bundles[i], i + 1) for i in range(DP - 1)]
     arrived = all_to_all(wire_out)
-    heads_all_s = [heads_s] + [swap_dp(heads_s, i) for i in range(1, DP)]
-    blocks_t = blocks_t[:1] + [swap_dp(blocks_t[i], i) for i in range(1, DP)]
+    arrived, *near_t = lax.optimization_barrier((arrived, *near_t))
     wire_back = call(temporal_step, [wire], arrived, flops=6 * attention)
     returned = all_to_all(wire_back)
     partial_t, heads_t = call(temporal_return, [wide, narrow], returned, proj_t, flops=4 * product)
     partial_other = swap_pair(partial_t)
-    mixed_t = call(mix_temporal, [wide], heads_t, out_temporal, flops=product)
-    heads_all_t = [heads_t] + [swap_dp(heads_t, i) for i in range(1, DP)]
-    mixed_t_other = swap_pair(mixed_t)
+    heads_near = [swap_dp(heads_t, i) for i in range(1, DP)]
     grad_middle, scaled_s, *blocks_s = call(
         middle_back, [full, wide] + [block] * DP,
         place, cot, middle, mod, partial_t, partial_other, scalars=1, scratch=[held],
@@ -305,14 +356,22 @@
     blocks_s = blocks_s[:1] + [swap_dp(blocks_s[i], i) for i in range(1, DP)]
     partial_s = call(
         spatial_back, [wide],
-        scaled_s, packed_s, weights_s, out_spatial, proj_s, flops=4 * product + 5 * attention,
+        scaled_s, packed_s, weights_s, out_s, proj_s, apart=(4,),
+        scratch=[pltpu.VMEM(proj_s.shape, BF), pltpu.SemaphoreType.DMA],
+        flops=4 * product + 5 * attention,
     )
     partial_s_other = swap_pair(partial_s)
+    cut = 2 * width // DP // X_RING
     sums_out = call(
-        weight_products, [((SEQ * ROWS, local), BF)],
-        *blocks_s, *heads_all_s, *blocks_t, *heads_all_t, flops=4 * product,
-    )
-    sums_in = all_to_all(sums_out)
+        weight_products, [((X_RING, cut, local), BF)],
+        *blocks_s, own_t, heads_s, heads_t, *near_t, *heads_near, flops=4 * product,
+    )
+    sums_half = group_all_to_all(sums_out, X_GROUPS)
+    sums_half = call(weight_halfway, [((Z_RING, ROWS, local), BF)], sums_half)
+    sums_in = group_all_to_all(sums_half, Z_GROUPS)
+    heads_late, partial_s_other = lax.optimization_barrier((heads_t, partial_s_other))
+    mixed_t = call(mix_temporal, [wide], heads_late, out_t, flops=product)
+    mixed_t_other = swap_pair(mixed_t)
     block_output = call(output_step, [wide], middle, mod, mixed_t, mixed_t_other)
     latent_grad = call(latent_step, [full], x, mod, grad_middle, partial_s, partial_s_other)
     part = ((width // DP // SEQ, local), F32)

time: 166 us -> 141 us (0.85)
  blocking collectives: 55.7 us -> 26 us
  local copies, waits for them, and re-layouts: 31.2 us -> 15.6 us
  starting transfers between devices: 25.3 us -> 34.5 us
  waiting for transfers between devices: 29.1 us -> 36.8 us
  Pallas kernels: 23.3 us -> 26.9 us
    all_to_all x2 -> x1, blocking collectives: 55.7 us -> 26 us  [all_to_all(): moved = lax.all_to_all(cut, 'seq', split_axis=0, concat_axis=0, tiled=True)]
    unnamed x49 -> x50, local copies, waits for them, and re-layouts: 31.2 us -> 15.6 us
    ppermute x4, waiting for transfers between devices: 5.74 us -> 14.8 us  [swap_pair(): return lax.ppermute(array, 'tensor', PAIR)]
    all_to_all x0 -> x2, starting transfers between devices: none -> 7.24 us  [group_all_to_all(): lax.all_to_all(array, 'seq', split_axis=0, concat_axis=0, tiled=True, axi...]
    all_to_all x1, starting transfers between devices: 6.37 us -> 11.2 us  [all_to_all(): moved = lax.all_to_all(cut, 'seq', split_axis=0, concat_axis=0, tiled=True)]
    pallas_call x12 -> x13, Pallas kernels: 23.3 us -> 26.9 us  [call(): pl.pallas_call(body, out_shape=shapes[0] if single else shapes, in_specs=...]
    all_to_all x1, waiting for transfers between devices: 7.98 us -> 4.52 us  [all_to_all(): moved = lax.all_to_all(cut, 'seq', split_axis=0, concat_axis=0, tiled=True)]
    ppermute x12 -> x9, starting transfers between devices: 14.2 us -> 11 us  [swap_dp(): return lax.ppermute(array, 'dp', [(i, i ^ mask) for i in range(DP)])]
  transfers between devices with their start and end apart: 17 -> 16, of which waited for: 8 -> 10; matrix products, arithmetic and copies ran while one was open for 5% -> 0% of each run, Pallas kernels for 4% -> 7%
where the time goes in v2:
time: 141 us
  waiting for transfers between devices  36.8 us (26%)
  starting transfers between devices  34.5 us (24%)
  Pallas kernels  26.9 us (19%)
  blocking collectives  26 us (18%)
  local copies, waits for them, and re-layouts  15.6 us (11%)
    pallas_call x13, Pallas kernels, call(): pl.pallas_call(body, out_shape=shapes[0] if single else shapes, in_specs=...  26.9 us
    all_to_all x1, blocking collectives, all_to_all(): moved = lax.all_to_all(cut, 'seq', split_axis=0, concat_axis=0, tiled=True)  26 us
    unnamed x50, local copies, waits for them, and re-layouts  15.6 us
    ppermute x9, waiting for transfers between devices, swap_dp(): return lax.ppermute(array, 'dp', [(i, i ^ mask) for i in range(DP)])  15.5 us
    ppermute x4, waiting for transfers between devices, swap_pair(): return lax.ppermute(array, 'tensor', PAIR)  14.8 us
    all_to_all x1, starting transfers between devices, all_to_all(): moved = lax.all_to_all(cut, 'seq', split_axis=0, concat_axis=0, tiled=True)  11.2 us
    ppermute x9, starting transfers between devices, swap_dp(): return lax.ppermute(array, 'dp', [(i, i ^ mask) for i in range(DP)])  11 us
    all_to_all x2, starting transfers between devices, group_all_to_all(): lax.all_to_all(array, 'seq', split_axis=0, concat_axis=0, tiled=True, axi...  7.24 us
  transfers between devices with their start and end apart: 16, of which 10 were waited for; matrix products, arithmetic and copies ran while one was open for 0% of the time, Pallas kernels for 7%

profile of v2, /device:TPU:32, one launch (start us, length us, event | category | flops | bytes accessed | tf_op | source)
XLA Modules:
  0.0 140.7 jit_solution(17084633320730778602)
XLA Ops:
  0.7 6.5 %shard_map.102 = (bf16[3,128,576]{2,1,0:T(8,128)(2,1)}, f32[1024,128]{1,0:T(8,128)}, bf16[128,576]{1,0:T(8,128)(2,1)}, bf16[128,1152]{1,0:T(8,128)(2,1)}) custom-call(bf16[128,1152]{1,0:T(8,128)(2,1)} %bitcast.20, f32[6,1,1152]{2,1,0:T(1,128)} %bitcast.28, bf16[3,576,1152]{2,1,0:T(8,128)(2,1)} %bitcast.18, bf16[576,1152]{1,0:T(8,128)(2,1)} %bitcast.24), custom_call_target="tpu_custom_call" | custom-call | flops 981467136 | bytes 7040000 | tf_op jit(solution)/shard_map/pallas_call | solution.py:269
  11.8 4.5 %collective-permute-done.other_ref = bf16[128,1152]{1,0:T(8,128)(2,1)S(1)} collective-permute-done((bf16[128,1152]{1,0:T(8,128)(2,1)}, bf16[128,1152]{1,0:T(8,128)(2,1)S(1)}, u32[]{:S(2)}, u32[]{:S(2)}) %collective-permute-start) | collective-permute-done | bytes 294944 | tf_op jit(solution)/shard_map/ppermute | solution.py:281
  16.3 2.1 %copy-done = bf16[1152,3,576]{0,2,1:T(8,128)(2,1)S(1)} copy-done((bf16[1152,3,576]{0,2,1:T(8,128)(2,1)S(1)}, bf16[1152,3,576]{0,2,1:T(8,128)(2,1)}, u32[]{:S(2)}) %copy-start) | copy-done | bytes 3981336
  19.4 3.0 %shard_map.104 = (f32[128,1152]{1,0:T(8,128)S(1)}, bf16[512,576]{1,0:T(8,128)(2,1)}) custom-call(bf16[128,1152]{1,0:T(8,128)(2,1)S(1)} %bitcast.21, f32[6,1,1152]{2,1,0:T(1,128)S(1)} %bitcast.30, bf16[128,1152]{1,0:T(8,128)(2,1)S(1)} %copy-done.12, bf16[128,1152]{1,0:T(8,128)(2,1)S(1)} %collective-permute-done.other_ref, bf16[3,576,1152]{2,1,0:T(8,128)(2,1)S(1)} %bitcast.14, ...), custom_call_target="tpu_custom_call" | custom-call | flops 679477248 | bytes 6220800 | tf_op jit(solution)/shard_map/pallas_call | solution.py:269
  22.3 11.2 %all-to-all-start = ((bf16[32,16,576]{2,1,0:T(8,128)(2,1)}), bf16[32,16,576]{2,1,0:T(8,128)(2,1)S(1)}, u32[]{:S(2)}, u32[]{:S(2)}) async-start(bf16[32,16,576]{2,1,0:T(8,128)(2,1)} %bitcast.8), calls=%async_computation | async-start | bytes 1310720 | tf_op jit(solution)/shard_map/all_to_all | solution.py:291
  33.6 3.3 %collective-permute-start.2 = (bf16[128,864]{1,0:T(8,128)(2,1)}, bf16[128,864]{1,0:T(8,128)(2,1)S(1)}, u32[]{:S(2)}, u32[]{:S(2)}) collective-permute-start(bf16[128,864]{1,0:T(8,128)(2,1)} %copy-done.23), channel_id=1, source_target_pairs={{0,128},{64,192},{128,0},{192,64},{1,129},{65,193},{129,1},{193,65... | collective-permute-start | bytes 663560 | tf_op jit(solution)/shard_map/ppermute | solution.py:285
  37.7 6.1 %collective-permute-done.2.refs_8_ = bf16[128,864]{1,0:T(8,128)(2,1)S(1)} collective-permute-done((bf16[128,864]{1,0:T(8,128)(2,1)}, bf16[128,864]{1,0:T(8,128)(2,1)S(1)}, u32[]{:S(2)}, u32[]{:S(2)}) %collective-permute-start.2) | collective-permute-done | bytes 221216 | tf_op jit(solution)/shard_map/ppermute | solution.py:285
  44.5 3.3 %collective-permute-done.3.refs_9_ = bf16[128,864]{1,0:T(8,128)(2,1)S(1)} collective-permute-done((bf16[128,864]{1,0:T(8,128)(2,1)S(1)}, bf16[128,864]{1,0:T(8,128)(2,1)S(1)}, u32[]{:S(2)}, u32[]{:S(2)}) %collective-permute-start.3) | collective-permute-done | bytes 221216 | tf_op jit(solution)/shard_map/ppermute | solution.py:285
  48.5 4.5 %all-to-all-done = bf16[32,16,576]{2,1,0:T(8,128)(2,1)S(1)} async-done(((bf16[32,16,576]{2,1,0:T(8,128)(2,1)}), bf16[32,16,576]{2,1,0:T(8,128)(2,1)S(1)}, u32[]{:S(2)}, u32[]{:S(2)}) %all-to-all-start) | async-done | bytes 589856 | tf_op jit(solution)/shard_map/all_to_all | solution.py:291
  53.0 3.4 %shard_map.105 = bf16[512,576]{1,0:T(8,128)(2,1)S(1)} custom-call(bf16[512,576]{1,0:T(8,128)(2,1)S(1)} %bitcast.34), custom_call_target="tpu_custom_call" | custom-call | flops 1811939328 | bytes 1179648 | tf_op jit(solution)/shard_map/pallas_call | solution.py:269
  56.5 26.0 %all_to_all.20 = bf16[32,16,576]{2,1,0:T(8,128)(2,1)S(1)} all-to-all(bf16[32,16,576]{2,1,0:T(8,128)(2,1)S(1)} %bitcast.35), channel_id=1, replica_groups=mesh['dp'=4,'seq'=32,'tensor'=2] {'seq'}, dimensions={0} | all-to-all | bytes 1179648 | tf_op jit(solution)/shard_map/all_to_all | solution.py:291
  86.1 2.9 %collective-permute-start.11 = (bf16[128,576]{1,0:T(8,128)(2,1)S(1)}, bf16[128,576]{1,0:T(8,128)(2,1)S(1)}, u32[]{:S(2)}, u32[]{:S(2)}) collective-permute-start(bf16[128,576]{1,0:T(8,128)(2,1)S(1)} %get-tuple-element.45.heads_ref.refs_6_), channel_id=1, source_target_pairs={{0,128},{64,192},{128,0},{192,64},{1,129},{65,193},{129,1},{193,65... | collective-permute-start | bytes 442376 | tf_op jit(solution)/shard_map/ppermute | solution.py:285
  89.5 4.1 %collective-permute-done.4.other_ref = bf16[128,1152]{1,0:T(8,128)(2,1)S(1)} collective-permute-done((bf16[128,1152]{1,0:T(8,128)(2,1)S(1)}, bf16[128,1152]{1,0:T(8,128)(2,1)S(1)}, u32[]{:S(2)}, u32[]{:S(2)}) %collective-permute-start.4) | collective-permute-done | bytes 294944 | tf_op jit(solution)/shard_map/ppermute | solution.py:281
  95.7 4.0 %collective-permute-start.8 = (bf16[128,288]{1,0:T(8,128)(2,1)S(1)}, bf16[128,288]{1,0:T(8,128)(2,1)S(1)}, u32[]{:S(2)}, u32[]{:S(2)}) collective-permute-start(bf16[128,288]{1,0:T(8,128)(2,1)S(1)} %get-tuple-element.50), channel_id=1, source_target_pairs={{0,128},{64,192},{128,0},{192,64},{1,129},{65,193},{129,1},{193,65... | collective-permute-start | bytes 221192 | tf_op jit(solution)/shard_map/ppermute | solution.py:285
  100.0 3.6 %collective-permute-done.8.refs_2_ = bf16[128,288]{1,0:T(8,128)(2,1)S(1)} collective-permute-done((bf16[128,288]{1,0:T(8,128)(2,1)S(1)}, bf16[128,288]{1,0:T(8,128)(2,1)S(1)}, u32[]{:S(2)}, u32[]{:S(2)}) %collective-permute-start.8) | collective-permute-done | bytes 73760 | tf_op jit(solution)/shard_map/ppermute | solution.py:285
  103.5 2.5 %collective-permute-done.9.refs_3_ = bf16[128,288]{1,0:T(8,128)(2,1)S(1)} collective-permute-done((bf16[128,288]{1,0:T(8,128)(2,1)S(1)}, bf16[128,288]{1,0:T(8,128)(2,1)S(1)}, u32[]{:S(2)}, u32[]{:S(2)}) %collective-permute-start.9) | collective-permute-done | bytes 73760 | tf_op jit(solution)/shard_map/ppermute | solution.py:285
  107.9 3.5 %all-to-all-start.2 = ((bf16[4,144,576]{2,1,0:T(8,128)(2,1)}), bf16[4,144,576]{2,1,0:T(8,128)(2,1)S(1)}, u32[]{:S(2)}, u32[]{:S(2)}) async-start(bf16[4,144,576]{2,1,0:T(8,128)(2,1)} %shard_map.112), calls=%async_computation.2 | async-start | bytes 1474560 | tf_op jit(solution)/shard_map/all_to_all | solution.py:296
  111.4 2.1 %copy-done.3 = bf16[1152,3,576]{0,2,1:T(8,128)(2,1)S(1)} copy-done((bf16[1152,3,576]{0,2,1:T(8,128)(2,1)S(1)}, bf16[1152,3,576]{0,2,1:T(8,128)(2,1)}, u32[]{:S(2)}) %copy-start.3) | copy-done | bytes 3981336
  116.9 4.0 %shard_map.108.mine_ref = bf16[128,1152]{1,0:T(8,128)(2,1)} custom-call(bf16[128,1152]{1,0:T(8,128)(2,1)S(1)} %copy-done.22, bf16[3,128,576]{2,1,0:T(8,128)(2,1)S(1)} %copy-done.20, f32[1024,128]{1,0:T(8,128)S(1)} %copy-done.19, bf16[576,1152]{1,0:T(8,128)(2,1)S(1)} %bitcast.25, bf16[3,576,1152]{2,1,0:T(8,128)(2,1)S(1)} %bitcast.19), custom_call_target="tpu_custom_call" | custom-call | flops 2189426688 | bytes 6864896 | tf_op jit(solution)/shard_map/pallas_call | solution.py:269
  121.7 2.0 %all-to-all-done.2.arrived_ref = bf16[4,144,576]{2,1,0:T(8,128)(2,1)S(1)} async-done(((bf16[4,144,576]{2,1,0:T(8,128)(2,1)}), bf16[4,144,576]{2,1,0:T(8,128)(2,1)S(1)}, u32[]{:S(2)}, u32[]{:S(2)}) %all-to-all-start.2) | async-done | bytes 663584 | tf_op jit(solution)/shard_map/all_to_all | solution.py:296
  124.7 3.7 %all-to-all-start.3 = ((bf16[8,24,576]{2,1,0:T(8,128)(2,1)}), bf16[8,24,576]{2,1,0:T(8,128)(2,1)S(1)}, u32[]{:S(2)}, u32[]{:S(2)}) async-start(bf16[8,24,576]{2,1,0:T(8,128)(2,1)} %shard_map.113), calls=%async_computation.3 | async-start | bytes 491520 | tf_op jit(solution)/shard_map/all_to_all | solution.py:296
  128.5 2.0 %collective-permute-done.5.other_ref = bf16[128,1152]{1,0:T(8,128)(2,1)} collective-permute-done((bf16[128,1152]{1,0:T(8,128)(2,1)}, bf16[128,1152]{1,0:T(8,128)(2,1)}, u32[]{:S(2)}, u32[]{:S(2)}) %collective-permute-start.5) | collective-permute-done | bytes 294944 | tf_op jit(solution)/shard_map/ppermute | solution.py:281
  132.7 2.3 %shard_map.111 = f32[128,1152]{1,0:T(8,128)} custom-call(bf16[128,1152]{1,0:T(8,128)(2,1)S(1)} %bitcast.22, f32[6,1,1152]{2,1,0:T(1,128)S(1)} %bitcast.32, f32[128,1152]{1,0:T(8,128)S(1)} %copy-done.11, bf16[128,1152]{1,0:T(8,128)(2,1)} %shard_map.108.mine_ref, bf16[128,1152]{1,0:T(8,128)(2,1)} %collective-permute-done.5.other_ref), custom_call_target="tpu_custom_call" | custom-call | bytes 2092032 | tf_op jit(solution)/shard_map/pallas_call | solution.py:269
  135.0 4.2 %collective-permute-done.6.other_ref = bf16[128,1152]{1,0:T(8,128)(2,1)S(1)} collective-permute-done((bf16[128,1152]{1,0:T(8,128)(2,1)S(1)}, bf16[128,1152]{1,0:T(8,128)(2,1)S(1)}, u32[]{:S(2)}, u32[]{:S(2)}) %collective-permute-start.6) | collective-permute-done | bytes 294944 | tf_op jit(solution)/shard_map/ppermute | solution.py:281
  (72 shorter events, 24.9 us)
Async XLA Ops:
  0.6 15.7 %copy-start.4 = (bf16[1,1,128,1152]{3,2,1,0:T(8,128)(2,1)S(1)}, bf16[1,1,128,1152]{3,2,1,0:T(8,128)(2,1)}, u32[]{:S(2)}) copy-start(bf16[1,1,128,1152]{3,2,1,0:T(8,128)(2,1)} %param.7) | copy-start | bytes 884740
  0.6 8.3 %copy-start.7 = (f32[1,6,1152]{2,0,1:T(1,128)S(1)}, f32[1,6,1152]{2,0,1:T(1,128)}, u32[]{:S(2)}) copy-start(f32[1,6,1152]{2,0,1:T(1,128)} %param.8) | copy-start | bytes 82948
  7.2 9.1 %collective-permute-start = (bf16[128,1152]{1,0:T(8,128)(2,1)}, bf16[128,1152]{1,0:T(8,128)(2,1)S(1)}, u32[]{:S(2)}, u32[]{:S(2)}) collective-permute-start(bf16[128,1152]{1,0:T(8,128)(2,1)} %get-tuple-element.31.mine_ref), channel_id=1, source_target_pairs={{0,1},{1,0},{2,3},{3,2},{4,5},{5,4},{6,7},{7,6},{8,9},{9,8},{10,11... | collective-permute-start | bytes 884744 | tf_op jit(solution)/shard_map/ppermute | solution.py:281
  22.3 30.7 %all-to-all-start = ((bf16[32,16,576]{2,1,0:T(8,128)(2,1)}), bf16[32,16,576]{2,1,0:T(8,128)(2,1)S(1)}, u32[]{:S(2)}, u32[]{:S(2)}) async-start(bf16[32,16,576]{2,1,0:T(8,128)(2,1)} %bitcast.8), calls=%async_computation | async-start | bytes 1310720 | tf_op jit(solution)/shard_map/all_to_all | solution.py:291
  33.5 3.5 %collective-permute-start.1 = (bf16[128,864]{1,0:T(8,128)(2,1)}, bf16[128,864]{1,0:T(8,128)(2,1)S(1)}, u32[]{:S(2)}, u32[]{:S(2)}) collective-permute-start(bf16[128,864]{1,0:T(8,128)(2,1)} %copy-done.24), channel_id=1, source_target_pairs={{0,64},{64,0},{128,192},{192,128},{1,65},{65,1},{129,193},{193,129... | collective-permute-start | bytes 663560 | tf_op jit(solution)/shard_map/ppermute | solution.py:285
  33.6 10.2 %collective-permute-start.2 = (bf16[128,864]{1,0:T(8,128)(2,1)}, bf16[128,864]{1,0:T(8,128)(2,1)S(1)}, u32[]{:S(2)}, u32[]{:S(2)}) collective-permute-start(bf16[128,864]{1,0:T(8,128)(2,1)} %copy-done.23), channel_id=1, source_target_pairs={{0,128},{64,192},{128,0},{192,64},{1,129},{65,193},{129,1},{193,65... | collective-permute-start | bytes 663560 | tf_op jit(solution)/shard_map/ppermute | solution.py:285
  36.9 10.9 %collective-permute-start.3 = (bf16[128,864]{1,0:T(8,128)(2,1)S(1)}, bf16[128,864]{1,0:T(8,128)(2,1)S(1)}, u32[]{:S(2)}, u32[]{:S(2)}) collective-permute-start(bf16[128,864]{1,0:T(8,128)(2,1)S(1)} %get-tuple-element.38), channel_id=1, source_target_pairs={{0,192},{64,128},{128,64},{192,0},{1,193},{65,129},{129,65},{193,1... | collective-permute-start | bytes 663560 | tf_op jit(solution)/shard_map/ppermute | solution.py:285
  53.0 29.4 %copy-start.1 = (bf16[1152,3,576]{0,2,1:T(8,128)(2,1)S(1)}, bf16[1152,3,576]{0,2,1:T(8,128)(2,1)}, u32[]{:S(2)}) copy-start(bf16[1152,3,576]{0,2,1:T(8,128)(2,1)} %param.12) | copy-start | bytes 11943940
  56.4 49.6 %copy-start.9 = (bf16[128,576]{1,0:T(8,128)(2,1)S(1)}, bf16[128,576]{1,0:T(8,128)(2,1)}, u32[]{:S(2)}) copy-start(bf16[128,576]{1,0:T(8,128)(2,1)} %get-tuple-element.32.heads_ref.refs_5_) | copy-start | bytes 442372
  56.4 49.6 %copy-start.14 = (bf16[128,864]{1,0:T(8,128)(2,1)S(1)}, bf16[128,864]{1,0:T(8,128)(2,1)}, u32[]{:S(2)}) copy-start(bf16[128,864]{1,0:T(8,128)(2,1)} %copy-done.13) | copy-start | bytes 663556
  56.4 49.6 %copy-start.16 = (bf16[128,864]{1,0:T(8,128)(2,1)S(1)}, bf16[128,864]{1,0:T(8,128)(2,1)}, u32[]{:S(2)}) copy-start(bf16[128,864]{1,0:T(8,128)(2,1)} %copy-done.15) | copy-start | bytes 663556
  56.4 49.6 %copy-start.18 = (bf16[128,864]{1,0:T(8,128)(2,1)S(1)}, bf16[128,864]{1,0:T(8,128)(2,1)}, u32[]{:S(2)}) copy-start(bf16[128,864]{1,0:T(8,128)(2,1)} %copy-done.17) | copy-start | bytes 663556
  84.2 9.4 %collective-permute-start.4 = (bf16[128,1152]{1,0:T(8,128)(2,1)S(1)}, bf16[128,1152]{1,0:T(8,128)(2,1)S(1)}, u32[]{:S(2)}, u32[]{:S(2)}) collective-permute-start(bf16[128,1152]{1,0:T(8,128)(2,1)S(1)} %get-tuple-element.41.mine_ref), channel_id=1, source_target_pairs={{0,1},{1,0},{2,3},{3,2},{4,5},{5,4},{6,7},{7,6},{8,9},{9,8},{10,11... | collective-permute-start | bytes 884744 | tf_op jit(solution)/shard_map/ppermute | solution.py:281
  86.1 13.7 %collective-permute-start.10 = (bf16[128,576]{1,0:T(8,128)(2,1)S(1)}, bf16[128,576]{1,0:T(8,128)(2,1)S(1)}, u32[]{:S(2)}, u32[]{:S(2)}) collective-permute-start(bf16[128,576]{1,0:T(8,128)(2,1)S(1)} %get-tuple-element.45.heads_ref.refs_6_), channel_id=1, source_target_pairs={{0,64},{64,0},{128,192},{192,128},{1,65},{65,1},{129,193},{193,129... | collective-permute-start | bytes 442376 | tf_op jit(solution)/shard_map/ppermute | solution.py:285
  86.1 13.9 %collective-permute-start.11 = (bf16[128,576]{1,0:T(8,128)(2,1)S(1)}, bf16[128,576]{1,0:T(8,128)(2,1)S(1)}, u32[]{:S(2)}, u32[]{:S(2)}) collective-permute-start(bf16[128,576]{1,0:T(8,128)(2,1)S(1)} %get-tuple-element.45.heads_ref.refs_6_), channel_id=1, source_target_pairs={{0,128},{64,192},{128,0},{192,64},{1,129},{65,193},{129,1},{193,65... | collective-permute-start | bytes 442376 | tf_op jit(solution)/shard_map/ppermute | solution.py:285
  89.0 11.0 %collective-permute-start.12 = (bf16[128,576]{1,0:T(8,128)(2,1)S(1)}, bf16[128,576]{1,0:T(8,128)(2,1)S(1)}, u32[]{:S(2)}, u32[]{:S(2)}) collective-permute-start(bf16[128,576]{1,0:T(8,128)(2,1)S(1)} %get-tuple-element.45.heads_ref.refs_6_), channel_id=1, source_target_pairs={{0,192},{64,128},{128,64},{192,0},{1,193},{65,129},{129,65},{193,1... | collective-permute-start | bytes 442376 | tf_op jit(solution)/shard_map/ppermute | solution.py:285
  95.7 15.6 %copy-start.22 = (bf16[128,1152]{1,0:T(8,128)(2,1)S(1)}, bf16[128,1152]{1,0:T(8,128)(2,1)}, u32[]{:S(2)}) copy-start(bf16[128,1152]{1,0:T(8,128)(2,1)} %copy-done.21) | copy-start | bytes 884740
  95.7 4.2 %collective-permute-start.7 = (bf16[128,288]{1,0:T(8,128)(2,1)S(1)}, bf16[128,288]{1,0:T(8,128)(2,1)S(1)}, u32[]{:S(2)}, u32[]{:S(2)}) collective-permute-start(bf16[128,288]{1,0:T(8,128)(2,1)S(1)} %get-tuple-element.49), channel_id=1, source_target_pairs={{0,64},{64,0},{128,192},{192,128},{1,65},{65,1},{129,193},{193,129... | collective-permute-start | bytes 221192 | tf_op jit(solution)/shard_map/ppermute | solution.py:285
  95.7 7.8 %collective-permute-start.8 = (bf16[128,288]{1,0:T(8,128)(2,1)S(1)}, bf16[128,288]{1,0:T(8,128)(2,1)S(1)}, u32[]{:S(2)}, u32[]{:S(2)}) collective-permute-start(bf16[128,288]{1,0:T(8,128)(2,1)S(1)} %get-tuple-element.50), channel_id=1, source_target_pairs={{0,128},{64,192},{128,0},{192,64},{1,129},{65,193},{129,1},{193,65... | collective-permute-start | bytes 221192 | tf_op jit(solution)/shard_map/ppermute | solution.py:285
  99.8 6.2 %collective-permute-start.9 = (bf16[128,288]{1,0:T(8,128)(2,1)S(1)}, bf16[128,288]{1,0:T(8,128)(2,1)S(1)}, u32[]{:S(2)}, u32[]{:S(2)}) collective-permute-start(bf16[128,288]{1,0:T(8,128)(2,1)S(1)} %get-tuple-element.51), channel_id=1, source_target_pairs={{0,192},{64,128},{128,64},{192,0},{1,193},{65,129},{129,65},{193,1... | collective-permute-start | bytes 221192 | tf_op jit(solution)/shard_map/ppermute | solution.py:285
  107.9 15.8 %all-to-all-start.2 = ((bf16[4,144,576]{2,1,0:T(8,128)(2,1)}), bf16[4,144,576]{2,1,0:T(8,128)(2,1)S(1)}, u32[]{:S(2)}, u32[]{:S(2)}) async-start(bf16[4,144,576]{2,1,0:T(8,128)(2,1)} %shard_map.112), calls=%async_computation.2 | async-start | bytes 1474560 | tf_op jit(solution)/shard_map/all_to_all | solution.py:296
  121.0 9.5 %collective-permute-start.5 = (bf16[128,1152]{1,0:T(8,128)(2,1)}, bf16[128,1152]{1,0:T(8,128)(2,1)}, u32[]{:S(2)}, u32[]{:S(2)}) collective-permute-start(bf16[128,1152]{1,0:T(8,128)(2,1)} %shard_map.108.mine_ref), channel_id=1, source_target_pairs={{0,1},{1,0},{2,3},{3,2},{4,5},{5,4},{6,7},{7,6},{8,9},{9,8},{10,11... | collective-permute-start | bytes 884744 | tf_op jit(solution)/shard_map/ppermute | solution.py:281
  124.7 15.3 %all-to-all-start.3 = ((bf16[8,24,576]{2,1,0:T(8,128)(2,1)}), bf16[8,24,576]{2,1,0:T(8,128)(2,1)S(1)}, u32[]{:S(2)}, u32[]{:S(2)}) async-start(bf16[8,24,576]{2,1,0:T(8,128)(2,1)} %shard_map.113), calls=%async_computation.3 | async-start | bytes 491520 | tf_op jit(solution)/shard_map/all_to_all | solution.py:296
  130.9 8.4 %collective-permute-start.6 = (bf16[128,1152]{1,0:T(8,128)(2,1)S(1)}, bf16[128,1152]{1,0:T(8,128)(2,1)S(1)}, u32[]{:S(2)}, u32[]{:S(2)}) collective-permute-start(bf16[128,1152]{1,0:T(8,128)(2,1)S(1)} %shard_map.109.mine_ref), channel_id=1, source_target_pairs={{0,1},{1,0},{2,3},{3,2},{4,5},{5,4},{6,7},{7,6},{8,9},{9,8},{10,11... | collective-permute-start | bytes 884744 | tf_op jit(solution)/shard_map/ppermute | solution.py:281
  (17 other events, 32.1 us)

commit v3 on v2

v3 whole, which is shorter than its diff:
```python
import functools

import jax
import jax.numpy as jnp
from jax import lax
from jax.experimental import pallas as pl
from jax.experimental.pallas import tpu as pltpu
from jax.sharding import PartitionSpec as P

HEAD_DIM = 72
NORM_EPS = 1e-06
PAIR = ((0, 1), (1, 0))
DP = 4
SEQ = 32
BF = jnp.bfloat16
F32 = jnp.float32
ROWS = 24
X_RING = 4
Z_RING = 8
Z_GROUPS = tuple(tuple(z + Z_RING * x for z in range(Z_RING)) for x in range(X_RING))


def mm(left, right):
    return jnp.dot(left, right, preferred_element_type=F32)


def mm_rt(left, right):
    return lax.dot_general(left, right, (((1,), (1,)), ((), ())), preferred_element_type=F32)


def mm_lt(left, right):
    return lax.dot_general(left, right, (((0,), (0,)), ((), ())), preferred_element_type=F32)


def normalise(values):
    average = jnp.mean(values, axis=-1, keepdims=True)
    centred = values - average
    inverse = lax.rsqrt(jnp.mean(centred * centred, axis=-1, keepdims=True) + NORM_EPS)
    return centred * inverse, inverse


def norm_back(values, scale_row, incoming):
    unit, inverse = normalise(values)
    scaled = incoming * (1.0 + scale_row)
    mean_plain = jnp.mean(scaled, axis=-1, keepdims=True)
    mean_unit = jnp.mean(scaled * unit, axis=-1, keepdims=True)
    return inverse * (scaled - mean_plain - unit * mean_unit)


def stack_heads(values):
    width = values.shape[1]
    owner = lax.broadcasted_iota(jnp.int32, (1, width), 1) // HEAD_DIM
    parts = [values * (owner == head).astype(F32).astype(BF) for head in range(width // HEAD_DIM)]
    return jnp.concatenate(parts, axis=0)


def side_by_side(stacked):
    tokens = stacked.shape[1]
    heads = stacked.shape[0] // tokens
    return jnp.concatenate([stacked[h * tokens : (h + 1) * tokens] for h in range(heads)], axis=1)


def softmax_weights(queries, keys_in, same=None):
    scores = mm_rt(stack_heads(queries), keys_in) * HEAD_DIM**-0.5
    if same is not None:
        scores = jnp.where(same, scores, -1e30)
    raised = jnp.exp(scores - jnp.max(scores, axis=-1, keepdims=True))
    return raised / jnp.sum(raised, axis=-1, keepdims=True)


def attend_back(queries, keys_in, values_in, grad_out, weights):
    grad_stacked = stack_heads(grad_out)
    grad_weights = mm_rt(grad_stacked, values_in)
    inner_sum = jnp.sum(grad_weights * weights, axis=-1, keepdims=True)
    grad_scores = (weights * (grad_weights - inner_sum) * HEAD_DIM**-0.5).astype(BF)
    grad_queries = mm(side_by_side(grad_scores), stack_heads(keys_in)).astype(BF)
    grad_keys = mm_lt(grad_scores, stack_heads(queries)).astype(BF)
    grad_values = mm_lt(weights.astype(BF), grad_stacked).astype(BF)
    return grad_queries, grad_keys, grad_values


LANES = 128
QUARTERS = 4


def wire_slots(columns):
    slots = QUARTERS * columns // LANES
    return -(-slots // 8) * 8


def wire_pieces(columns):
    pieces, slot = [], 0
    for start in range(0, columns, LANES):
        wide = min(LANES, columns - start)
        for quarter in range(QUARTERS if wide == LANES else QUARTERS // 2):
            pieces.append((slot, start, wide, quarter))
            slot += 1
    return pieces, slot


def to_wire(arrays, held_ref, wire_ref):
    devices = arrays[0].shape[0] // QUARTERS
    slots = held_ref.shape[0] // devices
    base = 0
    for values in arrays:
        values = values.astype(F32)
        pieces, used = wire_pieces(values.shape[1])
        for slot, start, wide, quarter in pieces:
            part = values[quarter * devices : (quarter + 1) * devices, start : start + wide]
            if wide < LANES:
                later = (quarter + 2) * devices
                other = values[later : later + devices, start : start + wide]
                part = jnp.concatenate([part, other], axis=1)
            held_ref[pl.ds(base + slot, devices, stride=slots), :] = part
        base += used
    for slot in range(base, slots):
        held_ref[pl.ds(slot, devices, stride=slots), :] = jnp.zeros((devices, LANES), F32)
    wire_ref[...] = held_ref[...].astype(BF)


def from_wire(wire_ref, held_ref, widths):
    devices = SEQ
    slots = held_ref.shape[0] // devices
    held_ref[...] = wire_ref[...].astype(F32)
    base = 0
    arrays = []
    for columns in widths:
        pieces, used = wire_pieces(columns)
        tiles = {}
        for slot, start, wide, quarter in pieces:
            part = held_ref[pl.ds(base + slot, devices, stride=slots), :]
            if wide < LANES:
                tiles[start, quarter] = part[:, :wide]
                tiles[start, quarter + 2] = part[:, wide:]
            else:
                tiles[start, quarter] = part
        base += used
        starts = sorted({start for start, _ in tiles})
        columns_of = [
            jnp.concatenate([tiles[start, quarter] for quarter in range(QUARTERS)], axis=0)
            for start in starts
        ]
        arrays.append(jnp.concatenate(columns_of, axis=1))
    return arrays


def spatial_forward(
    x_ref, mod_ref, proj_ref, out_ref, packed_ref, weights_ref, heads_ref, mixed_ref
):
    unit, _ = normalise(x_ref[...].astype(F32))
    normed = (unit * (1.0 + mod_ref[1]) + mod_ref[0]).astype(BF)
    parts = []
    for i in range(3):
        parts.append(mm_rt(normed, proj_ref[i]).astype(BF))
        packed_ref[i] = parts[i]
    queries, keys_in, values_in = parts
    weights = softmax_weights(queries, keys_in)
    weights_ref[...] = weights
    heads = mm(side_by_side(weights.astype(BF)), stack_heads(values_in)).astype(BF)
    heads_ref[...] = heads
    mixed_ref[...] = mm(heads, out_ref[...]).astype(BF)


def split_columns(scaled, place, held_ref):
    piece = scaled.shape[1] // (DP * X_RING)
    for x_low in range(2):
        for core in range(2):
            starts = [
                ((far * 2 + core) * X_RING + x_high * 2 + x_low) * piece
                for far in range(2)
                for x_high in range(2)
            ]
            parts = [scaled[:, start : start + piece] for start in starts]
            held_ref[2 * x_low + core] = jnp.concatenate(parts, axis=1)
    return [held_ref[place ^ i] for i in range(DP)]


def upstream_start(
    place_ref, cot_ref, mod_ref, out_ref, x_ref, proj_ref, grad_ref, b0, b1, b2, b3, held_ref
):
    del x_ref, proj_ref
    scaled = (mod_ref[5] * cot_ref[...].astype(F32)).astype(BF)
    grad_ref[...] = mm_rt(scaled, out_ref[...]).astype(BF)
    for block, ref in zip(split_columns(scaled, place_ref[0], held_ref), (b0, b1, b2, b3)):
        ref[...] = block


def middle_step(
    x_ref, mine_ref, other_ref, mod_ref, grad_ref, proj_ref, wire_ref, middle_ref, held_ref
):
    mixed = mine_ref[...].astype(F32) + other_ref[...].astype(F32)
    middle = x_ref[...].astype(F32) + mod_ref[2] * mixed
    middle_ref[...] = middle
    unit, _ = normalise(middle)
    normed = (unit * (1.0 + mod_ref[4]) + mod_ref[3]).astype(BF)
    parts = [mm_rt(normed, proj_ref[i]).astype(BF) for i in range(3)]
    to_wire(parts + [grad_ref[...]], held_ref, wire_ref)


def temporal_step(arrived_ref, wire_ref, held_ref):
    local = arrived_ref.shape[0] * LANES // (QUARTERS * SEQ) // 4
    parts = from_wire(arrived_ref, held_ref, (local,) * 4)
    queries, keys_in, values_in, grad_out = [part.astype(BF) for part in parts]
    tokens = queries.shape[0]
    frames = tokens // QUARTERS
    stacked = (local // HEAD_DIM * tokens, tokens)
    row = lax.broadcasted_iota(jnp.int32, stacked, 0) % tokens
    column = lax.broadcasted_iota(jnp.int32, stacked, 1)
    weights = softmax_weights(queries, keys_in, row // frames == column // frames)
    out = mm(side_by_side(weights.astype(BF)), stack_heads(values_in)).astype(BF)
    grads = attend_back(queries, keys_in, values_in, grad_out, weights)
    to_wire(list(grads) + [out], held_ref, wire_ref)


def temporal_return(arrived_ref, proj_ref, partial_ref, heads_ref, held_ref):
    local = heads_ref.shape[1]
    parts = from_wire(arrived_ref, held_ref, (local,) * 4)
    *grads, heads = [part.astype(BF) for part in parts]
    heads_ref[...] = heads
    total = mm(grads[0], proj_ref[0]) + mm(grads[1], proj_ref[1])
    partial_ref[...] = (total + mm(grads[2], proj_ref[2])).astype(BF)


def mix_temporal(heads_ref, out_ref, mixed_ref):
    mixed_ref[...] = mm(heads_ref[...], out_ref[...]).astype(BF)


def middle_back(
    place_ref, cot_ref, middle_ref, mod_ref, mine_ref, other_ref, b0, b1, b2, b3, scaled_ref, grad_ref,
    held_ref,
):
    incoming = mine_ref[...].astype(F32) + other_ref[...].astype(F32)
    grad = cot_ref[...].astype(F32) + norm_back(middle_ref[...], mod_ref[4], incoming)
    scaled = (mod_ref[2] * grad).astype(BF)
    for block, ref in zip(split_columns(scaled, place_ref[0], held_ref), (b0, b1, b2, b3)):
        ref[...] = block
    scaled_ref[...] = scaled
    grad_ref[...] = grad


def spatial_back(scaled_ref, packed_ref, weights_ref, out_ref, proj_ref, partial_ref):
    grad_heads = mm_rt(scaled_ref[...], out_ref[...]).astype(BF)
    grads = attend_back(
        packed_ref[0], packed_ref[1], packed_ref[2], grad_heads, weights_ref[...]
    )
    total = mm(grads[0], proj_ref[0]) + mm(grads[1], proj_ref[1])
    partial_ref[...] = (total + mm(grads[2], proj_ref[2])).astype(BF)


def latent_step(x_ref, mod_ref, grad_ref, mine_ref, other_ref, latent_ref):
    incoming = mine_ref[...].astype(F32) + other_ref[...].astype(F32)
    latent_ref[...] = grad_ref[...] + norm_back(x_ref[...].astype(F32), mod_ref[1], incoming)


def output_step(middle_ref, mod_ref, mine_ref, other_ref, block_ref):
    mixed = mine_ref[...].astype(F32) + other_ref[...].astype(F32)
    block_ref[...] = (middle_ref[...] + mod_ref[5] * mixed).astype(BF)


def weight_products(place_ref, *refs):
    out_refs, held_ref = refs[4 * DP : -1], refs[-1]
    spatial, temporal = 0.0, 0.0
    for i in range(DP):
        temporal = temporal + mm_lt(refs[2 * DP + i][...], refs[3 * DP + i][...])
    for i in range(DP):
        spatial = spatial + mm_lt(refs[i][...], refs[DP + i][...])
    cut = spatial.shape[0] // DP
    for i in range(DP):
        rows = slice(i * cut, (i + 1) * cut)
        held_ref[i] = jnp.concatenate([spatial[rows], temporal[rows]], axis=0).astype(BF)
    for i in range(DP):
        out_refs[i][...] = held_ref[place_ref[0] ^ i]


def add_sources(parts):
    total = parts[0].astype(F32)
    for part in parts[1:]:
        total = total + part.astype(F32)
    return total


def weight_halfway(*refs):
    wire_ref = refs[-1]
    total = add_sources([ref[...] for ref in refs[:-1]]).astype(BF)
    rows = total.shape[0]
    part = rows // 2 // Z_RING
    index = lax.broadcasted_iota(jnp.int32, (1, rows), 1)
    which, index = index // (rows // 2), index % (rows // 2)
    held = ROWS * (index // part) + part * which + index % part
    place = lax.broadcasted_iota(jnp.int32, (Z_RING * ROWS, rows), 0) == held
    wire_ref[...] = mm(place.astype(F32).astype(BF), total).astype(BF).reshape(wire_ref.shape)


def weight_sums(arrived_ref, spatial_ref, temporal_ref):
    part = spatial_ref.shape[0]
    total = add_sources([arrived_ref[i] for i in range(arrived_ref.shape[0])])
    spatial_ref[...] = total[:part]
    temporal_ref[...] = total[part : 2 * part]


class Late:
    def __init__(self, source, target, sems):
        self.target = target
        self.shape = target.shape
        parts = self.shape[0] if len(self.shape) == 3 and self.shape[0] == 3 else 0
        self.parts = parts
        if parts:
            self.copies = [
                pltpu.make_async_copy(source.at[i], target.at[i], sems.at[i]) for i in range(parts)
            ]
        else:
            self.copies = [pltpu.make_async_copy(source, target, sems.at[0])]
        self.waiting = [True] * len(self.copies)
        for copy in self.copies:
            copy.start()

    def wait(self, wanted):
        for i in wanted:
            if self.waiting[i]:
                self.copies[i].wait()
                self.waiting[i] = False

    def __getitem__(self, index):
        one = self.parts and isinstance(index, int)
        self.wait([index] if one else range(len(self.copies)))
        return self.target[index]


class Early:
    def __init__(self, source, target, sem):
        self.source = source
        self.shape = source.shape
        self.dtype = source.dtype
        self.copy = pltpu.make_async_copy(source, target, sem)
        self.started = False

    def start(self):
        if not self.started:
            self.copy.start()
            self.started = True

    def __setitem__(self, index, value):
        self.source[index] = value
        if index is Ellipsis:
            self.start()


def call(body, outs, *operands, scalars=0, scratch=(), flops=0, manual=False):
    smem, whole = [pl.BlockSpec(memory_space=space) for space in (pltpu.SMEM, pltpu.VMEM)]
    apart = pl.BlockSpec(memory_space=pl.ANY) if manual else whole
    count = len(operands)
    late = range(scalars, count) if manual else ()
    early = range(len(outs)) if manual else ()
    specs = [smem if i < scalars else apart for i in range(count)]
    shapes = [jax.ShapeDtypeStruct(shape, dtype) for shape, dtype in outs]
    out_specs = [apart] * len(outs)
    moved = sum(x.size * x.dtype.itemsize for x in [*operands, *shapes])
    held = [pltpu.VMEM(operands[i].shape, operands[i].dtype) for i in late]
    held += [pltpu.VMEM(shapes[i].shape, shapes[i].dtype) for i in early]
    sems = [pltpu.SemaphoreType.DMA((3,))] * len(late) + [pltpu.SemaphoreType.DMA] * len(early)
    own = list(scratch)

    def wrapped(*refs):
        refs = list(refs)
        extra = refs[count + len(outs) :]
        buffers, marks = extra[len(own) : len(own) + len(held)], extra[len(own) + len(held) :]
        for n, i in enumerate(late):
            refs[i] = Late(refs[i], buffers[n], marks[n])
        results = []
        for n, i in enumerate(early):
            at = len(late) + n
            refs[count + i] = Early(buffers[at], refs[count + i], marks[at])
            results.append(refs[count + i])
        body(*refs[: count + len(outs)], *extra[: len(own)])
        for result in results:
            result.start()
        for result in results:
            result.copy.wait()

    single = len(shapes) == 1
    return pl.pallas_call(
        wrapped,
        out_shape=shapes[0] if single else shapes,
        in_specs=specs,
        out_specs=out_specs[0] if single else out_specs,
        scratch_shapes=own + held + sems,
        cost_estimate=pl.CostEstimate(flops=flops, bytes_accessed=moved, transcendentals=0),
        compiler_params=pltpu.CompilerParams(vmem_limit_bytes=(60 if manual else 40) * 1024 * 1024),
    )(*operands)


def swap_pair(array):
    return lax.ppermute(array, "tensor", PAIR)


def swap_both(array, dp_mask, seq_mask):
    if not seq_mask:
        return swap_dp(array, dp_mask)
    if not dp_mask:
        return lax.ppermute(array, "seq", [(i, i ^ seq_mask) for i in range(SEQ)])
    mask = dp_mask * SEQ + seq_mask
    return lax.ppermute(array, ("dp", "seq"), [(i, i ^ mask) for i in range(DP * SEQ)])


def swap_near(array, index):
    return swap_both(array, index % 2, Z_RING * (index // 2))


def swap_dp(array, mask):
    return lax.ppermute(array, "dp", [(i, i ^ mask) for i in range(DP)])


def all_to_all(array):
    rows, width = array.shape
    cut = array.reshape(SEQ, rows // SEQ, width)
    moved = lax.all_to_all(cut, "seq", split_axis=0, concat_axis=0, tiled=True)
    return moved.reshape(rows, width)


def group_all_to_all(array, groups):
    return lax.all_to_all(
        array, "seq", split_axis=0, concat_axis=0, tiled=True, axis_index_groups=groups
    )


def per_device(
    latents, modulation, cotangent, proj_spatial, out_spatial, proj_temporal, out_temporal
):
    tokens, width = latents.shape[-2:]
    local = out_spatial.shape[1]
    heads = local // HEAD_DIM
    x = latents.reshape(tokens, width)
    cot = cotangent.reshape(tokens, width)
    mod = modulation.transpose(1, 0, 2)
    proj_s = proj_spatial.transpose(1, 2, 0)
    proj_t = proj_temporal.transpose(1, 2, 0)
    out_s = out_spatial.T
    out_t = out_temporal.T
    dp, seq = lax.axis_index("dp"), lax.axis_index("seq")
    x_low, x_high = seq // Z_RING % 2, seq // Z_RING // 2
    near_place = (2 * x_low + dp % 2).astype(jnp.int32).reshape(1)
    far_place = (2 * (dp // 2) + x_high).astype(jnp.int32).reshape(1)
    wide = ((tokens, width), BF)
    narrow = ((tokens, local), BF)
    full = ((tokens, width), F32)
    block = ((tokens, width // DP), BF)
    blocks_held = pltpu.VMEM((DP, tokens, width // DP), BF)
    slots = wire_slots(4 * local)
    wire = ((SEQ * slots, LANES), BF)
    wire_held = pltpu.VMEM((SEQ * slots, LANES), F32)
    product = 2 * tokens * width * local
    attention = 4 * heads * tokens * tokens * local

    packed_s, weights_s, heads_s, mixed_s = call(
        spatial_forward,
        [((3, tokens, local), BF), ((heads * tokens, tokens), F32), narrow, wide],
        x, mod, proj_s, out_s, manual=True, flops=4 * product + attention,
    )
    mixed_other = swap_pair(mixed_s)
    grad_heads_t, *blocks_t = call(
        upstream_start, [narrow] + [block] * DP,
        near_place, cot, mod, out_t, x, proj_t, scalars=1, scratch=[blocks_held], flops=product,
    )
    heads_x = swap_near(heads_s, 2)
    heads_core = swap_near(heads_s, 1)
    mixed_other, heads_x, heads_core = lax.optimization_barrier((mixed_other, heads_x, heads_core))
    wire_out, middle = call(
        middle_step, [wire, full],
        x, mixed_s, mixed_other, mod, grad_heads_t, proj_t, scratch=[wire_held],
        flops=4 * product,
    )
    heads_s = [heads_s, heads_core, heads_x, swap_near(heads_x, 1)]
    blocks_t = [blocks_t[0]] + [swap_near(blocks_t[i], i) for i in range(1, DP)]
    arrived = all_to_all(wire_out)
    wire_back = call(
        temporal_step, [wire], arrived, scratch=[wire_held], flops=6 * attention
    )
    returned = all_to_all(wire_back)
    returned, heads_s, blocks_t = lax.optimization_barrier((returned, heads_s, blocks_t))
    partial_t, heads_t = call(
        temporal_return, [wide, narrow], returned, proj_t, scratch=[wire_held], flops=4 * product
    )
    partial_other = swap_pair(partial_t)
    heads_near = [swap_near(heads_t, i) for i in range(1, DP)]
    *blocks_s, scaled_s, grad_middle = call(
        middle_back, [block] * DP + [wide, full],
        near_place, cot, middle, mod, partial_t, partial_other, scalars=1, scratch=[blocks_held],
    )
    blocks_s = [blocks_s[0]] + [swap_near(blocks_s[i], i) for i in range(1, DP)]
    partial_s = call(
        spatial_back, [wide],
        scaled_s, packed_s, weights_s, out_s, proj_s, flops=4 * product + 5 * attention,
    )
    partial_s_other = swap_pair(partial_s)
    piece = ((2 * width // DP // X_RING, local), BF)
    sums = call(
        weight_products, [piece] * DP,
        far_place, *blocks_s, *heads_s, *blocks_t, heads_t, *heads_near, scalars=1, manual=True,
        flops=4 * product, scratch=[pltpu.VMEM((DP, *piece[0]), BF)],
    )
    sums = [sums[0]] + [
        swap_both(sums[i], 2 * (i // 2), 2 * Z_RING * (i % 2)) for i in range(1, DP)
    ]
    sums_half = call(weight_halfway, [((Z_RING, ROWS, local), BF)], *sums)
    sums_in = group_all_to_all(sums_half, Z_GROUPS)
    heads_late, partial_s_other = lax.optimization_barrier((heads_t, partial_s_other))
    mixed_t = call(mix_temporal, [wide], heads_late, out_t, flops=product)
    mixed_t_other = swap_pair(mixed_t)
    block_output = call(output_step, [wide], middle, mod, mixed_t, mixed_t_other)
    latent_grad = call(latent_step, [full], x, mod, grad_middle, partial_s, partial_s_other)
    part = ((width // DP // SEQ, local), F32)
    grad_out_s, grad_out_t = call(weight_sums, [part, part], sums_in)
    return (
        block_output.reshape(latents.shape),
        latent_grad.reshape(latents.shape),
        grad_out_s,
        grad_out_t,
    )


def solution(mesh):
    placed = (
        P("dp", "seq", None, None),
        P("dp", None, None),
        P("dp", "seq", None, None),
        P(None, None, "tensor"),
        P(None, "tensor"),
        P(None, None, "tensor"),
        P(None, "tensor"),
    )
    return jax.shard_map(
        per_device,
        mesh=mesh,
        in_specs=placed,
        out_specs=(
            P("dp", "seq", None, None),
            P("dp", "seq", None, None),
            P(("dp", "seq"), "tensor"),
            P(("dp", "seq"), "tensor"),
        ),
        check_vma=False,
    )
```

time: 141 us -> 137 us (0.972)
  starting transfers between devices: 34.5 us -> 28.8 us
  waiting for transfers between devices: 36.8 us -> 33.6 us
  blocking collectives: 26 us -> 29.1 us
    ppermute x0 -> x9, waiting for transfers between devices: none -> 13.5 us  [the longest x5 9.14 us: swap_both(): return lax.ppermute(array, 'seq', [(i, i ^ seq_mask) for i in range(SEQ)])]
    ppermute x9 -> x6, waiting for transfers between devices: 15.5 us -> 4.02 us  [swap_dp(): return lax.ppermute(array, 'dp', [(i, i ^ mask) for i in range(DP)])]
    ppermute x0 -> x9, starting transfers between devices: none -> 10.4 us  [the longest x5 5.65 us: swap_both(): return lax.ppermute(array, 'seq', [(i, i ^ seq_mask) for i in range(SEQ)])]
    ppermute x9 -> x6, starting transfers between devices: 11 us -> 3.47 us  [swap_dp(): return lax.ppermute(array, 'dp', [(i, i ^ mask) for i in range(DP)])]
    all_to_all x1, starting transfers between devices: 11.2 us -> 4.94 us  [all_to_all(): moved = lax.all_to_all(cut, 'seq', split_axis=0, concat_axis=0, tiled=True)]
    ppermute x4, waiting for transfers between devices: 14.8 us -> 9.26 us  [swap_pair(): return lax.ppermute(array, 'tensor', PAIR)]
    all_to_all x1, blocking collectives: 26 us -> 29.1 us  [all_to_all(): moved = lax.all_to_all(cut, 'seq', split_axis=0, concat_axis=0, tiled=True)]
    all_to_all x2 -> x1, starting transfers between devices: 7.24 us -> 4.85 us  [group_all_to_all(): lax.all_to_all(array, 'seq', split_axis=0, concat_axis=0, tiled=True, axi...]
  transfers between devices with their start and end apart: 16 -> 21, of which waited for: 10 -> 10; matrix products, arithmetic and copies ran while one was open for 0% -> 0% of each run, Pallas kernels for 7% -> 11%
where the time goes in v3:
time: 137 us; the launch traced here: 136 us
  waiting for transfers between devices  33.6 us (25%)
  blocking collectives  29.1 us (21%)
  starting transfers between devices  28.8 us (21%)
  Pallas kernels  27.9 us (20%)
  local copies, waits for them, and re-layouts  15.8 us (12%)
    all_to_all x1, blocking collectives, all_to_all(): moved = lax.all_to_all(cut, 'seq', split_axis=0, concat_axis=0, tiled=True)  29.1 us
    pallas_call x13, Pallas kernels, call(): pl.pallas_call(wrapped, out_shape=shapes[0] if single else shapes, in_spe...  27.9 us
    unnamed x56, local copies, waits for them, and re-layouts  15.8 us
    ppermute x4, waiting for transfers between devices, swap_pair(): return lax.ppermute(array, 'tensor', PAIR)  9.26 us
    ppermute x5, waiting for transfers between devices, swap_both(): return lax.ppermute(array, 'seq', [(i, i ^ seq_mask) for i in range(SEQ)])  9.14 us
    all_to_all x1, waiting for transfers between devices, all_to_all(): moved = lax.all_to_all(cut, 'seq', split_axis=0, concat_axis=0, tiled=True)  6.72 us
    ppermute x5, starting transfers between devices, swap_both(): return lax.ppermute(array, 'seq', [(i, i ^ seq_mask) for i in range(SEQ)])  5.65 us
    ppermute x4, starting transfers between devices, swap_pair(): return lax.ppermute(array, 'tensor', PAIR)  5.14 us
  transfers between devices with their start and end apart: 21, of which 10 were waited for; matrix products, arithmetic and copies ran while one was open for 0% of the time, Pallas kernels for 11%

profile of v3, /device:TPU:32, one launch (start us, length us, event | category | flops | bytes accessed | tf_op | source)
XLA Modules:
  0.0 136.0 jit_solution(2976430387528280557)
XLA Ops:
  0.7 7.0 %shard_map.102 = (bf16[3,128,576]{2,1,0:T(8,128)(2,1)}, f32[1024,128]{1,0:T(8,128)}, bf16[128,576]{1,0:T(8,128)(2,1)}, bf16[128,1152]{1,0:T(8,128)(2,1)}) custom-call(bf16[128,1152]{1,0:T(8,128)(2,1)} %bitcast.20, f32[6,1,1152]{2,1,0:T(1,128)} %bitcast.31, bf16[3,576,1152]{2,1,0:T(8,128)(2,1)} %bitcast.24, bf16[576,1152]{1,0:T(8,128)(2,1)} %bitcast.27), custom_call_target="tpu_custom_call" | custom-call | flops 981467136 | bytes 7040000 | tf_op jit(solution)/shard_map/pallas_call | solution.py:381
  7.7 1.7 %collective-permute-start = (bf16[128,1152]{1,0:T(8,128)(2,1)}, bf16[128,1152]{1,0:T(8,128)(2,1)S(1)}, u32[]{:S(2)}, u32[]{:S(2)}) collective-permute-start(bf16[128,1152]{1,0:T(8,128)(2,1)} %get-tuple-element.43.refs_1_), channel_id=1, source_target_pairs={{0,1},{1,0},{2,3},{3,2},{4,5},{5,4},{6,7},{7,6},{8,9},{9,8},{10,11... | collective-permute-start | bytes 884744 | tf_op jit(solution)/shard_map/ppermute | solution.py:393
  10.9 2.1 %copy-done = bf16[1152,3,576]{0,2,1:T(8,128)(2,1)S(1)} copy-done((bf16[1152,3,576]{0,2,1:T(8,128)(2,1)S(1)}, bf16[1152,3,576]{0,2,1:T(8,128)(2,1)}, u32[]{:S(2)}) %copy-start) | copy-done | bytes 3981336
  16.7 1.7 %shard_map.104 = (bf16[2304,128]{1,0:T(8,128)(2,1)S(1)}, f32[128,1152]{1,0:T(8,128)S(1)}) custom-call(bf16[128,1152]{1,0:T(8,128)(2,1)S(1)} %bitcast.22, bf16[128,1152]{1,0:T(8,128)(2,1)S(1)} %copy-done.10, bf16[128,1152]{1,0:T(8,128)(2,1)S(1)} %collective-permute-done.refs_2_, f32[6,1,1152]{2,1,0:T(1,128)S(1)} %bitcast.33, ...), custom_call_target="tpu_custom_call" | custom-call | flops 679477248 | bytes 6220800 | tf_op jit(solution)/shard_map/pallas_call | solution.py:381
  18.5 29.1 %all_to_all.15 = bf16[32,72,128]{2,1,0:T(8,128)(2,1)S(1)} all-to-all(bf16[32,72,128]{2,1,0:T(8,128)(2,1)S(1)} %bitcast.38), channel_id=1, replica_groups=mesh['dp'=4,'seq'=32,'tensor'=2] {'seq'}, dimensions={0} | all-to-all | bytes 1179648 | tf_op jit(solution)/shard_map/all_to_all | solution.py:416
  47.6 2.5 %shard_map.105 = bf16[2304,128]{1,0:T(8,128)(2,1)S(1)} custom-call(bf16[2304,128]{1,0:T(8,128)(2,1)S(1)} %bitcast.39), custom_call_target="tpu_custom_call" | custom-call | flops 1811939328 | bytes 1179648 | tf_op jit(solution)/shard_map/pallas_call | solution.py:381
  50.9 4.9 %all-to-all-start.1 = ((bf16[32,72,128]{2,1,0:T(8,128)(2,1)}), bf16[32,72,128]{2,1,0:T(8,128)(2,1)S(1)}, u32[]{:S(2)}, u32[]{:S(2)}) async-start(bf16[32,72,128]{2,1,0:T(8,128)(2,1)} %bitcast.37), calls=%async_computation.1 | async-start | bytes 1179648 | tf_op jit(solution)/shard_map/all_to_all | solution.py:416
  57.9 6.3 %collective-permute-done.5.refs_11_ = bf16[128,288]{1,0:T(8,128)(2,1)S(1)} collective-permute-done((bf16[128,288]{1,0:T(8,128)(2,1)S(1)}, bf16[128,288]{1,0:T(8,128)(2,1)S(1)}, u32[]{:S(2)}, u32[]{:S(2)}) %collective-permute-start.5) | collective-permute-done | bytes 73760 | tf_op jit(solution)/shard_map/ppermute | solution.py:400
  64.3 2.2 %collective-permute-done.6.refs_12_ = bf16[128,288]{1,0:T(8,128)(2,1)S(1)} collective-permute-done((bf16[128,288]{1,0:T(8,128)(2,1)S(1)}, bf16[128,288]{1,0:T(8,128)(2,1)S(1)}, u32[]{:S(2)}, u32[]{:S(2)}) %collective-permute-start.6) | collective-permute-done | bytes 73760 | tf_op jit(solution)/shard_map/ppermute | solution.py:402
  67.1 6.7 %all-to-all-done.1 = bf16[32,72,128]{2,1,0:T(8,128)(2,1)S(1)} async-done(((bf16[32,72,128]{2,1,0:T(8,128)(2,1)}), bf16[32,72,128]{2,1,0:T(8,128)(2,1)S(1)}, u32[]{:S(2)}, u32[]{:S(2)}) %all-to-all-start.1) | async-done | bytes 589856 | tf_op jit(solution)/shard_map/all_to_all | solution.py:416
  73.9 2.1 %copy-done.2 = bf16[1152,3,576]{0,2,1:T(8,128)(2,1)S(1)} copy-done((bf16[1152,3,576]{0,2,1:T(8,128)(2,1)S(1)}, bf16[1152,3,576]{0,2,1:T(8,128)(2,1)}, u32[]{:S(2)}) %copy-start.2) | copy-done | bytes 3981336
  81.1 3.3 %collective-permute-done.7.refs_5_ = bf16[128,1152]{1,0:T(8,128)(2,1)S(1)} collective-permute-done((bf16[128,1152]{1,0:T(8,128)(2,1)S(1)}, bf16[128,1152]{1,0:T(8,128)(2,1)S(1)}, u32[]{:S(2)}, u32[]{:S(2)}) %collective-permute-start.7) | collective-permute-done | bytes 294944 | tf_op jit(solution)/shard_map/ppermute | solution.py:393
  89.2 2.1 %copy-done.5 = bf16[1152,3,576]{0,2,1:T(8,128)(2,1)S(1)} copy-done((bf16[1152,3,576]{0,2,1:T(8,128)(2,1)S(1)}, bf16[1152,3,576]{0,2,1:T(8,128)(2,1)}, u32[]{:S(2)}) %copy-start.5) | copy-done | bytes 3981336
  94.7 2.8 %shard_map.108.refs_3_ = bf16[128,1152]{1,0:T(8,128)(2,1)S(1)} custom-call(bf16[128,1152]{1,0:T(8,128)(2,1)S(1)} %get-tuple-element.58.refs_0_, bf16[3,128,576]{2,1,0:T(8,128)(2,1)S(1)} %copy-done.15, f32[1024,128]{1,0:T(8,128)S(1)} %copy-done.14, bf16[576,1152]{1,0:T(8,128)(2,1)S(1)} %bitcast.28, bf16[3,576,1152]{2,1,0:T(8,128)(2,1)S(1)} %bitcast.25), custom_call_target="tpu_custom_call" | custom-call | flops 2189426688 | bytes 6864896 | tf_op jit(solution)/shard_map/pallas_call | solution.py:381
  97.6 1.7 %collective-permute-start.8 = (bf16[128,1152]{1,0:T(8,128)(2,1)S(1)}, bf16[128,1152]{1,0:T(8,128)(2,1)}, u32[]{:S(2)}, u32[]{:S(2)}) collective-permute-start(bf16[128,1152]{1,0:T(8,128)(2,1)S(1)} %shard_map.108.refs_3_), channel_id=1, source_target_pairs={{0,1},{1,0},{2,3},{3,2},{4,5},{5,4},{6,7},{7,6},{8,9},{9,8},{10,11... | collective-permute-start | bytes 884744 | tf_op jit(solution)/shard_map/ppermute | solution.py:393
  100.1 4.8 %shard_map.112 = (bf16[144,576]{1,0:T(8,128)(2,1)}, bf16[144,576]{1,0:T(8,128)(2,1)}, bf16[144,576]{1,0:T(8,128)(2,1)}, bf16[144,576]{1,0:T(8,128)(2,1)}) custom-call(s32[1]{0:T(128)} %bitcast.14.refs_0_, bf16[128,288]{1,0:T(8,128)(2,1)} %copy-done.17, bf16[128,288]{1,0:T(8,128)(2,1)} %copy-done.25, bf16[128,288]{1,0:T(8,128)(2,1)} %copy-done.26, ...), custom_call_target="tpu_custom_call" | custom-call | flops 679477248 | bytes 2433028 | tf_op jit(solution)/shard_map/pallas_call | solution.py:381
  106.4 2.9 %collective-permute-start.17 = (bf16[144,576]{1,0:T(8,128)(2,1)}, bf16[144,576]{1,0:T(8,128)(2,1)S(1)}, u32[]{:S(2)}, u32[]{:S(2)}) collective-permute-start(bf16[144,576]{1,0:T(8,128)(2,1)} %get-tuple-element.78), channel_id=1, source_target_pairs={{0,128},{64,192},{128,0},{192,64},{1,129},{65,193},{129,1},{193,65... | collective-permute-start | bytes 497672 | tf_op jit(solution)/shard_map/ppermute | solution.py:410
  109.2 2.2 %collective-permute-start.18 = (bf16[144,576]{1,0:T(8,128)(2,1)}, bf16[144,576]{1,0:T(8,128)(2,1)S(1)}, u32[]{:S(2)}, u32[]{:S(2)}) collective-permute-start(bf16[144,576]{1,0:T(8,128)(2,1)} %get-tuple-element.79), channel_id=1, source_target_pairs={{0,160},{2,162},{4,164},{6,166},{8,168},{10,170},{12,172},{14,174}... | collective-permute-start | bytes 497672 | tf_op jit(solution)/shard_map/ppermute | solution.py:402
  111.5 1.8 %collective-permute-done.16.refs_1_ = bf16[144,576]{1,0:T(8,128)(2,1)S(1)} collective-permute-done((bf16[144,576]{1,0:T(8,128)(2,1)}, bf16[144,576]{1,0:T(8,128)(2,1)S(1)}, u32[]{:S(2)}, u32[]{:S(2)}) %collective-permute-start.16) | collective-permute-done | bytes 165920 | tf_op jit(solution)/shard_map/ppermute | solution.py:400
  113.3 4.0 %collective-permute-done.17.refs_2_ = bf16[144,576]{1,0:T(8,128)(2,1)S(1)} collective-permute-done((bf16[144,576]{1,0:T(8,128)(2,1)}, bf16[144,576]{1,0:T(8,128)(2,1)S(1)}, u32[]{:S(2)}, u32[]{:S(2)}) %collective-permute-start.17) | collective-permute-done | bytes 165920 | tf_op jit(solution)/shard_map/ppermute | solution.py:410
  117.3 2.2 %collective-permute-done.18.refs_3_ = bf16[144,576]{1,0:T(8,128)(2,1)S(1)} collective-permute-done((bf16[144,576]{1,0:T(8,128)(2,1)}, bf16[144,576]{1,0:T(8,128)(2,1)S(1)}, u32[]{:S(2)}, u32[]{:S(2)}) %collective-permute-start.18) | collective-permute-done | bytes 165920 | tf_op jit(solution)/shard_map/ppermute | solution.py:402
  121.4 4.8 %all-to-all-start.2 = ((bf16[8,24,576]{2,1,0:T(8,128)(2,1)}), bf16[8,24,576]{2,1,0:T(8,128)(2,1)S(1)}, u32[]{:S(2)}, u32[]{:S(2)}) async-start(bf16[8,24,576]{2,1,0:T(8,128)(2,1)} %shard_map.113), calls=%async_computation.2 | async-start | bytes 491520 | tf_op jit(solution)/shard_map/all_to_all | solution.py:421
  127.8 2.3 %shard_map.111 = f32[128,1152]{1,0:T(8,128)} custom-call(bf16[128,1152]{1,0:T(8,128)(2,1)S(1)} %bitcast.23, f32[6,1,1152]{2,1,0:T(1,128)S(1)} %bitcast.35, f32[128,1152]{1,0:T(8,128)S(1)} %get-tuple-element.62.refs_2_, bf16[128,1152]{1,0:T(8,128)(2,1)S(1)} %shard_map.108.refs_3_, bf16[128,1152]{1,0:T(8,128)(2,1)} %collective-permute-done.8.refs_4_), custom_call_target="tpu_custom_call" | custom-call | bytes 2092032 | tf_op jit(solution)/shard_map/pallas_call | solution.py:381
  130.1 4.5 %collective-permute-done.9.refs_3_ = bf16[128,1152]{1,0:T(8,128)(2,1)S(1)} collective-permute-done((bf16[128,1152]{1,0:T(8,128)(2,1)S(1)}, bf16[128,1152]{1,0:T(8,128)(2,1)S(1)}, u32[]{:S(2)}, u32[]{:S(2)}) %collective-permute-start.9) | collective-permute-done | bytes 294944 | tf_op jit(solution)/shard_map/ppermute | solution.py:393
  (88 shorter events, 29.3 us)
Async XLA Ops:
  0.6 10.2 %copy-start.4 = (bf16[1,1,128,1152]{3,2,1,0:T(8,128)(2,1)S(1)}, bf16[1,1,128,1152]{3,2,1,0:T(8,128)(2,1)}, u32[]{:S(2)}) copy-start(bf16[1,1,128,1152]{3,2,1,0:T(8,128)(2,1)} %param.7) | copy-start | bytes 884740
  7.7 9.1 %collective-permute-start = (bf16[128,1152]{1,0:T(8,128)(2,1)}, bf16[128,1152]{1,0:T(8,128)(2,1)S(1)}, u32[]{:S(2)}, u32[]{:S(2)}) collective-permute-start(bf16[128,1152]{1,0:T(8,128)(2,1)} %get-tuple-element.43.refs_1_), channel_id=1, source_target_pairs={{0,1},{1,0},{2,3},{3,2},{4,5},{5,4},{6,7},{7,6},{8,9},{9,8},{10,11... | collective-permute-start | bytes 884744 | tf_op jit(solution)/shard_map/ppermute | solution.py:393
  9.3 5.9 %collective-permute-start.1 = (bf16[128,576]{1,0:T(8,128)(2,1)}, bf16[128,576]{1,0:T(8,128)(2,1)S(1)}, u32[]{:S(2)}, u32[]{:S(2)}) collective-permute-start(bf16[128,576]{1,0:T(8,128)(2,1)} %get-tuple-element.68.refs_5_), channel_id=1, source_target_pairs={{0,16},{2,18},{4,20},{6,22},{8,24},{10,26},{12,28},{14,30},{16,0},... | collective-permute-start | bytes 442376 | tf_op jit(solution)/shard_map/ppermute | solution.py:400
  10.8 4.4 %collective-permute-start.2 = (bf16[128,576]{1,0:T(8,128)(2,1)}, bf16[128,576]{1,0:T(8,128)(2,1)S(1)}, u32[]{:S(2)}, u32[]{:S(2)}) collective-permute-start(bf16[128,576]{1,0:T(8,128)(2,1)} %get-tuple-element.68.refs_5_), channel_id=1, source_target_pairs={{0,64},{64,0},{128,192},{192,128},{1,65},{65,1},{129,193},{193,129... | collective-permute-start | bytes 442376 | tf_op jit(solution)/shard_map/ppermute | solution.py:410
  15.2 35.7 %copy-start.18 = (bf16[128,576]{1,0:T(8,128)(2,1)}, bf16[128,576]{1,0:T(8,128)(2,1)S(1)}, u32[]{:S(2)}) copy-start(bf16[128,576]{1,0:T(8,128)(2,1)S(1)} %collective-permute-done.1.refs_7_) | copy-start | bytes 442372
  50.9 23.0 %all-to-all-start.1 = ((bf16[32,72,128]{2,1,0:T(8,128)(2,1)}), bf16[32,72,128]{2,1,0:T(8,128)(2,1)S(1)}, u32[]{:S(2)}, u32[]{:S(2)}) async-start(bf16[32,72,128]{2,1,0:T(8,128)(2,1)} %bitcast.37), calls=%async_computation.1 | async-start | bytes 1179648 | tf_op jit(solution)/shard_map/all_to_all | solution.py:416
  55.8 11.3 %collective-permute-start.3 = (bf16[128,576]{1,0:T(8,128)(2,1)}, bf16[128,576]{1,0:T(8,128)(2,1)}, u32[]{:S(2)}, u32[]{:S(2)}) collective-permute-start(bf16[128,576]{1,0:T(8,128)(2,1)} %copy-done.18), channel_id=1, source_target_pairs={{0,64},{64,0},{128,192},{192,128},{1,65},{65,1},{129,193},{193,129... | collective-permute-start | bytes 442376 | tf_op jit(solution)/shard_map/ppermute | solution.py:410
  55.9 2.0 %collective-permute-start.4 = (bf16[128,288]{1,0:T(8,128)(2,1)S(1)}, bf16[128,288]{1,0:T(8,128)(2,1)S(1)}, u32[]{:S(2)}, u32[]{:S(2)}) collective-permute-start(bf16[128,288]{1,0:T(8,128)(2,1)S(1)} %get-tuple-element.52), channel_id=1, source_target_pairs={{0,64},{64,0},{128,192},{192,128},{1,65},{65,1},{129,193},{193,129... | collective-permute-start | bytes 221192 | tf_op jit(solution)/shard_map/ppermute | solution.py:410
  56.4 7.8 %collective-permute-start.5 = (bf16[128,288]{1,0:T(8,128)(2,1)S(1)}, bf16[128,288]{1,0:T(8,128)(2,1)S(1)}, u32[]{:S(2)}, u32[]{:S(2)}) collective-permute-start(bf16[128,288]{1,0:T(8,128)(2,1)S(1)} %get-tuple-element.53), channel_id=1, source_target_pairs={{0,16},{2,18},{4,20},{6,22},{8,24},{10,26},{12,28},{14,30},{16,0},... | collective-permute-start | bytes 221192 | tf_op jit(solution)/shard_map/ppermute | solution.py:400
  57.9 8.6 %collective-permute-start.6 = (bf16[128,288]{1,0:T(8,128)(2,1)S(1)}, bf16[128,288]{1,0:T(8,128)(2,1)S(1)}, u32[]{:S(2)}, u32[]{:S(2)}) collective-permute-start(bf16[128,288]{1,0:T(8,128)(2,1)S(1)} %get-tuple-element.54), channel_id=1, source_target_pairs={{0,80},{2,82},{4,84},{6,86},{8,88},{10,90},{12,92},{14,94},{16,64}... | collective-permute-start | bytes 221192 | tf_op jit(solution)/shard_map/ppermute | solution.py:402
  57.9 39.7 %copy-start.22 = (bf16[128,288]{1,0:T(8,128)(2,1)}, bf16[128,288]{1,0:T(8,128)(2,1)S(1)}, u32[]{:S(2)}) copy-start(bf16[128,288]{1,0:T(8,128)(2,1)S(1)} %collective-permute-done.4.refs_10_) | copy-start | bytes 221188
  77.6 6.7 %collective-permute-start.7 = (bf16[128,1152]{1,0:T(8,128)(2,1)S(1)}, bf16[128,1152]{1,0:T(8,128)(2,1)S(1)}, u32[]{:S(2)}, u32[]{:S(2)}) collective-permute-start(bf16[128,1152]{1,0:T(8,128)(2,1)S(1)} %get-tuple-element.57.refs_4_), channel_id=1, source_target_pairs={{0,1},{1,0},{2,3},{3,2},{4,5},{5,4},{6,7},{7,6},{8,9},{9,8},{10,11... | collective-permute-start | bytes 884744 | tf_op jit(solution)/shard_map/ppermute | solution.py:393
  79.2 8.8 %collective-permute-start.13 = (bf16[128,576]{1,0:T(8,128)(2,1)}, bf16[128,576]{1,0:T(8,128)(2,1)}, u32[]{:S(2)}, u32[]{:S(2)}) collective-permute-start(bf16[128,576]{1,0:T(8,128)(2,1)} %get-tuple-element.61.refs_0_.refs_13_), channel_id=1, source_target_pairs={{0,64},{64,0},{128,192},{192,128},{1,65},{65,1},{129,193},{193,129... | collective-permute-start | bytes 442376 | tf_op jit(solution)/shard_map/ppermute | solution.py:410
  79.2 18.4 %collective-permute-start.14 = (bf16[128,576]{1,0:T(8,128)(2,1)}, bf16[128,576]{1,0:T(8,128)(2,1)S(1)}, u32[]{:S(2)}, u32[]{:S(2)}) collective-permute-start(bf16[128,576]{1,0:T(8,128)(2,1)} %get-tuple-element.61.refs_0_.refs_13_), channel_id=1, source_target_pairs={{0,16},{2,18},{4,20},{6,22},{8,24},{10,26},{12,28},{14,30},{16,0},... | collective-permute-start | bytes 442376 | tf_op jit(solution)/shard_map/ppermute | solution.py:400
  79.8 19.5 %collective-permute-start.15 = (bf16[128,576]{1,0:T(8,128)(2,1)}, bf16[128,576]{1,0:T(8,128)(2,1)S(1)}, u32[]{:S(2)}, u32[]{:S(2)}) collective-permute-start(bf16[128,576]{1,0:T(8,128)(2,1)} %get-tuple-element.61.refs_0_.refs_13_), channel_id=1, source_target_pairs={{0,80},{2,82},{4,84},{6,86},{8,88},{10,90},{12,92},{14,94},{16,64}... | collective-permute-start | bytes 442376 | tf_op jit(solution)/shard_map/ppermute | solution.py:402
  87.3 11.9 %collective-permute-start.10 = (bf16[128,288]{1,0:T(8,128)(2,1)S(1)}, bf16[128,288]{1,0:T(8,128)(2,1)S(1)}, u32[]{:S(2)}, u32[]{:S(2)}) collective-permute-start(bf16[128,288]{1,0:T(8,128)(2,1)S(1)} %get-tuple-element.65), channel_id=1, source_target_pairs={{0,64},{64,0},{128,192},{192,128},{1,65},{65,1},{129,193},{193,129... | collective-permute-start | bytes 221192 | tf_op jit(solution)/shard_map/ppermute | solution.py:410
  87.4 11.9 %collective-permute-start.11 = (bf16[128,288]{1,0:T(8,128)(2,1)S(1)}, bf16[128,288]{1,0:T(8,128)(2,1)S(1)}, u32[]{:S(2)}, u32[]{:S(2)}) collective-permute-start(bf16[128,288]{1,0:T(8,128)(2,1)S(1)} %get-tuple-element.66), channel_id=1, source_target_pairs={{0,16},{2,18},{4,20},{6,22},{8,24},{10,26},{12,28},{14,30},{16,0},... | collective-permute-start | bytes 221192 | tf_op jit(solution)/shard_map/ppermute | solution.py:400
  88.0 11.4 %collective-permute-start.12 = (bf16[128,288]{1,0:T(8,128)(2,1)S(1)}, bf16[128,288]{1,0:T(8,128)(2,1)S(1)}, u32[]{:S(2)}, u32[]{:S(2)}) collective-permute-start(bf16[128,288]{1,0:T(8,128)(2,1)S(1)} %get-tuple-element.67), channel_id=1, source_target_pairs={{0,80},{2,82},{4,84},{6,86},{8,88},{10,90},{12,92},{14,94},{16,64}... | collective-permute-start | bytes 221192 | tf_op jit(solution)/shard_map/ppermute | solution.py:402
  97.6 28.6 %collective-permute-start.8 = (bf16[128,1152]{1,0:T(8,128)(2,1)S(1)}, bf16[128,1152]{1,0:T(8,128)(2,1)}, u32[]{:S(2)}, u32[]{:S(2)}) collective-permute-start(bf16[128,1152]{1,0:T(8,128)(2,1)S(1)} %shard_map.108.refs_3_), channel_id=1, source_target_pairs={{0,1},{1,0},{2,3},{3,2},{4,5},{5,4},{6,7},{7,6},{8,9},{9,8},{10,11... | collective-permute-start | bytes 884744 | tf_op jit(solution)/shard_map/ppermute | solution.py:393
  104.9 8.4 %collective-permute-start.16 = (bf16[144,576]{1,0:T(8,128)(2,1)}, bf16[144,576]{1,0:T(8,128)(2,1)S(1)}, u32[]{:S(2)}, u32[]{:S(2)}) collective-permute-start(bf16[144,576]{1,0:T(8,128)(2,1)} %get-tuple-element.77), channel_id=1, source_target_pairs={{0,32},{2,34},{4,36},{6,38},{8,40},{10,42},{12,44},{14,46},{16,48}... | collective-permute-start | bytes 497672 | tf_op jit(solution)/shard_map/ppermute | solution.py:400
  106.4 10.9 %collective-permute-start.17 = (bf16[144,576]{1,0:T(8,128)(2,1)}, bf16[144,576]{1,0:T(8,128)(2,1)S(1)}, u32[]{:S(2)}, u32[]{:S(2)}) collective-permute-start(bf16[144,576]{1,0:T(8,128)(2,1)} %get-tuple-element.78), channel_id=1, source_target_pairs={{0,128},{64,192},{128,0},{192,64},{1,129},{65,193},{129,1},{193,65... | collective-permute-start | bytes 497672 | tf_op jit(solution)/shard_map/ppermute | solution.py:410
  109.2 10.2 %collective-permute-start.18 = (bf16[144,576]{1,0:T(8,128)(2,1)}, bf16[144,576]{1,0:T(8,128)(2,1)S(1)}, u32[]{:S(2)}, u32[]{:S(2)}) collective-permute-start(bf16[144,576]{1,0:T(8,128)(2,1)} %get-tuple-element.79), channel_id=1, source_target_pairs={{0,160},{2,162},{4,164},{6,166},{8,168},{10,170},{12,172},{14,174}... | collective-permute-start | bytes 497672 | tf_op jit(solution)/shard_map/ppermute | solution.py:402
  121.4 14.0 %all-to-all-start.2 = ((bf16[8,24,576]{2,1,0:T(8,128)(2,1)}), bf16[8,24,576]{2,1,0:T(8,128)(2,1)S(1)}, u32[]{:S(2)}, u32[]{:S(2)}) async-start(bf16[8,24,576]{2,1,0:T(8,128)(2,1)} %shard_map.113), calls=%async_computation.2 | async-start | bytes 491520 | tf_op jit(solution)/shard_map/all_to_all | solution.py:421
  127.6 7.0 %collective-permute-start.9 = (bf16[128,1152]{1,0:T(8,128)(2,1)S(1)}, bf16[128,1152]{1,0:T(8,128)(2,1)S(1)}, u32[]{:S(2)}, u32[]{:S(2)}) collective-permute-start(bf16[128,1152]{1,0:T(8,128)(2,1)S(1)} %shard_map.109.refs_2_), channel_id=1, source_target_pairs={{0,1},{1,0},{2,3},{3,2},{4,5},{5,4},{6,7},{7,6},{8,9},{9,8},{10,11... | collective-permute-start | bytes 884744 | tf_op jit(solution)/shard_map/ppermute | solution.py:393
  (25 other events, 61.4 us)

commit v4 on v3

--- a/solution.py
+++ b/solution.py
@@ -14,10 +14,8 @@
 SEQ = 32
 BF = jnp.bfloat16
 F32 = jnp.float32
-ROWS = 24
 X_RING = 4
 Z_RING = 8
-Z_GROUPS = tuple(tuple(z + Z_RING * x for z in range(Z_RING)) for x in range(X_RING))
 
 
 def mm(left, right):
@@ -79,6 +77,16 @@
     return grad_queries, grad_keys, grad_values
 
 
+FAR_GROUPS = tuple(
+    tuple(
+        ((2 * far + core) * X_RING + 2 * x_high + x_low) * Z_RING + z
+        for far in range(2)
+        for x_high in range(2)
+        for z in range(Z_RING)
+    )
+    for core in range(2)
+    for x_low in range(2)
+)
 LANES = 128
 QUARTERS = 4
 
@@ -197,7 +205,7 @@
     to_wire(parts + [grad_ref[...]], held_ref, wire_ref)
 
 
-def temporal_step(arrived_ref, wire_ref, held_ref):
+def temporal_step(arrived_ref, proj_ref, wire_ref, held_ref, back_ref):
     local = arrived_ref.shape[0] * LANES // (QUARTERS * SEQ) // 4
     parts = from_wire(arrived_ref, held_ref, (local,) * 4)
     queries, keys_in, values_in, grad_out = [part.astype(BF) for part in parts]
@@ -209,16 +217,16 @@
     weights = softmax_weights(queries, keys_in, row // frames == column // frames)
     out = mm(side_by_side(weights.astype(BF)), stack_heads(values_in)).astype(BF)
     grads = attend_back(queries, keys_in, values_in, grad_out, weights)
-    to_wire(list(grads) + [out], held_ref, wire_ref)
-
-
-def temporal_return(arrived_ref, proj_ref, partial_ref, heads_ref, held_ref):
-    local = heads_ref.shape[1]
-    parts = from_wire(arrived_ref, held_ref, (local,) * 4)
-    *grads, heads = [part.astype(BF) for part in parts]
-    heads_ref[...] = heads
     total = mm(grads[0], proj_ref[0]) + mm(grads[1], proj_ref[1])
-    partial_ref[...] = (total + mm(grads[2], proj_ref[2])).astype(BF)
+    partial = (total + mm(grads[2], proj_ref[2])).astype(BF)
+    to_wire([partial, out], back_ref, wire_ref)
+
+
+def temporal_return(arrived_ref, partial_ref, heads_ref, held_ref):
+    widths = partial_ref.shape[1], heads_ref.shape[1]
+    partial, heads = from_wire(arrived_ref, held_ref, widths)
+    partial_ref[...] = partial.astype(BF)
+    heads_ref[...] = heads.astype(BF)
 
 
 def mix_temporal(heads_ref, out_ref, mixed_ref):
@@ -238,7 +246,7 @@
     grad_ref[...] = grad
 
 
-def spatial_back(scaled_ref, packed_ref, weights_ref, out_ref, proj_ref, partial_ref):
+def spatial_back(scaled_ref, out_ref, packed_ref, weights_ref, proj_ref, partial_ref):
     grad_heads = mm_rt(scaled_ref[...], out_ref[...]).astype(BF)
     grads = attend_back(
         packed_ref[0], packed_ref[1], packed_ref[2], grad_heads, weights_ref[...]
@@ -257,45 +265,52 @@
     block_ref[...] = (middle_ref[...] + mod_ref[5] * mixed).astype(BF)
 
 
-def weight_products(place_ref, *refs):
-    out_refs, held_ref = refs[4 * DP : -1], refs[-1]
-    spatial, temporal = 0.0, 0.0
+def product_of(refs):
+    total = 0.0
     for i in range(DP):
-        temporal = temporal + mm_lt(refs[2 * DP + i][...], refs[3 * DP + i][...])
-    for i in range(DP):
-        spatial = spatial + mm_lt(refs[i][...], refs[DP + i][...])
-    cut = spatial.shape[0] // DP
-    for i in range(DP):
-        rows = slice(i * cut, (i + 1) * cut)
-        held_ref[i] = jnp.concatenate([spatial[rows], temporal[rows]], axis=0).astype(BF)
-    for i in range(DP):
-        out_refs[i][...] = held_ref[place_ref[0] ^ i]
-
-
-def add_sources(parts):
-    total = parts[0].astype(F32)
-    for part in parts[1:]:
-        total = total + part.astype(F32)
+        total = total + mm_lt(refs[i][...], refs[DP + i][...])
     return total
 
 
-def weight_halfway(*refs):
-    wire_ref = refs[-1]
-    total = add_sources([ref[...] for ref in refs[:-1]]).astype(BF)
-    rows = total.shape[0]
-    part = rows // 2 // Z_RING
-    index = lax.broadcasted_iota(jnp.int32, (1, rows), 1)
-    which, index = index // (rows // 2), index % (rows // 2)
-    held = ROWS * (index // part) + part * which + index % part
-    place = lax.broadcasted_iota(jnp.int32, (Z_RING * ROWS, rows), 0) == held
-    wire_ref[...] = mm(place.astype(F32).astype(BF), total).astype(BF).reshape(wire_ref.shape)
+def temporal_product(*refs):
+    refs[-1][...] = product_of(refs[:-1])
+
+
+def weight_products(*refs):
+    temporal_ref, wire_ref, tiles_ref, held_ref = refs[2 * DP :]
+    totals = (product_of(refs[: 2 * DP]), temporal_ref[...])
+    rows, columns = totals[0].shape
+    whole = columns // LANES * LANES
+    tiles = [total[:, at : at + LANES] for total in totals for at in range(0, whole, LANES)]
+    tiles.append(jnp.concatenate([total[:, whole:] for total in totals], axis=1))
+    for i, tile in enumerate(tiles):
+        tiles_ref[i * rows : (i + 1) * rows] = tile
+    part = rows // SEQ
+    slots = held_ref.shape[0] // SEQ
+    for slot in range(slots):
+        tile, row = slot // part, slot % part
+        if tile < len(tiles):
+            taken = tiles_ref[pl.ds(tile * rows + row, SEQ, stride=part), :]
+        else:
+            taken = jnp.zeros((SEQ, LANES), F32)
+        held_ref[pl.ds(slot, SEQ, stride=slots), :] = taken
+    wire_ref[...] = held_ref[...].astype(BF)
 
 
 def weight_sums(arrived_ref, spatial_ref, temporal_ref):
-    part = spatial_ref.shape[0]
-    total = add_sources([arrived_ref[i] for i in range(arrived_ref.shape[0])])
-    spatial_ref[...] = total[:part]
-    temporal_ref[...] = total[part : 2 * part]
+    slots = arrived_ref.shape[0] // SEQ
+    total = arrived_ref[:slots].astype(F32)
+    for i in range(1, SEQ):
+        total = total + arrived_ref[i * slots : (i + 1) * slots].astype(F32)
+    part, columns = spatial_ref.shape
+    whole = columns // LANES * LANES
+    at = 0
+    for ref in (spatial_ref, temporal_ref):
+        for start in range(0, whole, LANES):
+            ref[:, start : start + LANES] = total[at : at + part]
+            at += part
+    spatial_ref[:, whole:] = total[at : at + part, : columns - whole]
+    temporal_ref[:, whole:] = total[at : at + part, columns - whole :]
 
 
 class Late:
@@ -345,7 +360,7 @@
             self.start()
 
 
-def call(body, outs, *operands, scalars=0, scratch=(), flops=0, manual=False):
+def call(body, outs, *operands, scalars=0, scratch=(), flops=0, manual=False, vmem=0):
     smem, whole = [pl.BlockSpec(memory_space=space) for space in (pltpu.SMEM, pltpu.VMEM)]
     apart = pl.BlockSpec(memory_space=pl.ANY) if manual else whole
     count = len(operands)
@@ -385,7 +400,7 @@
         out_specs=out_specs[0] if single else out_specs,
         scratch_shapes=own + held + sems,
         cost_estimate=pl.CostEstimate(flops=flops, bytes_accessed=moved, transcendentals=0),
-        compiler_params=pltpu.CompilerParams(vmem_limit_bytes=(60 if manual else 40) * 1024 * 1024),
+        compiler_params=pltpu.CompilerParams(vmem_limit_bytes=(vmem or (60 if manual else 40)) * 1024 * 1024),
     )(*operands)
 
 
@@ -415,12 +430,6 @@
     cut = array.reshape(SEQ, rows // SEQ, width)
     moved = lax.all_to_all(cut, "seq", split_axis=0, concat_axis=0, tiled=True)
     return moved.reshape(rows, width)
-
-
-def group_all_to_all(array, groups):
-    return lax.all_to_all(
-        array, "seq", split_axis=0, concat_axis=0, tiled=True, axis_index_groups=groups
-    )
 
 
 def per_device(
@@ -437,9 +446,8 @@
     out_s = out_spatial.T
     out_t = out_temporal.T
     dp, seq = lax.axis_index("dp"), lax.axis_index("seq")
-    x_low, x_high = seq // Z_RING % 2, seq // Z_RING // 2
+    x_low = seq // Z_RING % 2
     near_place = (2 * x_low + dp % 2).astype(jnp.int32).reshape(1)
-    far_place = (2 * (dp // 2) + x_high).astype(jnp.int32).reshape(1)
     wide = ((tokens, width), BF)
     narrow = ((tokens, local), BF)
     full = ((tokens, width), F32)
@@ -448,6 +456,9 @@
     slots = wire_slots(4 * local)
     wire = ((SEQ * slots, LANES), BF)
     wire_held = pltpu.VMEM((SEQ * slots, LANES), F32)
+    slots = wire_slots(width + local)
+    back = ((SEQ * slots, LANES), BF)
+    back_held = pltpu.VMEM((SEQ * slots, LANES), F32)
     product = 2 * tokens * width * local
     attention = 4 * heads * tokens * tokens * local
 
@@ -473,12 +484,13 @@
     blocks_t = [blocks_t[0]] + [swap_near(blocks_t[i], i) for i in range(1, DP)]
     arrived = all_to_all(wire_out)
     wire_back = call(
-        temporal_step, [wire], arrived, scratch=[wire_held], flops=6 * attention
+        temporal_step, [back], arrived, proj_t, manual=True, vmem=40, scratch=[wire_held, back_held],
+        flops=3 * product + 6 * attention,
     )
     returned = all_to_all(wire_back)
     returned, heads_s, blocks_t = lax.optimization_barrier((returned, heads_s, blocks_t))
     partial_t, heads_t = call(
-        temporal_return, [wide, narrow], returned, proj_t, scratch=[wire_held], flops=4 * product
+        temporal_return, [wide, narrow], returned, scratch=[back_held]
     )
     partial_other = swap_pair(partial_t)
     heads_near = [swap_near(heads_t, i) for i in range(1, DP)]
@@ -489,27 +501,34 @@
     blocks_s = [blocks_s[0]] + [swap_near(blocks_s[i], i) for i in range(1, DP)]
     partial_s = call(
         spatial_back, [wide],
-        scaled_s, packed_s, weights_s, out_s, proj_s, flops=4 * product + 5 * attention,
+        scaled_s, out_s, packed_s, weights_s, proj_s, manual=True,
+        flops=4 * product + 5 * attention,
     )
     partial_s_other = swap_pair(partial_s)
-    piece = ((2 * width // DP // X_RING, local), BF)
+    temporal_sum = call(
+        temporal_product, [((width // DP, local), F32)], *blocks_t, heads_t, *heads_near, manual=True,
+        flops=2 * product, vmem=60,
+    )
+    slots = wire_slots(2 * width // DP // SEQ * local // QUARTERS)
     sums = call(
-        weight_products, [piece] * DP,
-        far_place, *blocks_s, *heads_s, *blocks_t, heads_t, *heads_near, scalars=1, manual=True,
-        flops=4 * product, scratch=[pltpu.VMEM((DP, *piece[0]), BF)],
-    )
-    sums = [sums[0]] + [
-        swap_both(sums[i], 2 * (i // 2), 2 * Z_RING * (i % 2)) for i in range(1, DP)
-    ]
-    sums_half = call(weight_halfway, [((Z_RING, ROWS, local), BF)], *sums)
-    sums_in = group_all_to_all(sums_half, Z_GROUPS)
-    heads_late, partial_s_other = lax.optimization_barrier((heads_t, partial_s_other))
+        weight_products, [((SEQ * slots, LANES), BF)],
+        *blocks_s, *heads_s, temporal_sum, manual=True, flops=2 * product, vmem=60,
+        scratch=[
+            pltpu.VMEM((2 * local // LANES * width // DP, LANES), F32),
+            pltpu.VMEM((SEQ * slots, LANES), F32),
+        ],
+    )
+    heads_late, sums = lax.optimization_barrier((heads_t, sums))
     mixed_t = call(mix_temporal, [wide], heads_late, out_t, flops=product)
     mixed_t_other = swap_pair(mixed_t)
+    sums = lax.all_to_all(
+        sums.reshape(SEQ, slots, LANES), ("dp", "seq"), split_axis=0, concat_axis=0, tiled=True,
+        axis_index_groups=FAR_GROUPS,
+    ).reshape(SEQ * slots, LANES)
     block_output = call(output_step, [wide], middle, mod, mixed_t, mixed_t_other)
     latent_grad = call(latent_step, [full], x, mod, grad_middle, partial_s, partial_s_other)
     part = ((width // DP // SEQ, local), F32)
-    grad_out_s, grad_out_t = call(weight_sums, [part, part], sums_in)
+    grad_out_s, grad_out_t = call(weight_sums, [part, part], sums)
     return (
         block_output.reshape(latents.shape),
         latent_grad.reshape(latents.shape),

time: 137 us -> 132 us (0.964)
  local copies, waits for them, and re-layouts: 15.8 us -> 6.83 us
  Pallas kernels: 27.9 us -> 31.7 us
    unnamed x56 -> x50, local copies, waits for them, and re-layouts: 15.8 us -> 6.83 us
    ppermute x4, waiting for transfers between devices: 9.26 us -> 17.9 us  [swap_pair(): return lax.ppermute(array, 'tensor', PAIR)]
    all_to_all x1, starting transfers between devices: 4.85 us -> 9.51 us  [per_device(): lax.all_to_all(sums.reshape(SEQ, slots, LANES), ('dp', 'seq'), split_axis...]
    ppermute x6 -> x5, waiting for transfers between devices: 4.02 us -> 0.01 us  [swap_dp(): return lax.ppermute(array, 'dp', [(i, i ^ mask) for i in range(DP)])]
    pallas_call x13, Pallas kernels: 27.9 us -> 31.7 us  [call(): pl.pallas_call(wrapped, out_shape=shapes[0] if single else shapes, in_spe...]
    ppermute x4 -> x3, starting transfers between devices: 4.75 us -> 1.27 us  [swap_both(): lax.ppermute(array, ('dp', 'seq'), [(i, i ^ mask) for i in range(DP * SEQ)])]
    ppermute x6 -> x5, starting transfers between devices: 3.47 us -> 1.49 us  [swap_dp(): return lax.ppermute(array, 'dp', [(i, i ^ mask) for i in range(DP)])]
    all_to_all x1, waiting for transfers between devices: 6.72 us -> 4.81 us  [all_to_all(): moved = lax.all_to_all(cut, 'seq', split_axis=0, concat_axis=0, tiled=True)]
  transfers between devices with their start and end apart: 21 -> 18, of which waited for: 10 -> 10; matrix products, arithmetic and copies ran while one was open for 0% -> 0% of each run, Pallas kernels for 11% -> 10%
where the time goes in v4:
time: 132 us; the launch traced here: 130 us
  waiting for transfers between devices  33.9 us (26%)
  Pallas kernels  31.7 us (24%)
  blocking collectives  29.1 us (22%)
  starting transfers between devices  27.5 us (21%)
  local copies, waits for them, and re-layouts  6.83 us (5%)
    pallas_call x13, Pallas kernels, call(): pl.pallas_call(wrapped, out_shape=shapes[0] if single else shapes, in_spe...  31.7 us
    all_to_all x1, blocking collectives, all_to_all(): moved = lax.all_to_all(cut, 'seq', split_axis=0, concat_axis=0, tiled=True)  29.1 us
    ppermute x4, waiting for transfers between devices, swap_pair(): return lax.ppermute(array, 'tensor', PAIR)  17.9 us
    all_to_all x1, starting transfers between devices, per_device(): lax.all_to_all(sums.reshape(SEQ, slots, LANES), ('dp', 'seq'), split_axis...  9.51 us
    ppermute x4, waiting for transfers between devices, swap_both(): return lax.ppermute(array, 'seq', [(i, i ^ seq_mask) for i in range(SEQ)])  8.65 us
    unnamed x50, local copies, waits for them, and re-layouts  6.83 us
    ppermute x4, starting transfers between devices, swap_pair(): return lax.ppermute(array, 'tensor', PAIR)  5.52 us
    all_to_all x1, starting transfers between devices, all_to_all(): moved = lax.all_to_all(cut, 'seq', split_axis=0, concat_axis=0, tiled=True)  4.95 us
  transfers between devices with their start and end apart: 18, of which 10 were waited for; matrix products, arithmetic and copies ran while one was open for 0% of the time, Pallas kernels for 10%

profile of v4, /device:TPU:32, one launch (start us, length us, event | category | flops | bytes accessed | tf_op | source)
XLA Modules:
  0.0 130.0 jit_solution(7788494022370709007)
XLA Ops:
  0.7 7.0 %shard_map.102 = (bf16[3,128,576]{2,1,0:T(8,128)(2,1)}, f32[1024,128]{1,0:T(8,128)}, bf16[128,576]{1,0:T(8,128)(2,1)}, bf16[128,1152]{1,0:T(8,128)(2,1)}) custom-call(bf16[128,1152]{1,0:T(8,128)(2,1)} %bitcast.21, f32[6,1,1152]{2,1,0:T(1,128)} %bitcast.29, bf16[3,576,1152]{2,1,0:T(8,128)(2,1)} %bitcast.37, bf16[576,1152]{1,0:T(8,128)(2,1)} %bitcast.40), custom_call_target="tpu_custom_call" | custom-call | flops 981467136 | bytes 7040000 | tf_op jit(solution)/shard_map/pallas_call | solution.py:396
  7.7 1.7 %collective-permute-start = (bf16[128,1152]{1,0:T(8,128)(2,1)}, bf16[128,1152]{1,0:T(8,128)(2,1)S(1)}, u32[]{:S(2)}, u32[]{:S(2)}) collective-permute-start(bf16[128,1152]{1,0:T(8,128)(2,1)} %get-tuple-element.39.refs_1_), channel_id=1, source_target_pairs={{0,1},{1,0},{2,3},{3,2},{4,5},{5,4},{6,7},{7,6},{8,9},{9,8},{10,11... | collective-permute-start | bytes 884744 | tf_op jit(solution)/shard_map/ppermute | solution.py:408
  9.3 1.5 %collective-permute-start.1 = (bf16[128,576]{1,0:T(8,128)(2,1)}, bf16[128,576]{1,0:T(8,128)(2,1)S(1)}, u32[]{:S(2)}, u32[]{:S(2)}) collective-permute-start(bf16[128,576]{1,0:T(8,128)(2,1)} %get-tuple-element.58.refs_4_), channel_id=1, source_target_pairs={{0,16},{2,18},{4,20},{6,22},{8,24},{10,26},{12,28},{14,30},{16,0},... | collective-permute-start | bytes 442376 | tf_op jit(solution)/shard_map/ppermute | solution.py:415
  10.9 2.1 %copy-done = bf16[1152,3,576]{0,2,1:T(8,128)(2,1)S(1)} copy-done((bf16[1152,3,576]{0,2,1:T(8,128)(2,1)S(1)}, bf16[1152,3,576]{0,2,1:T(8,128)(2,1)}, u32[]{:S(2)}) %copy-start) | copy-done | bytes 3981336
  13.6 1.6 %collective-permute-done.1.refs_6_ = bf16[128,576]{1,0:T(8,128)(2,1)S(1)} collective-permute-done((bf16[128,576]{1,0:T(8,128)(2,1)}, bf16[128,576]{1,0:T(8,128)(2,1)S(1)}, u32[]{:S(2)}, u32[]{:S(2)}) %collective-permute-start.1) | collective-permute-done | bytes 147488 | tf_op jit(solution)/shard_map/ppermute | solution.py:415
  15.2 1.5 %collective-permute-done.refs_2_ = bf16[128,1152]{1,0:T(8,128)(2,1)S(1)} collective-permute-done((bf16[128,1152]{1,0:T(8,128)(2,1)}, bf16[128,1152]{1,0:T(8,128)(2,1)S(1)}, u32[]{:S(2)}, u32[]{:S(2)}) %collective-permute-start) | collective-permute-done | bytes 294944 | tf_op jit(solution)/shard_map/ppermute | solution.py:408
  16.7 1.7 %shard_map.104 = (bf16[2304,128]{1,0:T(8,128)(2,1)S(1)}, f32[128,1152]{1,0:T(8,128)S(1)}) custom-call(bf16[128,1152]{1,0:T(8,128)(2,1)S(1)} %bitcast.23, bf16[128,1152]{1,0:T(8,128)(2,1)S(1)} %copy-done.10, bf16[128,1152]{1,0:T(8,128)(2,1)S(1)} %collective-permute-done.refs_2_, f32[6,1,1152]{2,1,0:T(1,128)S(1)} %bitcast.31, ...), custom_call_target="tpu_custom_call" | custom-call | flops 679477248 | bytes 6220800 | tf_op jit(solution)/shard_map/pallas_call | solution.py:396
  18.5 29.1 %all_to_all.15 = bf16[32,72,128]{2,1,0:T(8,128)(2,1)S(1)} all-to-all(bf16[32,72,128]{2,1,0:T(8,128)(2,1)S(1)} %bitcast.35), channel_id=1, replica_groups=mesh['dp'=4,'seq'=32,'tensor'=2] {'seq'}, dimensions={0} | all-to-all | bytes 1179648 | tf_op jit(solution)/shard_map/all_to_all | solution.py:431
  47.6 4.9 %shard_map.105 = bf16[1792,128]{1,0:T(8,128)(2,1)} custom-call(bf16[2304,128]{1,0:T(8,128)(2,1)S(1)} %bitcast.36, bf16[3,576,1152]{2,1,0:T(8,128)(2,1)S(1)} %bitcast.18), custom_call_target="tpu_custom_call" | custom-call | flops 2321547264 | bytes 5029888 | tf_op jit(solution)/shard_map/pallas_call | solution.py:396
  52.5 4.9 %all-to-all-start.1 = ((bf16[32,56,128]{2,1,0:T(8,128)(2,1)}), bf16[32,56,128]{2,1,0:T(8,128)(2,1)S(1)}, u32[]{:S(2)}, u32[]{:S(2)}) async-start(bf16[32,56,128]{2,1,0:T(8,128)(2,1)} %bitcast.10), calls=%async_computation.1 | async-start | bytes 917504 | tf_op jit(solution)/shard_map/all_to_all | solution.py:431
  58.1 1.5 %collective-permute-start.5 = (bf16[128,288]{1,0:T(8,128)(2,1)S(1)}, bf16[128,288]{1,0:T(8,128)(2,1)S(1)}, u32[]{:S(2)}, u32[]{:S(2)}) collective-permute-start(bf16[128,288]{1,0:T(8,128)(2,1)S(1)} %get-tuple-element.49), channel_id=1, source_target_pairs={{0,16},{2,18},{4,20},{6,22},{8,24},{10,26},{12,28},{14,30},{16,0},... | collective-permute-start | bytes 221192 | tf_op jit(solution)/shard_map/ppermute | solution.py:415
  59.6 5.7 %collective-permute-done.5.refs_2_ = bf16[128,288]{1,0:T(8,128)(2,1)S(1)} collective-permute-done((bf16[128,288]{1,0:T(8,128)(2,1)S(1)}, bf16[128,288]{1,0:T(8,128)(2,1)S(1)}, u32[]{:S(2)}, u32[]{:S(2)}) %collective-permute-start.5) | collective-permute-done | bytes 73760 | tf_op jit(solution)/shard_map/ppermute | solution.py:415
  65.3 2.1 %collective-permute-done.6.refs_3_ = bf16[128,288]{1,0:T(8,128)(2,1)S(1)} collective-permute-done((bf16[128,288]{1,0:T(8,128)(2,1)S(1)}, bf16[128,288]{1,0:T(8,128)(2,1)S(1)}, u32[]{:S(2)}, u32[]{:S(2)}) %collective-permute-start.6) | collective-permute-done | bytes 73760 | tf_op jit(solution)/shard_map/ppermute | solution.py:417
  68.0 4.8 %all-to-all-done.1 = bf16[32,56,128]{2,1,0:T(8,128)(2,1)S(1)} async-done(((bf16[32,56,128]{2,1,0:T(8,128)(2,1)}), bf16[32,56,128]{2,1,0:T(8,128)(2,1)S(1)}, u32[]{:S(2)}, u32[]{:S(2)}) %all-to-all-start.1) | async-done | bytes 458784 | tf_op jit(solution)/shard_map/all_to_all | solution.py:431
  73.0 1.6 %collective-permute-start.7 = (bf16[128,1152]{1,0:T(8,128)(2,1)S(1)}, bf16[128,1152]{1,0:T(8,128)(2,1)S(1)}, u32[]{:S(2)}, u32[]{:S(2)}) collective-permute-start(bf16[128,1152]{1,0:T(8,128)(2,1)S(1)} %get-tuple-element.53.refs_4_), channel_id=1, source_target_pairs={{0,1},{1,0},{2,3},{3,2},{4,5},{5,4},{6,7},{7,6},{8,9},{9,8},{10,11... | collective-permute-start | bytes 884744 | tf_op jit(solution)/shard_map/ppermute | solution.py:408
  76.5 3.3 %collective-permute-done.7.refs_5_ = bf16[128,1152]{1,0:T(8,128)(2,1)S(1)} collective-permute-done((bf16[128,1152]{1,0:T(8,128)(2,1)S(1)}, bf16[128,1152]{1,0:T(8,128)(2,1)S(1)}, u32[]{:S(2)}, u32[]{:S(2)}) %collective-permute-start.7) | collective-permute-done | bytes 294944 | tf_op jit(solution)/shard_map/ppermute | solution.py:408
  84.5 3.1 %shard_map.108.refs_8_ = f32[288,576]{1,0:T(8,128)} custom-call(bf16[128,288]{1,0:T(8,128)(2,1)} %copy-done.13, bf16[128,288]{1,0:T(8,128)(2,1)} %copy-done.22, bf16[128,288]{1,0:T(8,128)(2,1)} %copy-done.23, bf16[128,288]{1,0:T(8,128)(2,1)} %copy-done.24, bf16[128,576]{1,0:T(8,128)(2,1)} %copy-done.6, bf16[128,576]{1,0:T(8,128)(2,1)} %copy-done.17, ...), custom_call_target="tpu_custom_call" | custom-call | flops 339738624 | bytes 1548288 | tf_op jit(solution)/shard_map/pallas_call | solution.py:396
  87.7 1.3 %collective-permute-done.9.refs_2_ = bf16[128,288]{1,0:T(8,128)(2,1)S(1)} collective-permute-done((bf16[128,288]{1,0:T(8,128)(2,1)S(1)}, bf16[128,288]{1,0:T(8,128)(2,1)S(1)}, u32[]{:S(2)}, u32[]{:S(2)}) %collective-permute-start.9) | collective-permute-done | bytes 73760 | tf_op jit(solution)/shard_map/ppermute | solution.py:415
  89.6 3.5 %shard_map.109 = bf16[2816,128]{1,0:T(8,128)(2,1)} custom-call(bf16[128,288]{1,0:T(8,128)(2,1)} %copy-done.12, bf16[128,288]{1,0:T(8,128)(2,1)} %copy-done.20, bf16[128,288]{1,0:T(8,128)(2,1)} %copy-done.21, bf16[128,288]{1,0:T(8,128)(2,1)} %copy-done.19, bf16[128,576]{1,0:T(8,128)(2,1)} %get-tuple-element.58.refs_4_, bf16[128,576]{1,0:T(8,128)(2,1)} %copy-done.16, ...), custom_call_target="tpu_custom_call" | custom-call | flops 339738624 | bytes 2269184 | tf_op jit(solution)/shard_map/pallas_call | solution.py:396
  93.2 9.5 %all-to-all-start.2 = ((bf16[32,88,128]{2,1,0:T(8,128)(2,1)}), bf16[32,88,128]{2,1,0:T(8,128)(2,1)S(1)}, u32[]{:S(2)}, u32[]{:S(2)}) async-start(bf16[32,88,128]{2,1,0:T(8,128)(2,1)} %bitcast.39), calls=%async_computation.2 | async-start | bytes 1441792 | tf_op jit(solution)/shard_map/all_to_all | solution.py:524
  102.7 6.7 %shard_map.112.refs_3_ = bf16[128,1152]{1,0:T(8,128)(2,1)} custom-call(bf16[128,1152]{1,0:T(8,128)(2,1)} %copy-done.14, bf16[576,1152]{1,0:T(8,128)(2,1)} %bitcast.41, bf16[3,128,576]{2,1,0:T(8,128)(2,1)} %get-tuple-element.69.refs_2_, f32[1024,128]{1,0:T(8,128)} %get-tuple-element.70.refs_3_, bf16[3,576,1152]{2,1,0:T(8,128)(2,1)} %bitcast.38), custom_call_target="tpu_custom_call" | custom-call | flops 2189426688 | bytes 6864896 | tf_op jit(solution)/shard_map/pallas_call | solution.py:396
  110.6 1.4 %collective-permute-start.14 = (bf16[128,1152]{1,0:T(8,128)(2,1)S(1)}, bf16[128,1152]{1,0:T(8,128)(2,1)S(1)}, u32[]{:S(2)}, u32[]{:S(2)}) collective-permute-start(bf16[128,1152]{1,0:T(8,128)(2,1)S(1)} %shard_map.110.refs_2_), channel_id=1, source_target_pairs={{0,1},{1,0},{2,3},{3,2},{4,5},{5,4},{6,7},{7,6},{8,9},{9,8},{10,11... | collective-permute-start | bytes 884744 | tf_op jit(solution)/shard_map/ppermute | solution.py:408
  112.0 10.8 %collective-permute-done.15.refs_4_ = bf16[128,1152]{1,0:T(8,128)(2,1)S(1)} collective-permute-done((bf16[128,1152]{1,0:T(8,128)(2,1)}, bf16[128,1152]{1,0:T(8,128)(2,1)S(1)}, u32[]{:S(2)}, u32[]{:S(2)}) %collective-permute-start.15) | collective-permute-done | bytes 294944 | tf_op jit(solution)/shard_map/ppermute | solution.py:408
  126.1 2.3 %collective-permute-done.14.refs_3_ = bf16[128,1152]{1,0:T(8,128)(2,1)S(1)} collective-permute-done((bf16[128,1152]{1,0:T(8,128)(2,1)S(1)}, bf16[128,1152]{1,0:T(8,128)(2,1)S(1)}, u32[]{:S(2)}, u32[]{:S(2)}) %collective-permute-start.14) | collective-permute-done | bytes 294944 | tf_op jit(solution)/shard_map/ppermute | solution.py:408
  (76 shorter events, 15.3 us)
Async XLA Ops:
  7.7 9.1 %collective-permute-start = (bf16[128,1152]{1,0:T(8,128)(2,1)}, bf16[128,1152]{1,0:T(8,128)(2,1)S(1)}, u32[]{:S(2)}, u32[]{:S(2)}) collective-permute-start(bf16[128,1152]{1,0:T(8,128)(2,1)} %get-tuple-element.39.refs_1_), channel_id=1, source_target_pairs={{0,1},{1,0},{2,3},{3,2},{4,5},{5,4},{6,7},{7,6},{8,9},{9,8},{10,11... | collective-permute-start | bytes 884744 | tf_op jit(solution)/shard_map/ppermute | solution.py:408
  9.3 5.9 %collective-permute-start.1 = (bf16[128,576]{1,0:T(8,128)(2,1)}, bf16[128,576]{1,0:T(8,128)(2,1)S(1)}, u32[]{:S(2)}, u32[]{:S(2)}) collective-permute-start(bf16[128,576]{1,0:T(8,128)(2,1)} %get-tuple-element.58.refs_4_), channel_id=1, source_target_pairs={{0,16},{2,18},{4,20},{6,22},{8,24},{10,26},{12,28},{14,30},{16,0},... | collective-permute-start | bytes 442376 | tf_op jit(solution)/shard_map/ppermute | solution.py:415
  10.8 4.4 %collective-permute-start.2 = (bf16[128,576]{1,0:T(8,128)(2,1)}, bf16[128,576]{1,0:T(8,128)(2,1)S(1)}, u32[]{:S(2)}, u32[]{:S(2)}) collective-permute-start(bf16[128,576]{1,0:T(8,128)(2,1)} %get-tuple-element.58.refs_4_), channel_id=1, source_target_pairs={{0,64},{64,0},{128,192},{192,128},{1,65},{65,1},{129,193},{193,129... | collective-permute-start | bytes 442376 | tf_op jit(solution)/shard_map/ppermute | solution.py:425
  13.6 38.9 %copy-start.13 = (bf16[128,288]{1,0:T(8,128)(2,1)}, bf16[128,288]{1,0:T(8,128)(2,1)S(1)}, u32[]{:S(2)}) copy-start(bf16[128,288]{1,0:T(8,128)(2,1)S(1)} %get-tuple-element.62.refs_0_) | copy-start | bytes 221188
  15.2 42.2 %copy-start.15 = (bf16[128,576]{1,0:T(8,128)(2,1)}, bf16[128,576]{1,0:T(8,128)(2,1)S(1)}, u32[]{:S(2)}) copy-start(bf16[128,576]{1,0:T(8,128)(2,1)S(1)} %collective-permute-done.1.refs_6_) | copy-start | bytes 442372
  15.2 37.3 %copy-start.16 = (bf16[128,576]{1,0:T(8,128)(2,1)}, bf16[128,576]{1,0:T(8,128)(2,1)S(1)}, u32[]{:S(2)}) copy-start(bf16[128,576]{1,0:T(8,128)(2,1)S(1)} %collective-permute-done.2.refs_5_) | copy-start | bytes 442372
  52.5 20.3 %all-to-all-start.1 = ((bf16[32,56,128]{2,1,0:T(8,128)(2,1)}), bf16[32,56,128]{2,1,0:T(8,128)(2,1)S(1)}, u32[]{:S(2)}, u32[]{:S(2)}) async-start(bf16[32,56,128]{2,1,0:T(8,128)(2,1)} %bitcast.10), calls=%async_computation.1 | async-start | bytes 917504 | tf_op jit(solution)/shard_map/all_to_all | solution.py:431
  57.5 10.5 %collective-permute-start.3 = (bf16[128,576]{1,0:T(8,128)(2,1)S(1)}, bf16[128,576]{1,0:T(8,128)(2,1)}, u32[]{:S(2)}, u32[]{:S(2)}) collective-permute-start(bf16[128,576]{1,0:T(8,128)(2,1)S(1)} %collective-permute-done.1.refs_6_), channel_id=1, source_target_pairs={{0,64},{64,0},{128,192},{192,128},{1,65},{65,1},{129,193},{193,129... | collective-permute-start | bytes 442376 | tf_op jit(solution)/shard_map/ppermute | solution.py:425
  57.6 2.0 %collective-permute-start.4 = (bf16[128,288]{1,0:T(8,128)(2,1)S(1)}, bf16[128,288]{1,0:T(8,128)(2,1)S(1)}, u32[]{:S(2)}, u32[]{:S(2)}) collective-permute-start(bf16[128,288]{1,0:T(8,128)(2,1)S(1)} %get-tuple-element.48), channel_id=1, source_target_pairs={{0,64},{64,0},{128,192},{192,128},{1,65},{65,1},{129,193},{193,129... | collective-permute-start | bytes 221192 | tf_op jit(solution)/shard_map/ppermute | solution.py:425
  58.1 7.2 %collective-permute-start.5 = (bf16[128,288]{1,0:T(8,128)(2,1)S(1)}, bf16[128,288]{1,0:T(8,128)(2,1)S(1)}, u32[]{:S(2)}, u32[]{:S(2)}) collective-permute-start(bf16[128,288]{1,0:T(8,128)(2,1)S(1)} %get-tuple-element.49), channel_id=1, source_target_pairs={{0,16},{2,18},{4,20},{6,22},{8,24},{10,26},{12,28},{14,30},{16,0},... | collective-permute-start | bytes 221192 | tf_op jit(solution)/shard_map/ppermute | solution.py:415
  59.5 7.8 %collective-permute-start.6 = (bf16[128,288]{1,0:T(8,128)(2,1)S(1)}, bf16[128,288]{1,0:T(8,128)(2,1)S(1)}, u32[]{:S(2)}, u32[]{:S(2)}) collective-permute-start(bf16[128,288]{1,0:T(8,128)(2,1)S(1)} %get-tuple-element.50), channel_id=1, source_target_pairs={{0,80},{2,82},{4,84},{6,86},{8,88},{10,90},{12,92},{14,94},{16,64}... | collective-permute-start | bytes 221192 | tf_op jit(solution)/shard_map/ppermute | solution.py:417
  59.5 25.0 %copy-start.22 = (bf16[128,288]{1,0:T(8,128)(2,1)}, bf16[128,288]{1,0:T(8,128)(2,1)S(1)}, u32[]{:S(2)}) copy-start(bf16[128,288]{1,0:T(8,128)(2,1)S(1)} %collective-permute-done.4.refs_1_) | copy-start | bytes 221188
  73.0 11.5 %copy-start.6 = (bf16[128,576]{1,0:T(8,128)(2,1)}, bf16[128,576]{1,0:T(8,128)(2,1)S(1)}, u32[]{:S(2)}) copy-start(bf16[128,576]{1,0:T(8,128)(2,1)S(1)} %get-tuple-element.66.refs_4_.refs_0_) | copy-start | bytes 442372
  73.0 6.8 %collective-permute-start.7 = (bf16[128,1152]{1,0:T(8,128)(2,1)S(1)}, bf16[128,1152]{1,0:T(8,128)(2,1)S(1)}, u32[]{:S(2)}, u32[]{:S(2)}) collective-permute-start(bf16[128,1152]{1,0:T(8,128)(2,1)S(1)} %get-tuple-element.53.refs_4_), channel_id=1, source_target_pairs={{0,1},{1,0},{2,3},{3,2},{4,5},{5,4},{6,7},{7,6},{8,9},{9,8},{10,11... | collective-permute-start | bytes 884744 | tf_op jit(solution)/shard_map/ppermute | solution.py:408
  74.7 7.5 %collective-permute-start.11 = (bf16[128,576]{1,0:T(8,128)(2,1)S(1)}, bf16[128,576]{1,0:T(8,128)(2,1)S(1)}, u32[]{:S(2)}, u32[]{:S(2)}) collective-permute-start(bf16[128,576]{1,0:T(8,128)(2,1)S(1)} %get-tuple-element.66.refs_4_.refs_0_), channel_id=1, source_target_pairs={{0,64},{64,0},{128,192},{192,128},{1,65},{65,1},{129,193},{193,129... | collective-permute-start | bytes 442376 | tf_op jit(solution)/shard_map/ppermute | solution.py:425
  74.7 8.7 %collective-permute-start.12 = (bf16[128,576]{1,0:T(8,128)(2,1)S(1)}, bf16[128,576]{1,0:T(8,128)(2,1)S(1)}, u32[]{:S(2)}, u32[]{:S(2)}) collective-permute-start(bf16[128,576]{1,0:T(8,128)(2,1)S(1)} %get-tuple-element.66.refs_4_.refs_0_), channel_id=1, source_target_pairs={{0,16},{2,18},{4,20},{6,22},{8,24},{10,26},{12,28},{14,30},{16,0},... | collective-permute-start | bytes 442376 | tf_op jit(solution)/shard_map/ppermute | solution.py:415
  75.3 9.2 %collective-permute-start.13 = (bf16[128,576]{1,0:T(8,128)(2,1)S(1)}, bf16[128,576]{1,0:T(8,128)(2,1)}, u32[]{:S(2)}, u32[]{:S(2)}) collective-permute-start(bf16[128,576]{1,0:T(8,128)(2,1)S(1)} %get-tuple-element.66.refs_4_.refs_0_), channel_id=1, source_target_pairs={{0,80},{2,82},{4,84},{6,86},{8,88},{10,90},{12,92},{14,94},{16,64}... | collective-permute-start | bytes 442376 | tf_op jit(solution)/shard_map/ppermute | solution.py:417
  81.2 11.9 %copy-start.8 = (f32[128,1152]{1,0:T(8,128)}, f32[128,1152]{1,0:T(8,128)S(1)}, u32[]{:S(2)}) copy-start(f32[128,1152]{1,0:T(8,128)S(1)} %get-tuple-element.67.refs_2_) | copy-start | bytes 1769476
  81.2 6.4 %collective-permute-start.10 = (bf16[128,288]{1,0:T(8,128)(2,1)S(1)}, bf16[128,288]{1,0:T(8,128)(2,1)S(1)}, u32[]{:S(2)}, u32[]{:S(2)}) collective-permute-start(bf16[128,288]{1,0:T(8,128)(2,1)S(1)} %get-tuple-element.57), channel_id=1, source_target_pairs={{0,80},{2,82},{4,84},{6,86},{8,88},{10,90},{12,92},{14,94},{16,64}... | collective-permute-start | bytes 221192 | tf_op jit(solution)/shard_map/ppermute | solution.py:417
  81.2 6.4 %collective-permute-start.8 = (bf16[128,288]{1,0:T(8,128)(2,1)S(1)}, bf16[128,288]{1,0:T(8,128)(2,1)S(1)}, u32[]{:S(2)}, u32[]{:S(2)}) collective-permute-start(bf16[128,288]{1,0:T(8,128)(2,1)S(1)} %get-tuple-element.55), channel_id=1, source_target_pairs={{0,64},{64,0},{128,192},{192,128},{1,65},{65,1},{129,193},{193,129... | collective-permute-start | bytes 221192 | tf_op jit(solution)/shard_map/ppermute | solution.py:425
  82.2 6.9 %collective-permute-start.9 = (bf16[128,288]{1,0:T(8,128)(2,1)S(1)}, bf16[128,288]{1,0:T(8,128)(2,1)S(1)}, u32[]{:S(2)}, u32[]{:S(2)}) collective-permute-start(bf16[128,288]{1,0:T(8,128)(2,1)S(1)} %get-tuple-element.56), channel_id=1, source_target_pairs={{0,16},{2,18},{4,20},{6,22},{8,24},{10,26},{12,28},{14,30},{16,0},... | collective-permute-start | bytes 221192 | tf_op jit(solution)/shard_map/ppermute | solution.py:415
  93.2 36.1 %all-to-all-start.2 = ((bf16[32,88,128]{2,1,0:T(8,128)(2,1)}), bf16[32,88,128]{2,1,0:T(8,128)(2,1)S(1)}, u32[]{:S(2)}, u32[]{:S(2)}) async-start(bf16[32,88,128]{2,1,0:T(8,128)(2,1)} %bitcast.39), calls=%async_computation.2 | async-start | bytes 1441792 | tf_op jit(solution)/shard_map/all_to_all | solution.py:524
  109.4 13.4 %collective-permute-start.15 = (bf16[128,1152]{1,0:T(8,128)(2,1)}, bf16[128,1152]{1,0:T(8,128)(2,1)S(1)}, u32[]{:S(2)}, u32[]{:S(2)}) collective-permute-start(bf16[128,1152]{1,0:T(8,128)(2,1)} %shard_map.112.refs_3_), channel_id=1, source_target_pairs={{0,1},{1,0},{2,3},{3,2},{4,5},{5,4},{6,7},{7,6},{8,9},{9,8},{10,11... | collective-permute-start | bytes 884744 | tf_op jit(solution)/shard_map/ppermute | solution.py:408
  110.6 17.8 %collective-permute-start.14 = (bf16[128,1152]{1,0:T(8,128)(2,1)S(1)}, bf16[128,1152]{1,0:T(8,128)(2,1)S(1)}, u32[]{:S(2)}, u32[]{:S(2)}) collective-permute-start(bf16[128,1152]{1,0:T(8,128)(2,1)S(1)} %shard_map.110.refs_2_), channel_id=1, source_target_pairs={{0,1},{1,0},{2,3},{3,2},{4,5},{5,4},{6,7},{7,6},{8,9},{9,8},{10,11... | collective-permute-start | bytes 884744 | tf_op jit(solution)/shard_map/ppermute | solution.py:408
  (19 other events, 76.4 us)

commit v5 on v4

--- a/solution.py
+++ b/solution.py
@@ -493,7 +493,9 @@
         temporal_return, [wide, narrow], returned, scratch=[back_held]
     )
     partial_other = swap_pair(partial_t)
-    heads_near = [swap_near(heads_t, i) for i in range(1, DP)]
+    heads_near = [swap_near(heads_t, 1), swap_near(heads_t, 2)]
+    heads_near.append(swap_near(heads_near[1], 1))
+    partial_other, heads_near[1] = lax.optimization_barrier((partial_other, heads_near[1]))
     *blocks_s, scaled_s, grad_middle = call(
         middle_back, [block] * DP + [wide, full],
         near_place, cot, middle, mod, partial_t, partial_other, scalars=1, scratch=[blocks_held],
@@ -509,6 +511,10 @@
         temporal_product, [((width // DP, local), F32)], *blocks_t, heads_t, *heads_near, manual=True,
         flops=2 * product, vmem=60,
     )
+    heads_late, _ = lax.optimization_barrier((heads_t, blocks_s[0]))
+    mixed_t = call(mix_temporal, [wide], heads_late, out_t, flops=product)
+    mixed_t_other = swap_pair(mixed_t)
+    temporal_sum, mixed_t_other = lax.optimization_barrier((temporal_sum, mixed_t_other))
     slots = wire_slots(2 * width // DP // SEQ * local // QUARTERS)
     sums = call(
         weight_products, [((SEQ * slots, LANES), BF)],
@@ -518,9 +524,6 @@
             pltpu.VMEM((SEQ * slots, LANES), F32),
         ],
     )
-    heads_late, sums = lax.optimization_barrier((heads_t, sums))
-    mixed_t = call(mix_temporal, [wide], heads_late, out_t, flops=product)
-    mixed_t_other = swap_pair(mixed_t)
     sums = lax.all_to_all(
         sums.reshape(SEQ, slots, LANES), ("dp", "seq"), split_axis=0, concat_axis=0, tiled=True,
         axis_index_groups=FAR_GROUPS,

time: 132 us -> 130 us (0.985); the launches traced: 130 us -> 129 us
  local copies, waits for them, and re-layouts: 6.83 us -> 5.08 us
    ppermute x4, waiting for transfers between devices: 17.9 us -> 10.6 us  [swap_pair(): return lax.ppermute(array, 'tensor', PAIR)]
    ppermute x4, waiting for transfers between devices: 8.65 us -> 13 us  [swap_both(): return lax.ppermute(array, 'seq', [(i, i ^ seq_mask) for i in range(SEQ)])]
    all_to_all x1, waiting for transfers between devices: 0.01 us -> 3.2 us  [per_device(): lax.all_to_all(sums.reshape(SEQ, slots, LANES), ('dp', 'seq'), split_axis...]
    unnamed x50 -> x52, local copies, waits for them, and re-layouts: 6.83 us -> 5.08 us
    ppermute x3 -> x2, waiting for transfers between devices: 2.54 us -> 3.21 us  [swap_both(): lax.ppermute(array, ('dp', 'seq'), [(i, i ^ mask) for i in range(DP * SEQ)])]
  transfers between devices with their start and end apart: 18 -> 18, of which waited for: 10 -> 11; matrix products, arithmetic and copies ran while one was open for 0% -> 0% of each run, Pallas kernels for 10% -> 10%
where the time goes in v5:
time: 130 us; the launch traced here: 129 us
  waiting for transfers between devices  35 us (27%)
  Pallas kernels  31.7 us (24%)
  blocking collectives  29.3 us (23%)
  starting transfers between devices  27.3 us (21%)
  local copies, waits for them, and re-layouts  5.08 us (4%)
    pallas_call x13, Pallas kernels, call(): pl.pallas_call(wrapped, out_shape=shapes[0] if single else shapes, in_spe...  31.7 us
    all_to_all x1, blocking collectives, all_to_all(): moved = lax.all_to_all(cut, 'seq', split_axis=0, concat_axis=0, tiled=True)  29.3 us
    ppermute x4, waiting for transfers between devices, swap_both(): return lax.ppermute(array, 'seq', [(i, i ^ seq_mask) for i in range(SEQ)])  13 us
    ppermute x4, waiting for transfers between devices, swap_pair(): return lax.ppermute(array, 'tensor', PAIR)  10.6 us
    all_to_all x1, starting transfers between devices, per_device(): lax.all_to_all(sums.reshape(SEQ, slots, LANES), ('dp', 'seq'), split_axis...  10.5 us
    ppermute x4, starting transfers between devices, swap_pair(): return lax.ppermute(array, 'tensor', PAIR)  5.32 us
    unnamed x52, local copies, waits for them, and re-layouts  5.08 us
    all_to_all x1, starting transfers between devices, all_to_all(): moved = lax.all_to_all(cut, 'seq', split_axis=0, concat_axis=0, tiled=True)  4.95 us
  transfers between devices with their start and end apart: 18, of which 11 were waited for; matrix products, arithmetic and copies ran while one was open for 0% of the time, Pallas kernels for 10%

profile of v5, /device:TPU:32, one launch (start us, length us, event | category | flops | bytes accessed | tf_op | source)
XLA Modules:
  0.0 129.3 jit_solution(17247565986669549026)
XLA Ops:
  0.7 7.0 %shard_map.102 = (bf16[3,128,576]{2,1,0:T(8,128)(2,1)}, f32[1024,128]{1,0:T(8,128)}, bf16[128,576]{1,0:T(8,128)(2,1)}, bf16[128,1152]{1,0:T(8,128)(2,1)}) custom-call(bf16[128,1152]{1,0:T(8,128)(2,1)} %bitcast.21, f32[6,1,1152]{2,1,0:T(1,128)} %bitcast.29, bf16[3,576,1152]{2,1,0:T(8,128)(2,1)} %bitcast.37, bf16[576,1152]{1,0:T(8,128)(2,1)} %bitcast.40), custom_call_target="tpu_custom_call" | custom-call | flops 981467136 | bytes 7040000 | tf_op jit(solution)/shard_map/pallas_call | solution.py:396
  7.7 1.7 %collective-permute-start = (bf16[128,1152]{1,0:T(8,128)(2,1)}, bf16[128,1152]{1,0:T(8,128)(2,1)S(1)}, u32[]{:S(2)}, u32[]{:S(2)}) collective-permute-start(bf16[128,1152]{1,0:T(8,128)(2,1)} %get-tuple-element.42.refs_1_), channel_id=1, source_target_pairs={{0,1},{1,0},{2,3},{3,2},{4,5},{5,4},{6,7},{7,6},{8,9},{9,8},{10,11... | collective-permute-start | bytes 884744 | tf_op jit(solution)/shard_map/ppermute | solution.py:408
  9.4 1.5 %collective-permute-start.1 = (bf16[128,576]{1,0:T(8,128)(2,1)}, bf16[128,576]{1,0:T(8,128)(2,1)S(1)}, u32[]{:S(2)}, u32[]{:S(2)}) collective-permute-start(bf16[128,576]{1,0:T(8,128)(2,1)} %get-tuple-element.73.refs_4_), channel_id=1, source_target_pairs={{0,16},{2,18},{4,20},{6,22},{8,24},{10,26},{12,28},{14,30},{16,0},... | collective-permute-start | bytes 442376 | tf_op jit(solution)/shard_map/ppermute | solution.py:415
  10.9 2.1 %copy-done = bf16[1152,3,576]{0,2,1:T(8,128)(2,1)S(1)} copy-done((bf16[1152,3,576]{0,2,1:T(8,128)(2,1)S(1)}, bf16[1152,3,576]{0,2,1:T(8,128)(2,1)}, u32[]{:S(2)}) %copy-start) | copy-done | bytes 3981336
  13.6 2.5 %collective-permute-done.1.refs_6_ = bf16[128,576]{1,0:T(8,128)(2,1)S(1)} collective-permute-done((bf16[128,576]{1,0:T(8,128)(2,1)}, bf16[128,576]{1,0:T(8,128)(2,1)S(1)}, u32[]{:S(2)}, u32[]{:S(2)}) %collective-permute-start.1) | collective-permute-done | bytes 147488 | tf_op jit(solution)/shard_map/ppermute | solution.py:415
  16.7 1.7 %shard_map.104 = (bf16[2304,128]{1,0:T(8,128)(2,1)S(1)}, f32[128,1152]{1,0:T(8,128)S(1)}) custom-call(bf16[128,1152]{1,0:T(8,128)(2,1)S(1)} %bitcast.23, bf16[128,1152]{1,0:T(8,128)(2,1)S(1)} %copy-done.9, bf16[128,1152]{1,0:T(8,128)(2,1)S(1)} %collective-permute-done.refs_2_, f32[6,1,1152]{2,1,0:T(1,128)S(1)} %bitcast.31, ...), custom_call_target="tpu_custom_call" | custom-call | flops 679477248 | bytes 6220800 | tf_op jit(solution)/shard_map/pallas_call | solution.py:396
  18.5 29.3 %all_to_all.15 = bf16[32,72,128]{2,1,0:T(8,128)(2,1)S(1)} all-to-all(bf16[32,72,128]{2,1,0:T(8,128)(2,1)S(1)} %bitcast.35), channel_id=1, replica_groups=mesh['dp'=4,'seq'=32,'tensor'=2] {'seq'}, dimensions={0} | all-to-all | bytes 1179648 | tf_op jit(solution)/shard_map/all_to_all | solution.py:431
  47.8 4.9 %shard_map.105 = bf16[1792,128]{1,0:T(8,128)(2,1)} custom-call(bf16[2304,128]{1,0:T(8,128)(2,1)S(1)} %bitcast.36, bf16[3,576,1152]{2,1,0:T(8,128)(2,1)S(1)} %bitcast.18), custom_call_target="tpu_custom_call" | custom-call | flops 2321547264 | bytes 5029888 | tf_op jit(solution)/shard_map/pallas_call | solution.py:396
  52.7 4.9 %all-to-all-start.1 = ((bf16[32,56,128]{2,1,0:T(8,128)(2,1)}), bf16[32,56,128]{2,1,0:T(8,128)(2,1)S(1)}, u32[]{:S(2)}, u32[]{:S(2)}) async-start(bf16[32,56,128]{2,1,0:T(8,128)(2,1)} %bitcast.10), calls=%async_computation.1 | async-start | bytes 917504 | tf_op jit(solution)/shard_map/all_to_all | solution.py:431
  58.3 1.5 %collective-permute-start.5 = (bf16[128,288]{1,0:T(8,128)(2,1)S(1)}, bf16[128,288]{1,0:T(8,128)(2,1)S(1)}, u32[]{:S(2)}, u32[]{:S(2)}) collective-permute-start(bf16[128,288]{1,0:T(8,128)(2,1)S(1)} %get-tuple-element.52), channel_id=1, source_target_pairs={{0,16},{2,18},{4,20},{6,22},{8,24},{10,26},{12,28},{14,30},{16,0},... | collective-permute-start | bytes 221192 | tf_op jit(solution)/shard_map/ppermute | solution.py:415
  59.8 5.7 %collective-permute-done.5.refs_2_ = bf16[128,288]{1,0:T(8,128)(2,1)S(1)} collective-permute-done((bf16[128,288]{1,0:T(8,128)(2,1)S(1)}, bf16[128,288]{1,0:T(8,128)(2,1)S(1)}, u32[]{:S(2)}, u32[]{:S(2)}) %collective-permute-start.5) | collective-permute-done | bytes 73760 | tf_op jit(solution)/shard_map/ppermute | solution.py:415
  65.5 2.1 %collective-permute-done.6.refs_3_ = bf16[128,288]{1,0:T(8,128)(2,1)S(1)} collective-permute-done((bf16[128,288]{1,0:T(8,128)(2,1)S(1)}, bf16[128,288]{1,0:T(8,128)(2,1)S(1)}, u32[]{:S(2)}, u32[]{:S(2)}) %collective-permute-start.6) | collective-permute-done | bytes 73760 | tf_op jit(solution)/shard_map/ppermute | solution.py:417
  68.2 4.8 %all-to-all-done.1 = bf16[32,56,128]{2,1,0:T(8,128)(2,1)S(1)} async-done(((bf16[32,56,128]{2,1,0:T(8,128)(2,1)}), bf16[32,56,128]{2,1,0:T(8,128)(2,1)S(1)}, u32[]{:S(2)}, u32[]{:S(2)}) %all-to-all-start.1) | async-done | bytes 458784 | tf_op jit(solution)/shard_map/all_to_all | solution.py:431
  73.2 1.4 %collective-permute-start.7 = (bf16[128,1152]{1,0:T(8,128)(2,1)S(1)}, bf16[128,1152]{1,0:T(8,128)(2,1)S(1)}, u32[]{:S(2)}, u32[]{:S(2)}) collective-permute-start(bf16[128,1152]{1,0:T(8,128)(2,1)S(1)} %get-tuple-element.56.refs_4_), channel_id=1, source_target_pairs={{0,1},{1,0},{2,3},{3,2},{4,5},{5,4},{6,7},{7,6},{8,9},{9,8},{10,11... | collective-permute-start | bytes 884744 | tf_op jit(solution)/shard_map/ppermute | solution.py:408
  75.3 4.7 %collective-permute-done.8.refs_6_ = bf16[128,576]{1,0:T(8,128)(2,1)S(1)} collective-permute-done((bf16[128,576]{1,0:T(8,128)(2,1)S(1)}, bf16[128,576]{1,0:T(8,128)(2,1)S(1)}, u32[]{:S(2)}, u32[]{:S(2)}) %collective-permute-start.8) | collective-permute-done | bytes 147488 | tf_op jit(solution)/shard_map/ppermute | solution.py:415
  81.2 1.4 %collective-permute-start.11 = (bf16[128,1152]{1,0:T(8,128)(2,1)S(1)}, bf16[128,1152]{1,0:T(8,128)(2,1)S(1)}, u32[]{:S(2)}, u32[]{:S(2)}) collective-permute-start(bf16[128,1152]{1,0:T(8,128)(2,1)S(1)} %shard_map.108.refs_2_), channel_id=1, source_target_pairs={{0,1},{1,0},{2,3},{3,2},{4,5},{5,4},{6,7},{7,6},{8,9},{9,8},{10,11... | collective-permute-start | bytes 884744 | tf_op jit(solution)/shard_map/ppermute | solution.py:408
  85.8 3.1 %shard_map.109.refs_8_ = f32[288,576]{1,0:T(8,128)} custom-call(bf16[128,288]{1,0:T(8,128)(2,1)} %copy-done.12, bf16[128,288]{1,0:T(8,128)(2,1)} %copy-done.23, bf16[128,288]{1,0:T(8,128)(2,1)} %copy-done.24, bf16[128,288]{1,0:T(8,128)(2,1)} %copy-done.25, bf16[128,576]{1,0:T(8,128)(2,1)} %copy-done.6, bf16[128,576]{1,0:T(8,128)(2,1)} %copy-done.18, ...), custom_call_target="tpu_custom_call" | custom-call | flops 339738624 | bytes 1548288 | tf_op jit(solution)/shard_map/pallas_call | solution.py:396
  88.9 1.1 collective-permute-done.15.refs_3_
  90.7 3.5 %shard_map.113 = bf16[2816,128]{1,0:T(8,128)(2,1)} custom-call(bf16[128,288]{1,0:T(8,128)(2,1)} %copy-done.11, bf16[128,288]{1,0:T(8,128)(2,1)} %copy-done.20, bf16[128,288]{1,0:T(8,128)(2,1)} %copy-done.21, bf16[128,288]{1,0:T(8,128)(2,1)} %copy-done.22, bf16[128,576]{1,0:T(8,128)(2,1)} %get-tuple-element.73.refs_4_, bf16[128,576]{1,0:T(8,128)(2,1)} %copy-done.14, ...), custom_call_target="tpu_custom_call" | custom-call | flops 339738624 | bytes 2269184 | tf_op jit(solution)/shard_map/pallas_call | solution.py:396
  94.2 10.5 %all-to-all-start.2 = ((bf16[32,88,128]{2,1,0:T(8,128)(2,1)}), bf16[32,88,128]{2,1,0:T(8,128)(2,1)S(1)}, u32[]{:S(2)}, u32[]{:S(2)}) async-start(bf16[32,88,128]{2,1,0:T(8,128)(2,1)} %bitcast.39), calls=%async_computation.2 | async-start | bytes 1441792 | tf_op jit(solution)/shard_map/all_to_all | solution.py:527
  104.8 6.7 %shard_map.111.refs_3_ = bf16[128,1152]{1,0:T(8,128)(2,1)} custom-call(bf16[128,1152]{1,0:T(8,128)(2,1)} %copy-done.13, bf16[576,1152]{1,0:T(8,128)(2,1)} %bitcast.41, bf16[3,128,576]{2,1,0:T(8,128)(2,1)} %get-tuple-element.68.refs_2_, f32[1024,128]{1,0:T(8,128)} %get-tuple-element.69.refs_3_, bf16[3,576,1152]{2,1,0:T(8,128)(2,1)} %bitcast.38), custom_call_target="tpu_custom_call" | custom-call | flops 2189426688 | bytes 6864896 | tf_op jit(solution)/shard_map/pallas_call | solution.py:396
  113.1 10.0 %collective-permute-done.12.refs_4_ = bf16[128,1152]{1,0:T(8,128)(2,1)S(1)} collective-permute-done((bf16[128,1152]{1,0:T(8,128)(2,1)}, bf16[128,1152]{1,0:T(8,128)(2,1)S(1)}, u32[]{:S(2)}, u32[]{:S(2)}) %collective-permute-start.12) | collective-permute-done | bytes 294944 | tf_op jit(solution)/shard_map/ppermute | solution.py:408
  124.1 1.3 shard_map.112
  125.4 3.2 %all-to-all-done.2 = bf16[32,88,128]{2,1,0:T(8,128)(2,1)S(1)} async-done(((bf16[32,88,128]{2,1,0:T(8,128)(2,1)}), bf16[32,88,128]{2,1,0:T(8,128)(2,1)S(1)}, u32[]{:S(2)}, u32[]{:S(2)}) %all-to-all-start.2) | async-done | bytes 720928 | tf_op jit(solution)/shard_map/all_to_all | solution.py:527
  (78 shorter events, 11.5 us)
Async XLA Ops:
  7.7 9.1 %collective-permute-start = (bf16[128,1152]{1,0:T(8,128)(2,1)}, bf16[128,1152]{1,0:T(8,128)(2,1)S(1)}, u32[]{:S(2)}, u32[]{:S(2)}) collective-permute-start(bf16[128,1152]{1,0:T(8,128)(2,1)} %get-tuple-element.42.refs_1_), channel_id=1, source_target_pairs={{0,1},{1,0},{2,3},{3,2},{4,5},{5,4},{6,7},{7,6},{8,9},{9,8},{10,11... | collective-permute-start | bytes 884744 | tf_op jit(solution)/shard_map/ppermute | solution.py:408
  9.3 4.3 %collective-permute-start.2 = (bf16[128,576]{1,0:T(8,128)(2,1)}, bf16[128,576]{1,0:T(8,128)(2,1)S(1)}, u32[]{:S(2)}, u32[]{:S(2)}) collective-permute-start(bf16[128,576]{1,0:T(8,128)(2,1)} %get-tuple-element.73.refs_4_), channel_id=1, source_target_pairs={{0,64},{64,0},{128,192},{192,128},{1,65},{65,1},{129,193},{193,129... | collective-permute-start | bytes 442376 | tf_op jit(solution)/shard_map/ppermute | solution.py:425
  9.4 6.8 %collective-permute-start.1 = (bf16[128,576]{1,0:T(8,128)(2,1)}, bf16[128,576]{1,0:T(8,128)(2,1)S(1)}, u32[]{:S(2)}, u32[]{:S(2)}) collective-permute-start(bf16[128,576]{1,0:T(8,128)(2,1)} %get-tuple-element.73.refs_4_), channel_id=1, source_target_pairs={{0,16},{2,18},{4,20},{6,22},{8,24},{10,26},{12,28},{14,30},{16,0},... | collective-permute-start | bytes 442376 | tf_op jit(solution)/shard_map/ppermute | solution.py:415
  13.6 39.1 %copy-start.12 = (bf16[128,288]{1,0:T(8,128)(2,1)}, bf16[128,288]{1,0:T(8,128)(2,1)S(1)}, u32[]{:S(2)}) copy-start(bf16[128,288]{1,0:T(8,128)(2,1)S(1)} %get-tuple-element.60.refs_0_) | copy-start | bytes 221188
  13.6 39.1 %copy-start.14 = (bf16[128,576]{1,0:T(8,128)(2,1)}, bf16[128,576]{1,0:T(8,128)(2,1)S(1)}, u32[]{:S(2)}) copy-start(bf16[128,576]{1,0:T(8,128)(2,1)S(1)} %collective-permute-done.2.refs_5_) | copy-start | bytes 442372
  16.2 36.5 %copy-start.15 = (bf16[128,576]{1,0:T(8,128)(2,1)}, bf16[128,576]{1,0:T(8,128)(2,1)S(1)}, u32[]{:S(2)}) copy-start(bf16[128,576]{1,0:T(8,128)(2,1)S(1)} %collective-permute-done.1.refs_6_) | copy-start | bytes 442372
  52.7 20.3 %all-to-all-start.1 = ((bf16[32,56,128]{2,1,0:T(8,128)(2,1)}), bf16[32,56,128]{2,1,0:T(8,128)(2,1)S(1)}, u32[]{:S(2)}, u32[]{:S(2)}) async-start(bf16[32,56,128]{2,1,0:T(8,128)(2,1)} %bitcast.10), calls=%async_computation.1 | async-start | bytes 917504 | tf_op jit(solution)/shard_map/all_to_all | solution.py:431
  57.7 10.5 %collective-permute-start.3 = (bf16[128,576]{1,0:T(8,128)(2,1)}, bf16[128,576]{1,0:T(8,128)(2,1)S(1)}, u32[]{:S(2)}, u32[]{:S(2)}) collective-permute-start(bf16[128,576]{1,0:T(8,128)(2,1)} %copy-done.15), channel_id=1, source_target_pairs={{0,64},{64,0},{128,192},{192,128},{1,65},{65,1},{129,193},{193,129... | collective-permute-start | bytes 442376 | tf_op jit(solution)/shard_map/ppermute | solution.py:425
  57.8 2.0 %collective-permute-start.4 = (bf16[128,288]{1,0:T(8,128)(2,1)S(1)}, bf16[128,288]{1,0:T(8,128)(2,1)S(1)}, u32[]{:S(2)}, u32[]{:S(2)}) collective-permute-start(bf16[128,288]{1,0:T(8,128)(2,1)S(1)} %get-tuple-element.51), channel_id=1, source_target_pairs={{0,64},{64,0},{128,192},{192,128},{1,65},{65,1},{129,193},{193,129... | collective-permute-start | bytes 221192 | tf_op jit(solution)/shard_map/ppermute | solution.py:425
  58.3 7.2 %collective-permute-start.5 = (bf16[128,288]{1,0:T(8,128)(2,1)S(1)}, bf16[128,288]{1,0:T(8,128)(2,1)S(1)}, u32[]{:S(2)}, u32[]{:S(2)}) collective-permute-start(bf16[128,288]{1,0:T(8,128)(2,1)S(1)} %get-tuple-element.52), channel_id=1, source_target_pairs={{0,16},{2,18},{4,20},{6,22},{8,24},{10,26},{12,28},{14,30},{16,0},... | collective-permute-start | bytes 221192 | tf_op jit(solution)/shard_map/ppermute | solution.py:415
  59.8 7.8 %collective-permute-start.6 = (bf16[128,288]{1,0:T(8,128)(2,1)S(1)}, bf16[128,288]{1,0:T(8,128)(2,1)S(1)}, u32[]{:S(2)}, u32[]{:S(2)}) collective-permute-start(bf16[128,288]{1,0:T(8,128)(2,1)S(1)} %get-tuple-element.53), channel_id=1, source_target_pairs={{0,80},{2,82},{4,84},{6,86},{8,88},{10,90},{12,92},{14,94},{16,64}... | collective-permute-start | bytes 221192 | tf_op jit(solution)/shard_map/ppermute | solution.py:417
  59.8 25.3 %copy-start.23 = (bf16[128,288]{1,0:T(8,128)(2,1)}, bf16[128,288]{1,0:T(8,128)(2,1)S(1)}, u32[]{:S(2)}) copy-start(bf16[128,288]{1,0:T(8,128)(2,1)S(1)} %collective-permute-done.4.refs_1_) | copy-start | bytes 221188
  68.2 21.9 %copy-start.16 = (bf16[128,576]{1,0:T(8,128)(2,1)}, bf16[128,576]{1,0:T(8,128)(2,1)S(1)}, u32[]{:S(2)}) copy-start(bf16[128,576]{1,0:T(8,128)(2,1)S(1)} %collective-permute-done.3.refs_7_) | copy-start | bytes 442372
  73.2 6.8 %collective-permute-start.7 = (bf16[128,1152]{1,0:T(8,128)(2,1)S(1)}, bf16[128,1152]{1,0:T(8,128)(2,1)S(1)}, u32[]{:S(2)}, u32[]{:S(2)}) collective-permute-start(bf16[128,1152]{1,0:T(8,128)(2,1)S(1)} %get-tuple-element.56.refs_4_), channel_id=1, source_target_pairs={{0,1},{1,0},{2,3},{3,2},{4,5},{5,4},{6,7},{7,6},{8,9},{9,8},{10,11... | collective-permute-start | bytes 884744 | tf_op jit(solution)/shard_map/ppermute | solution.py:408
  74.7 5.3 %collective-permute-start.8 = (bf16[128,576]{1,0:T(8,128)(2,1)S(1)}, bf16[128,576]{1,0:T(8,128)(2,1)S(1)}, u32[]{:S(2)}, u32[]{:S(2)}) collective-permute-start(bf16[128,576]{1,0:T(8,128)(2,1)S(1)} %get-tuple-element.59.refs_0_.refs_4_), channel_id=1, source_target_pairs={{0,16},{2,18},{4,20},{6,22},{8,24},{10,26},{12,28},{14,30},{16,0},... | collective-permute-start | bytes 442376 | tf_op jit(solution)/shard_map/ppermute | solution.py:415
  81.2 7.7 %collective-permute-start.11 = (bf16[128,1152]{1,0:T(8,128)(2,1)S(1)}, bf16[128,1152]{1,0:T(8,128)(2,1)S(1)}, u32[]{:S(2)}, u32[]{:S(2)}) collective-permute-start(bf16[128,1152]{1,0:T(8,128)(2,1)S(1)} %shard_map.108.refs_2_), channel_id=1, source_target_pairs={{0,1},{1,0},{2,3},{3,2},{4,5},{5,4},{6,7},{7,6},{8,9},{9,8},{10,11... | collective-permute-start | bytes 884744 | tf_op jit(solution)/shard_map/ppermute | solution.py:408
  82.6 1.4 %collective-permute-start.9 = (bf16[128,576]{1,0:T(8,128)(2,1)S(1)}, bf16[128,576]{1,0:T(8,128)(2,1)S(1)}, u32[]{:S(2)}, u32[]{:S(2)}) collective-permute-start(bf16[128,576]{1,0:T(8,128)(2,1)S(1)} %get-tuple-element.59.refs_0_.refs_4_), channel_id=1, source_target_pairs={{0,64},{64,0},{128,192},{192,128},{1,65},{65,1},{129,193},{193,129... | collective-permute-start | bytes 442376 | tf_op jit(solution)/shard_map/ppermute | solution.py:425
  82.6 2.5 %collective-permute-start.10 = (bf16[128,576]{1,0:T(8,128)(2,1)S(1)}, bf16[128,576]{1,0:T(8,128)(2,1)S(1)}, u32[]{:S(2)}, u32[]{:S(2)}) collective-permute-start(bf16[128,576]{1,0:T(8,128)(2,1)S(1)} %collective-permute-done.8.refs_6_), channel_id=1, source_target_pairs={{0,64},{64,0},{128,192},{192,128},{1,65},{65,1},{129,193},{193,129... | collective-permute-start | bytes 442376 | tf_op jit(solution)/shard_map/ppermute | solution.py:425
  83.1 5.8 %collective-permute-start.13 = (bf16[128,288]{1,0:T(8,128)(2,1)S(1)}, bf16[128,288]{1,0:T(8,128)(2,1)S(1)}, u32[]{:S(2)}, u32[]{:S(2)}) collective-permute-start(bf16[128,288]{1,0:T(8,128)(2,1)S(1)} %get-tuple-element.70), channel_id=1, source_target_pairs={{0,64},{64,0},{128,192},{192,128},{1,65},{65,1},{129,193},{193,129... | collective-permute-start | bytes 221192 | tf_op jit(solution)/shard_map/ppermute | solution.py:425
  83.1 5.8 %collective-permute-start.14 = (bf16[128,288]{1,0:T(8,128)(2,1)S(1)}, bf16[128,288]{1,0:T(8,128)(2,1)S(1)}, u32[]{:S(2)}, u32[]{:S(2)}) collective-permute-start(bf16[128,288]{1,0:T(8,128)(2,1)S(1)} %get-tuple-element.71), channel_id=1, source_target_pairs={{0,16},{2,18},{4,20},{6,22},{8,24},{10,26},{12,28},{14,30},{16,0},... | collective-permute-start | bytes 221192 | tf_op jit(solution)/shard_map/ppermute | solution.py:415
  84.0 6.0 %collective-permute-start.15 = (bf16[128,288]{1,0:T(8,128)(2,1)S(1)}, bf16[128,288]{1,0:T(8,128)(2,1)S(1)}, u32[]{:S(2)}, u32[]{:S(2)}) collective-permute-start(bf16[128,288]{1,0:T(8,128)(2,1)S(1)} %get-tuple-element.72), channel_id=1, source_target_pairs={{0,80},{2,82},{4,84},{6,86},{8,88},{10,90},{12,92},{14,94},{16,64}... | collective-permute-start | bytes 221192 | tf_op jit(solution)/shard_map/ppermute | solution.py:417
  94.2 34.3 %all-to-all-start.2 = ((bf16[32,88,128]{2,1,0:T(8,128)(2,1)}), bf16[32,88,128]{2,1,0:T(8,128)(2,1)S(1)}, u32[]{:S(2)}, u32[]{:S(2)}) async-start(bf16[32,88,128]{2,1,0:T(8,128)(2,1)} %bitcast.39), calls=%async_computation.2 | async-start | bytes 1441792 | tf_op jit(solution)/shard_map/all_to_all | solution.py:527
  104.7 18.4 %copy-start.8 = (f32[128,1152]{1,0:T(8,128)S(1)}, f32[128,1152]{1,0:T(8,128)}, u32[]{:S(2)}) copy-start(f32[128,1152]{1,0:T(8,128)} %copy-done.7) | copy-start | bytes 1769476
  111.5 11.6 %collective-permute-start.12 = (bf16[128,1152]{1,0:T(8,128)(2,1)}, bf16[128,1152]{1,0:T(8,128)(2,1)S(1)}, u32[]{:S(2)}, u32[]{:S(2)}) collective-permute-start(bf16[128,1152]{1,0:T(8,128)(2,1)} %shard_map.111.refs_3_), channel_id=1, source_target_pairs={{0,1},{1,0},{2,3},{3,2},{4,5},{5,4},{6,7},{7,6},{8,9},{9,8},{10,11... | collective-permute-start | bytes 884744 | tf_op jit(solution)/shard_map/ppermute | solution.py:408
  (20 other events, 91.6 us)

commit v6 on v5

--- a/solution.py
+++ b/solution.py
@@ -16,6 +16,8 @@
 F32 = jnp.float32
 X_RING = 4
 Z_RING = 8
+Z_GROUPS = tuple(tuple(z + Z_RING * x for z in range(Z_RING)) for x in range(X_RING))
+ROWS = 9
 
 
 def mm(left, right):
@@ -78,14 +80,10 @@
 
 
 FAR_GROUPS = tuple(
-    tuple(
-        ((2 * far + core) * X_RING + 2 * x_high + x_low) * Z_RING + z
-        for far in range(2)
-        for x_high in range(2)
-        for z in range(Z_RING)
-    )
+    tuple(((2 * far + core) * X_RING + 2 * x_high + x_low) * Z_RING + z for far in range(2) for x_high in range(2))
     for core in range(2)
     for x_low in range(2)
+    for z in range(Z_RING)
 )
 LANES = 128
 QUARTERS = 4
@@ -277,30 +275,44 @@
 
 
 def weight_products(*refs):
-    temporal_ref, wire_ref, tiles_ref, held_ref = refs[2 * DP :]
+    temporal_ref, wire_ref = refs[2 * DP :]
     totals = (product_of(refs[: 2 * DP]), temporal_ref[...])
     rows, columns = totals[0].shape
     whole = columns // LANES * LANES
     tiles = [total[:, at : at + LANES] for total in totals for at in range(0, whole, LANES)]
     tiles.append(jnp.concatenate([total[:, whole:] for total in totals], axis=1))
-    for i, tile in enumerate(tiles):
-        tiles_ref[i * rows : (i + 1) * rows] = tile
-    part = rows // SEQ
-    slots = held_ref.shape[0] // SEQ
+    cut = rows // DP
+    for i in range(DP):
+        chunk = [tile[i * cut : (i + 1) * cut] for tile in tiles]
+        wire_ref[i] = jnp.concatenate(chunk, axis=0).astype(BF)
+
+
+def add_sources(parts):
+    total = parts[0].astype(F32)
+    for part in parts[1:]:
+        total = total + part.astype(F32)
+    return total
+
+
+def weight_halfway(arrived_ref, wire_ref, total_ref, held_ref):
+    total_ref[...] = add_sources([arrived_ref[i] for i in range(DP)])
+    slots = held_ref.shape[0] // Z_RING
+    part = ROWS
     for slot in range(slots):
         tile, row = slot // part, slot % part
-        if tile < len(tiles):
-            taken = tiles_ref[pl.ds(tile * rows + row, SEQ, stride=part), :]
+        start = tile * part * Z_RING + row
+        if start < total_ref.shape[0]:
+            taken = total_ref[pl.ds(start, Z_RING, stride=part), :]
         else:
-            taken = jnp.zeros((SEQ, LANES), F32)
-        held_ref[pl.ds(slot, SEQ, stride=slots), :] = taken
+            taken = jnp.zeros((Z_RING, LANES), F32)
+        held_ref[pl.ds(slot, Z_RING, stride=slots), :] = taken
     wire_ref[...] = held_ref[...].astype(BF)
 
 
 def weight_sums(arrived_ref, spatial_ref, temporal_ref):
-    slots = arrived_ref.shape[0] // SEQ
+    slots = arrived_ref.shape[0] // Z_RING
     total = arrived_ref[:slots].astype(F32)
-    for i in range(1, SEQ):
+    for i in range(1, Z_RING):
         total = total + arrived_ref[i * slots : (i + 1) * slots].astype(F32)
     part, columns = spatial_ref.shape
     whole = columns // LANES * LANES
@@ -400,7 +412,7 @@
         out_specs=out_specs[0] if single else out_specs,
         scratch_shapes=own + held + sems,
         cost_estimate=pl.CostEstimate(flops=flops, bytes_accessed=moved, transcendentals=0),
-        compiler_params=pltpu.CompilerParams(vmem_limit_bytes=(vmem or (60 if manual else 40)) * 1024 * 1024),
+        compiler_params=pltpu.CompilerParams(vmem_limit_bytes=(vmem or (60 if manual else 32)) * 1024 * 1024),
     )(*operands)
 
 
@@ -430,6 +442,12 @@
     cut = array.reshape(SEQ, rows // SEQ, width)
     moved = lax.all_to_all(cut, "seq", split_axis=0, concat_axis=0, tiled=True)
     return moved.reshape(rows, width)
+
+
+def group_all_to_all(array, groups):
+    return lax.all_to_all(
+        array, "seq", split_axis=0, concat_axis=0, tiled=True, axis_index_groups=groups
+    )
 
 
 def per_device(
@@ -501,37 +519,41 @@
         near_place, cot, middle, mod, partial_t, partial_other, scalars=1, scratch=[blocks_held],
     )
     blocks_s = [blocks_s[0]] + [swap_near(blocks_s[i], i) for i in range(1, DP)]
+    temporal_sum = call(
+        temporal_product, [((width // DP, local), F32)], *blocks_t, heads_t, *heads_near, manual=True,
+        flops=2 * product, vmem=60,
+    )
+    heads_late, _ = lax.optimization_barrier((heads_t, blocks_s[0]))
+    mixed_t = call(mix_temporal, [wide], heads_late, out_t, flops=product)
+    mixed_t_other = swap_pair(mixed_t)
+    temporal_sum, mixed_t_other = lax.optimization_barrier((temporal_sum, mixed_t_other))
+    tiled = 2 * local // LANES * width // DP // DP
+    piece = ((DP, tiled, LANES), BF)
+    slots = wire_slots(2 * ROWS * local // QUARTERS)
+    sums = call(
+        weight_products, [piece], *blocks_s, *heads_s, temporal_sum, manual=True, flops=2 * product,
+    )
+    scaled_s, sums = lax.optimization_barrier((scaled_s, sums))
     partial_s = call(
         spatial_back, [wide],
         scaled_s, out_s, packed_s, weights_s, proj_s, manual=True,
         flops=4 * product + 5 * attention,
     )
     partial_s_other = swap_pair(partial_s)
-    temporal_sum = call(
-        temporal_product, [((width // DP, local), F32)], *blocks_t, heads_t, *heads_near, manual=True,
-        flops=2 * product, vmem=60,
-    )
-    heads_late, _ = lax.optimization_barrier((heads_t, blocks_s[0]))
-    mixed_t = call(mix_temporal, [wide], heads_late, out_t, flops=product)
-    mixed_t_other = swap_pair(mixed_t)
-    temporal_sum, mixed_t_other = lax.optimization_barrier((temporal_sum, mixed_t_other))
-    slots = wire_slots(2 * width // DP // SEQ * local // QUARTERS)
-    sums = call(
-        weight_products, [((SEQ * slots, LANES), BF)],
-        *blocks_s, *heads_s, temporal_sum, manual=True, flops=2 * product, vmem=60,
-        scratch=[
-            pltpu.VMEM((2 * local // LANES * width // DP, LANES), F32),
-            pltpu.VMEM((SEQ * slots, LANES), F32),
-        ],
-    )
     sums = lax.all_to_all(
-        sums.reshape(SEQ, slots, LANES), ("dp", "seq"), split_axis=0, concat_axis=0, tiled=True,
-        axis_index_groups=FAR_GROUPS,
-    ).reshape(SEQ * slots, LANES)
+        sums, ("dp", "seq"), split_axis=0, concat_axis=0, tiled=True, axis_index_groups=FAR_GROUPS
+    )
+    sums, partial_s = lax.optimization_barrier((sums, partial_s))
+    sums_half = call(
+        weight_halfway, [((Z_RING * slots, LANES), BF)], sums,
+        scratch=[pltpu.VMEM((tiled, LANES), F32), pltpu.VMEM((Z_RING * slots, LANES), F32)],
+    )
+    sums_in = group_all_to_all(sums_half.reshape(Z_RING, slots, LANES), Z_GROUPS)
+    sums_in = sums_in.reshape(Z_RING * slots, LANES)
     block_output = call(output_step, [wide], middle, mod, mixed_t, mixed_t_other)
     latent_grad = call(latent_step, [full], x, mod, grad_middle, partial_s, partial_s_other)
     part = ((width // DP // SEQ, local), F32)
-    grad_out_s, grad_out_t = call(weight_sums, [part, part], sums)
+    grad_out_s, grad_out_t = call(weight_sums, [part, part], sums_in)
     return (
         block_output.reshape(latents.shape),
         latent_grad.reshape(latents.shape),

time: 130 us -> 129 us (level)
  waiting for transfers between devices: 35 us -> 32 us
  starting transfers between devices: 27.3 us -> 28.7 us
    ppermute x4, waiting for transfers between devices: 10.6 us -> 6.18 us  [swap_pair(): return lax.ppermute(array, 'tensor', PAIR)]
    all_to_all x1 -> x2, starting transfers between devices: 10.5 us -> 12.1 us  [the longest x1 6.33 us: group_all_to_all(): lax.all_to_all(array, 'seq', split_axis=0, concat_axis=0, tiled=True, axi...]
    all_to_all x1 -> x2, waiting for transfers between devices: 3.2 us -> 4.68 us  [the longest x1 4.67 us: per_device(): lax.all_to_all(sums, ('dp', 'seq'), split_axis=0, concat_axis=0, tiled=Tr...]
    pallas_call x13 -> x14, Pallas kernels: 31.7 us -> 32.2 us  [call(): pl.pallas_call(wrapped, out_shape=shapes[0] if single else shapes, in_spe...]
    unnamed x52 -> x50, local copies, waits for them, and re-layouts: 5.08 us -> 5.08 us
  transfers between devices with their start and end apart: 18 -> 19, of which waited for: 11 -> 10; matrix products, arithmetic and copies ran while one was open for 0% -> 0% of each run, Pallas kernels for 10% -> 10%
where the time goes in v6:
time: 129 us; the launch traced here: 128 us
  Pallas kernels  32.2 us (25%)
  waiting for transfers between devices  32 us (25%)
  blocking collectives  29.3 us (23%)
  starting transfers between devices  28.7 us (22%)
  local copies, waits for them, and re-layouts  5.08 us (4%)
    pallas_call x14, Pallas kernels, call(): pl.pallas_call(wrapped, out_shape=shapes[0] if single else shapes, in_spe...  32.2 us
    all_to_all x1, blocking collectives, all_to_all(): moved = lax.all_to_all(cut, 'seq', split_axis=0, concat_axis=0, tiled=True)  29.3 us
    ppermute x4, waiting for transfers between devices, swap_both(): return lax.ppermute(array, 'seq', [(i, i ^ seq_mask) for i in range(SEQ)])  13 us
    all_to_all x1, starting transfers between devices, group_all_to_all(): lax.all_to_all(array, 'seq', split_axis=0, concat_axis=0, tiled=True, axi...  6.33 us
    ppermute x4, waiting for transfers between devices, swap_pair(): return lax.ppermute(array, 'tensor', PAIR)  6.18 us
    all_to_all x1, starting transfers between devices, per_device(): lax.all_to_all(sums, ('dp', 'seq'), split_axis=0, concat_axis=0, tiled=Tr...  5.74 us
    ppermute x4, starting transfers between devices, swap_pair(): return lax.ppermute(array, 'tensor', PAIR)  5.15 us
    unnamed x50, local copies, waits for them, and re-layouts  5.08 us
  transfers between devices with their start and end apart: 19, of which 10 were waited for; matrix products, arithmetic and copies ran while one was open for 0% of the time, Pallas kernels for 10%

profile of v6, /device:TPU:32, one launch (start us, length us, event | category | flops | bytes accessed | tf_op | source)
XLA Modules:
  0.0 128.2 jit_solution(9517189080599219102)
XLA Ops:
  0.7 7.0 %shard_map.102 = (bf16[3,128,576]{2,1,0:T(8,128)(2,1)}, f32[1024,128]{1,0:T(8,128)}, bf16[128,576]{1,0:T(8,128)(2,1)}, bf16[128,1152]{1,0:T(8,128)(2,1)}) custom-call(bf16[128,1152]{1,0:T(8,128)(2,1)} %bitcast.21, f32[6,1,1152]{2,1,0:T(1,128)} %bitcast.28, bf16[3,576,1152]{2,1,0:T(8,128)(2,1)} %bitcast.37, bf16[576,1152]{1,0:T(8,128)(2,1)} %bitcast.39), custom_call_target="tpu_custom_call" | custom-call | flops 981467136 | bytes 7040000 | tf_op jit(solution)/shard_map/pallas_call | solution.py:408
  7.7 1.7 %collective-permute-start = (bf16[128,1152]{1,0:T(8,128)(2,1)}, bf16[128,1152]{1,0:T(8,128)(2,1)S(1)}, u32[]{:S(2)}, u32[]{:S(2)}) collective-permute-start(bf16[128,1152]{1,0:T(8,128)(2,1)} %get-tuple-element.46.refs_1_), channel_id=1, source_target_pairs={{0,1},{1,0},{2,3},{3,2},{4,5},{5,4},{6,7},{7,6},{8,9},{9,8},{10,11... | collective-permute-start | bytes 884744 | tf_op jit(solution)/shard_map/ppermute | solution.py:420
  9.4 1.5 %collective-permute-start.1 = (bf16[128,576]{1,0:T(8,128)(2,1)}, bf16[128,576]{1,0:T(8,128)(2,1)S(1)}, u32[]{:S(2)}, u32[]{:S(2)}) collective-permute-start(bf16[128,576]{1,0:T(8,128)(2,1)} %get-tuple-element.75.refs_4_), channel_id=1, source_target_pairs={{0,16},{2,18},{4,20},{6,22},{8,24},{10,26},{12,28},{14,30},{16,0},... | collective-permute-start | bytes 442376 | tf_op jit(solution)/shard_map/ppermute | solution.py:427
  10.9 2.1 %copy-done = bf16[1152,3,576]{0,2,1:T(8,128)(2,1)S(1)} copy-done((bf16[1152,3,576]{0,2,1:T(8,128)(2,1)S(1)}, bf16[1152,3,576]{0,2,1:T(8,128)(2,1)}, u32[]{:S(2)}) %copy-start) | copy-done | bytes 3981336
  13.6 2.5 %collective-permute-done.1.refs_6_ = bf16[128,576]{1,0:T(8,128)(2,1)S(1)} collective-permute-done((bf16[128,576]{1,0:T(8,128)(2,1)}, bf16[128,576]{1,0:T(8,128)(2,1)S(1)}, u32[]{:S(2)}, u32[]{:S(2)}) %collective-permute-start.1) | collective-permute-done | bytes 147488 | tf_op jit(solution)/shard_map/ppermute | solution.py:427
  16.7 1.7 %shard_map.104 = (bf16[2304,128]{1,0:T(8,128)(2,1)S(1)}, f32[128,1152]{1,0:T(8,128)S(1)}) custom-call(bf16[128,1152]{1,0:T(8,128)(2,1)S(1)} %bitcast.23, bf16[128,1152]{1,0:T(8,128)(2,1)S(1)} %copy-done.9, bf16[128,1152]{1,0:T(8,128)(2,1)S(1)} %collective-permute-done.refs_2_, f32[6,1,1152]{2,1,0:T(1,128)S(1)} %bitcast.30, ...), custom_call_target="tpu_custom_call" | custom-call | flops 679477248 | bytes 6220800 | tf_op jit(solution)/shard_map/pallas_call | solution.py:408
  18.5 29.3 %all_to_all.20 = bf16[32,72,128]{2,1,0:T(8,128)(2,1)S(1)} all-to-all(bf16[32,72,128]{2,1,0:T(8,128)(2,1)S(1)} %bitcast.35), channel_id=1, replica_groups=mesh['dp'=4,'seq'=32,'tensor'=2] {'seq'}, dimensions={0} | all-to-all | bytes 1179648 | tf_op jit(solution)/shard_map/all_to_all | solution.py:443
  47.8 4.9 %shard_map.105 = bf16[1792,128]{1,0:T(8,128)(2,1)} custom-call(bf16[2304,128]{1,0:T(8,128)(2,1)S(1)} %bitcast.36, bf16[3,576,1152]{2,1,0:T(8,128)(2,1)S(1)} %bitcast.18), custom_call_target="tpu_custom_call" | custom-call | flops 2321547264 | bytes 5029888 | tf_op jit(solution)/shard_map/pallas_call | solution.py:408
  52.7 4.9 %all-to-all-start.1 = ((bf16[32,56,128]{2,1,0:T(8,128)(2,1)}), bf16[32,56,128]{2,1,0:T(8,128)(2,1)S(1)}, u32[]{:S(2)}, u32[]{:S(2)}) async-start(bf16[32,56,128]{2,1,0:T(8,128)(2,1)} %bitcast.10), calls=%async_computation.1 | async-start | bytes 917504 | tf_op jit(solution)/shard_map/all_to_all | solution.py:443
  58.3 1.5 %collective-permute-start.5 = (bf16[128,288]{1,0:T(8,128)(2,1)S(1)}, bf16[128,288]{1,0:T(8,128)(2,1)S(1)}, u32[]{:S(2)}, u32[]{:S(2)}) collective-permute-start(bf16[128,288]{1,0:T(8,128)(2,1)S(1)} %get-tuple-element.56), channel_id=1, source_target_pairs={{0,16},{2,18},{4,20},{6,22},{8,24},{10,26},{12,28},{14,30},{16,0},... | collective-permute-start | bytes 221192 | tf_op jit(solution)/shard_map/ppermute | solution.py:427
  59.8 5.7 %collective-permute-done.5.refs_2_ = bf16[128,288]{1,0:T(8,128)(2,1)S(1)} collective-permute-done((bf16[128,288]{1,0:T(8,128)(2,1)S(1)}, bf16[128,288]{1,0:T(8,128)(2,1)S(1)}, u32[]{:S(2)}, u32[]{:S(2)}) %collective-permute-start.5) | collective-permute-done | bytes 73760 | tf_op jit(solution)/shard_map/ppermute | solution.py:427
  65.5 2.1 %collective-permute-done.6.refs_3_ = bf16[128,288]{1,0:T(8,128)(2,1)S(1)} collective-permute-done((bf16[128,288]{1,0:T(8,128)(2,1)S(1)}, bf16[128,288]{1,0:T(8,128)(2,1)S(1)}, u32[]{:S(2)}, u32[]{:S(2)}) %collective-permute-start.6) | collective-permute-done | bytes 73760 | tf_op jit(solution)/shard_map/ppermute | solution.py:429
  68.2 4.8 %all-to-all-done.1 = bf16[32,56,128]{2,1,0:T(8,128)(2,1)S(1)} async-done(((bf16[32,56,128]{2,1,0:T(8,128)(2,1)}), bf16[32,56,128]{2,1,0:T(8,128)(2,1)S(1)}, u32[]{:S(2)}, u32[]{:S(2)}) %all-to-all-start.1) | async-done | bytes 458784 | tf_op jit(solution)/shard_map/all_to_all | solution.py:443
  73.2 1.4 %collective-permute-start.7 = (bf16[128,1152]{1,0:T(8,128)(2,1)S(1)}, bf16[128,1152]{1,0:T(8,128)(2,1)S(1)}, u32[]{:S(2)}, u32[]{:S(2)}) collective-permute-start(bf16[128,1152]{1,0:T(8,128)(2,1)S(1)} %get-tuple-element.60.refs_4_), channel_id=1, source_target_pairs={{0,1},{1,0},{2,3},{3,2},{4,5},{5,4},{6,7},{7,6},{8,9},{9,8},{10,11... | collective-permute-start | bytes 884744 | tf_op jit(solution)/shard_map/ppermute | solution.py:420
  75.3 4.7 %collective-permute-done.8.refs_6_ = bf16[128,576]{1,0:T(8,128)(2,1)S(1)} collective-permute-done((bf16[128,576]{1,0:T(8,128)(2,1)S(1)}, bf16[128,576]{1,0:T(8,128)(2,1)S(1)}, u32[]{:S(2)}, u32[]{:S(2)}) %collective-permute-start.8) | collective-permute-done | bytes 147488 | tf_op jit(solution)/shard_map/ppermute | solution.py:427
  81.2 1.4 %collective-permute-start.11 = (bf16[128,1152]{1,0:T(8,128)(2,1)S(1)}, bf16[128,1152]{1,0:T(8,128)(2,1)S(1)}, u32[]{:S(2)}, u32[]{:S(2)}) collective-permute-start(bf16[128,1152]{1,0:T(8,128)(2,1)S(1)} %shard_map.108.refs_2_), channel_id=1, source_target_pairs={{0,1},{1,0},{2,3},{3,2},{4,5},{5,4},{6,7},{7,6},{8,9},{9,8},{10,11... | collective-permute-start | bytes 884744 | tf_op jit(solution)/shard_map/ppermute | solution.py:420
  85.8 3.1 %shard_map.109.refs_8_ = f32[288,576]{1,0:T(8,128)} custom-call(bf16[128,288]{1,0:T(8,128)(2,1)} %copy-done.12, bf16[128,288]{1,0:T(8,128)(2,1)} %copy-done.22, bf16[128,288]{1,0:T(8,128)(2,1)} %copy-done.23, bf16[128,288]{1,0:T(8,128)(2,1)} %copy-done.24, bf16[128,576]{1,0:T(8,128)(2,1)} %copy-done.6, bf16[128,576]{1,0:T(8,128)(2,1)} %copy-done.17, ...), custom_call_target="tpu_custom_call" | custom-call | flops 339738624 | bytes 1548288 | tf_op jit(solution)/shard_map/pallas_call | solution.py:408
  90.7 3.2 %shard_map.111 = bf16[4,648,128]{2,1,0:T(8,128)(2,1)} custom-call(bf16[128,288]{1,0:T(8,128)(2,1)} %copy-done.11, bf16[128,288]{1,0:T(8,128)(2,1)} %copy-done.19, bf16[128,288]{1,0:T(8,128)(2,1)} %copy-done.20, bf16[128,288]{1,0:T(8,128)(2,1)} %copy-done.21, bf16[128,576]{1,0:T(8,128)(2,1)} %get-tuple-element.75.refs_4_, bf16[128,576]{1,0:T(8,128)(2,1)} %copy-done.14, ...), custom_call_target="tpu_custom_call" | custom-call | flops 339738624 | bytes 2211840 | tf_op jit(solution)/shard_map/pallas_call | solution.py:408
  93.9 5.7 %all-to-all-start.2 = ((bf16[4,648,128]{2,1,0:T(8,128)(2,1)}), bf16[4,648,128]{2,1,0:T(8,128)(2,1)S(1)}, u32[]{:S(2)}, u32[]{:S(2)}) async-start(bf16[4,648,128]{2,1,0:T(8,128)(2,1)} %shard_map.111), calls=%async_computation.2 | async-start | bytes 1327104 | tf_op jit(solution)/shard_map/all_to_all | solution.py:543
  99.6 6.7 %shard_map.112.refs_3_ = bf16[128,1152]{1,0:T(8,128)(2,1)} custom-call(bf16[128,1152]{1,0:T(8,128)(2,1)} %copy-done.13, bf16[576,1152]{1,0:T(8,128)(2,1)} %bitcast.40, bf16[3,128,576]{2,1,0:T(8,128)(2,1)} %get-tuple-element.82.refs_2_, f32[1024,128]{1,0:T(8,128)} %get-tuple-element.83.refs_3_, bf16[3,576,1152]{2,1,0:T(8,128)(2,1)} %bitcast.38), custom_call_target="tpu_custom_call" | custom-call | flops 2189426688 | bytes 6864896 | tf_op jit(solution)/shard_map/pallas_call | solution.py:408
  106.3 4.7 %all-to-all-done.2.refs_0_ = bf16[4,648,128]{2,1,0:T(8,128)(2,1)S(1)} async-done(((bf16[4,648,128]{2,1,0:T(8,128)(2,1)}), bf16[4,648,128]{2,1,0:T(8,128)(2,1)S(1)}, u32[]{:S(2)}, u32[]{:S(2)}) %all-to-all-start.2) | async-done | bytes 663584 | tf_op jit(solution)/shard_map/all_to_all | solution.py:543
  111.9 6.3 %all-to-all-start.3 = ((bf16[8,88,128]{2,1,0:T(8,128)(2,1)}), bf16[8,88,128]{2,1,0:T(8,128)(2,1)S(1)}, u32[]{:S(2)}, u32[]{:S(2)}) async-start(bf16[8,88,128]{2,1,0:T(8,128)(2,1)} %bitcast.14), calls=%async_computation.3 | async-start | bytes 360448 | tf_op jit(solution)/shard_map/all_to_all | solution.py:448
  119.6 5.6 %collective-permute-done.15.refs_4_ = bf16[128,1152]{1,0:T(8,128)(2,1)S(1)} collective-permute-done((bf16[128,1152]{1,0:T(8,128)(2,1)}, bf16[128,1152]{1,0:T(8,128)(2,1)S(1)}, u32[]{:S(2)}, u32[]{:S(2)}) %collective-permute-start.15) | collective-permute-done | bytes 294944 | tf_op jit(solution)/shard_map/ppermute | solution.py:420
  126.2 1.3 %shard_map.113 = f32[128,1152]{1,0:T(8,128)} custom-call(bf16[128,1152]{1,0:T(8,128)(2,1)S(1)} %bitcast.24, f32[6,1,1152]{2,1,0:T(1,128)S(1)} %bitcast.33, f32[128,1152]{1,0:T(8,128)S(1)} %copy-done.8, bf16[128,1152]{1,0:T(8,128)(2,1)S(1)} %copy-done.10, bf16[128,1152]{1,0:T(8,128)(2,1)S(1)} %collective-permute-done.15.refs_4_), custom_call_target="tpu_custom_call" | custom-call | bytes 2092032 | tf_op jit(solution)/shard_map/pallas_call | solution.py:408
  (79 shorter events, 13.3 us)
Async XLA Ops:
  7.7 9.1 %collective-permute-start = (bf16[128,1152]{1,0:T(8,128)(2,1)}, bf16[128,1152]{1,0:T(8,128)(2,1)S(1)}, u32[]{:S(2)}, u32[]{:S(2)}) collective-permute-start(bf16[128,1152]{1,0:T(8,128)(2,1)} %get-tuple-element.46.refs_1_), channel_id=1, source_target_pairs={{0,1},{1,0},{2,3},{3,2},{4,5},{5,4},{6,7},{7,6},{8,9},{9,8},{10,11... | collective-permute-start | bytes 884744 | tf_op jit(solution)/shard_map/ppermute | solution.py:420
  9.3 4.3 %collective-permute-start.2 = (bf16[128,576]{1,0:T(8,128)(2,1)}, bf16[128,576]{1,0:T(8,128)(2,1)S(1)}, u32[]{:S(2)}, u32[]{:S(2)}) collective-permute-start(bf16[128,576]{1,0:T(8,128)(2,1)} %get-tuple-element.75.refs_4_), channel_id=1, source_target_pairs={{0,64},{64,0},{128,192},{192,128},{1,65},{65,1},{129,193},{193,129... | collective-permute-start | bytes 442376 | tf_op jit(solution)/shard_map/ppermute | solution.py:437
  9.4 6.8 %collective-permute-start.1 = (bf16[128,576]{1,0:T(8,128)(2,1)}, bf16[128,576]{1,0:T(8,128)(2,1)S(1)}, u32[]{:S(2)}, u32[]{:S(2)}) collective-permute-start(bf16[128,576]{1,0:T(8,128)(2,1)} %get-tuple-element.75.refs_4_), channel_id=1, source_target_pairs={{0,16},{2,18},{4,20},{6,22},{8,24},{10,26},{12,28},{14,30},{16,0},... | collective-permute-start | bytes 442376 | tf_op jit(solution)/shard_map/ppermute | solution.py:427
  13.6 34.2 %copy-start.12 = (bf16[128,288]{1,0:T(8,128)(2,1)}, bf16[128,288]{1,0:T(8,128)(2,1)S(1)}, u32[]{:S(2)}) copy-start(bf16[128,288]{1,0:T(8,128)(2,1)S(1)} %get-tuple-element.64.refs_0_) | copy-start | bytes 221188
  13.6 39.1 %copy-start.14 = (bf16[128,576]{1,0:T(8,128)(2,1)}, bf16[128,576]{1,0:T(8,128)(2,1)S(1)}, u32[]{:S(2)}) copy-start(bf16[128,576]{1,0:T(8,128)(2,1)S(1)} %collective-permute-done.2.refs_5_) | copy-start | bytes 442372
  16.2 41.5 %copy-start.15 = (bf16[128,576]{1,0:T(8,128)(2,1)}, bf16[128,576]{1,0:T(8,128)(2,1)S(1)}, u32[]{:S(2)}) copy-start(bf16[128,576]{1,0:T(8,128)(2,1)S(1)} %collective-permute-done.1.refs_6_) | copy-start | bytes 442372
  52.7 20.3 %all-to-all-start.1 = ((bf16[32,56,128]{2,1,0:T(8,128)(2,1)}), bf16[32,56,128]{2,1,0:T(8,128)(2,1)S(1)}, u32[]{:S(2)}, u32[]{:S(2)}) async-start(bf16[32,56,128]{2,1,0:T(8,128)(2,1)} %bitcast.10), calls=%async_computation.1 | async-start | bytes 917504 | tf_op jit(solution)/shard_map/all_to_all | solution.py:443
  57.7 10.5 %collective-permute-start.3 = (bf16[128,576]{1,0:T(8,128)(2,1)S(1)}, bf16[128,576]{1,0:T(8,128)(2,1)}, u32[]{:S(2)}, u32[]{:S(2)}) collective-permute-start(bf16[128,576]{1,0:T(8,128)(2,1)S(1)} %collective-permute-done.1.refs_6_), channel_id=1, source_target_pairs={{0,64},{64,0},{128,192},{192,128},{1,65},{65,1},{129,193},{193,129... | collective-permute-start | bytes 442376 | tf_op jit(solution)/shard_map/ppermute | solution.py:437
  57.8 2.0 %collective-permute-start.4 = (bf16[128,288]{1,0:T(8,128)(2,1)S(1)}, bf16[128,288]{1,0:T(8,128)(2,1)S(1)}, u32[]{:S(2)}, u32[]{:S(2)}) collective-permute-start(bf16[128,288]{1,0:T(8,128)(2,1)S(1)} %get-tuple-element.55), channel_id=1, source_target_pairs={{0,64},{64,0},{128,192},{192,128},{1,65},{65,1},{129,193},{193,129... | collective-permute-start | bytes 221192 | tf_op jit(solution)/shard_map/ppermute | solution.py:437
  58.3 7.2 %collective-permute-start.5 = (bf16[128,288]{1,0:T(8,128)(2,1)S(1)}, bf16[128,288]{1,0:T(8,128)(2,1)S(1)}, u32[]{:S(2)}, u32[]{:S(2)}) collective-permute-start(bf16[128,288]{1,0:T(8,128)(2,1)S(1)} %get-tuple-element.56), channel_id=1, source_target_pairs={{0,16},{2,18},{4,20},{6,22},{8,24},{10,26},{12,28},{14,30},{16,0},... | collective-permute-start | bytes 221192 | tf_op jit(solution)/shard_map/ppermute | solution.py:427
  59.7 7.8 %collective-permute-start.6 = (bf16[128,288]{1,0:T(8,128)(2,1)S(1)}, bf16[128,288]{1,0:T(8,128)(2,1)S(1)}, u32[]{:S(2)}, u32[]{:S(2)}) collective-permute-start(bf16[128,288]{1,0:T(8,128)(2,1)S(1)} %get-tuple-element.57), channel_id=1, source_target_pairs={{0,80},{2,82},{4,84},{6,86},{8,88},{10,90},{12,92},{14,94},{16,64}... | collective-permute-start | bytes 221192 | tf_op jit(solution)/shard_map/ppermute | solution.py:429
  59.8 25.3 %copy-start.22 = (bf16[128,288]{1,0:T(8,128)(2,1)}, bf16[128,288]{1,0:T(8,128)(2,1)S(1)}, u32[]{:S(2)}) copy-start(bf16[128,288]{1,0:T(8,128)(2,1)S(1)} %collective-permute-done.4.refs_1_) | copy-start | bytes 221188
  73.2 6.8 %collective-permute-start.7 = (bf16[128,1152]{1,0:T(8,128)(2,1)S(1)}, bf16[128,1152]{1,0:T(8,128)(2,1)S(1)}, u32[]{:S(2)}, u32[]{:S(2)}) collective-permute-start(bf16[128,1152]{1,0:T(8,128)(2,1)S(1)} %get-tuple-element.60.refs_4_), channel_id=1, source_target_pairs={{0,1},{1,0},{2,3},{3,2},{4,5},{5,4},{6,7},{7,6},{8,9},{9,8},{10,11... | collective-permute-start | bytes 884744 | tf_op jit(solution)/shard_map/ppermute | solution.py:420
  74.7 5.3 %collective-permute-start.8 = (bf16[128,576]{1,0:T(8,128)(2,1)S(1)}, bf16[128,576]{1,0:T(8,128)(2,1)S(1)}, u32[]{:S(2)}, u32[]{:S(2)}) collective-permute-start(bf16[128,576]{1,0:T(8,128)(2,1)S(1)} %get-tuple-element.63.refs_0_.refs_4_), channel_id=1, source_target_pairs={{0,16},{2,18},{4,20},{6,22},{8,24},{10,26},{12,28},{14,30},{16,0},... | collective-permute-start | bytes 442376 | tf_op jit(solution)/shard_map/ppermute | solution.py:427
  81.2 7.7 %collective-permute-start.11 = (bf16[128,1152]{1,0:T(8,128)(2,1)S(1)}, bf16[128,1152]{1,0:T(8,128)(2,1)S(1)}, u32[]{:S(2)}, u32[]{:S(2)}) collective-permute-start(bf16[128,1152]{1,0:T(8,128)(2,1)S(1)} %shard_map.108.refs_2_), channel_id=1, source_target_pairs={{0,1},{1,0},{2,3},{3,2},{4,5},{5,4},{6,7},{7,6},{8,9},{9,8},{10,11... | collective-permute-start | bytes 884744 | tf_op jit(solution)/shard_map/ppermute | solution.py:420
  82.6 1.4 %collective-permute-start.9 = (bf16[128,576]{1,0:T(8,128)(2,1)S(1)}, bf16[128,576]{1,0:T(8,128)(2,1)S(1)}, u32[]{:S(2)}, u32[]{:S(2)}) collective-permute-start(bf16[128,576]{1,0:T(8,128)(2,1)S(1)} %get-tuple-element.63.refs_0_.refs_4_), channel_id=1, source_target_pairs={{0,64},{64,0},{128,192},{192,128},{1,65},{65,1},{129,193},{193,129... | collective-permute-start | bytes 442376 | tf_op jit(solution)/shard_map/ppermute | solution.py:437
  82.6 2.5 %collective-permute-start.10 = (bf16[128,576]{1,0:T(8,128)(2,1)S(1)}, bf16[128,576]{1,0:T(8,128)(2,1)S(1)}, u32[]{:S(2)}, u32[]{:S(2)}) collective-permute-start(bf16[128,576]{1,0:T(8,128)(2,1)S(1)} %collective-permute-done.8.refs_6_), channel_id=1, source_target_pairs={{0,64},{64,0},{128,192},{192,128},{1,65},{65,1},{129,193},{193,129... | collective-permute-start | bytes 442376 | tf_op jit(solution)/shard_map/ppermute | solution.py:437
  83.1 5.7 %collective-permute-start.12 = (bf16[128,288]{1,0:T(8,128)(2,1)S(1)}, bf16[128,288]{1,0:T(8,128)(2,1)S(1)}, u32[]{:S(2)}, u32[]{:S(2)}) collective-permute-start(bf16[128,288]{1,0:T(8,128)(2,1)S(1)} %get-tuple-element.72), channel_id=1, source_target_pairs={{0,64},{64,0},{128,192},{192,128},{1,65},{65,1},{129,193},{193,129... | collective-permute-start | bytes 221192 | tf_op jit(solution)/shard_map/ppermute | solution.py:437
  83.1 5.8 %collective-permute-start.13 = (bf16[128,288]{1,0:T(8,128)(2,1)S(1)}, bf16[128,288]{1,0:T(8,128)(2,1)S(1)}, u32[]{:S(2)}, u32[]{:S(2)}) collective-permute-start(bf16[128,288]{1,0:T(8,128)(2,1)S(1)} %get-tuple-element.73), channel_id=1, source_target_pairs={{0,16},{2,18},{4,20},{6,22},{8,24},{10,26},{12,28},{14,30},{16,0},... | collective-permute-start | bytes 221192 | tf_op jit(solution)/shard_map/ppermute | solution.py:427
  84.0 6.0 %collective-permute-start.14 = (bf16[128,288]{1,0:T(8,128)(2,1)S(1)}, bf16[128,288]{1,0:T(8,128)(2,1)S(1)}, u32[]{:S(2)}, u32[]{:S(2)}) collective-permute-start(bf16[128,288]{1,0:T(8,128)(2,1)S(1)} %get-tuple-element.74), channel_id=1, source_target_pairs={{0,80},{2,82},{4,84},{6,86},{8,88},{10,90},{12,92},{14,94},{16,64}... | collective-permute-start | bytes 221192 | tf_op jit(solution)/shard_map/ppermute | solution.py:429
  93.9 17.1 %all-to-all-start.2 = ((bf16[4,648,128]{2,1,0:T(8,128)(2,1)}), bf16[4,648,128]{2,1,0:T(8,128)(2,1)S(1)}, u32[]{:S(2)}, u32[]{:S(2)}) async-start(bf16[4,648,128]{2,1,0:T(8,128)(2,1)} %shard_map.111), calls=%async_computation.2 | async-start | bytes 1327104 | tf_op jit(solution)/shard_map/all_to_all | solution.py:543
  99.6 25.6 %copy-start.8 = (f32[128,1152]{1,0:T(8,128)S(1)}, f32[128,1152]{1,0:T(8,128)}, u32[]{:S(2)}) copy-start(f32[128,1152]{1,0:T(8,128)} %copy-done.7) | copy-start | bytes 1769476
  111.9 15.6 %all-to-all-start.3 = ((bf16[8,88,128]{2,1,0:T(8,128)(2,1)}), bf16[8,88,128]{2,1,0:T(8,128)(2,1)S(1)}, u32[]{:S(2)}, u32[]{:S(2)}) async-start(bf16[8,88,128]{2,1,0:T(8,128)(2,1)} %bitcast.14), calls=%async_computation.3 | async-start | bytes 360448 | tf_op jit(solution)/shard_map/all_to_all | solution.py:448
  118.2 7.0 %collective-permute-start.15 = (bf16[128,1152]{1,0:T(8,128)(2,1)}, bf16[128,1152]{1,0:T(8,128)(2,1)S(1)}, u32[]{:S(2)}, u32[]{:S(2)}) collective-permute-start(bf16[128,1152]{1,0:T(8,128)(2,1)} %shard_map.112.refs_3_), channel_id=1, source_target_pairs={{0,1},{1,0},{2,3},{3,2},{4,5},{5,4},{6,7},{7,6},{8,9},{9,8},{10,11... | collective-permute-start | bytes 884744 | tf_op jit(solution)/shard_map/ppermute | solution.py:420
  (20 other events, 86.8 us)
